TPU v7x, 32 devices: a whole 2x2x4 slice. The times are simulated.
32 devices in a mesh: groups: 1, blk: 16 (over z, y, x), heads: 2 (over core).
Axes of the slice: x: 2, y: 2, z: 4, core: 2. Of those that a mesh axis runs over, the one named last changes fastest.
Arguments:
- queries: bfloat16 [4096, 2048], P(('groups', 'blk', 'heads')), may hold values from -186 to 186
- keys: bfloat16 [4096, 1024], P(('groups', 'blk', 'heads')), may hold values from -6 to 6
- values: bfloat16 [4096, 1024], P(('groups', 'blk', 'heads')), may hold values from -6 to 6
- upstream: bfloat16 [4096, 2048], P(('groups', 'blk', 'heads')), may hold values from -6 to 6
- doc_ids: int32 [32], P('groups'), may hold values from 0 to 3, never falling along the last dimension, each value on 1 to 16 neighbouring positions
- band: int32 [32], P('groups'), may hold values from 0 to 8, as said below
Outputs:
- query_grad: bfloat16 [4096, 2048], P(('groups', 'blk', 'heads'))
- key_gradient: bfloat16 [4096, 1024], P(('groups', 'blk', 'heads'))
- value_gradient: bfloat16 [4096, 1024], P(('groups', 'blk', 'heads'))
Inputs may be any that keep to these rules, and one draw needn't show every extreme that they name: `band`: earlier blocks a query block may see; some block sees 8 and some sees 0.
All inputs are finite; a program needn't handle non-finite values.
Results may differ from a plain program's by a relative error of at most 0.0083.
Values may be sent and summed in bfloat16 or wider, within the bound.
No kernel may reach another device: no remote copies, remote signals or barrier semaphores. Data moves between devices by JAX's collectives and lax.ppermute only.
A program may use at most 64 MiB of HBM per device.

v0:
```python
import functools
import math

import jax
import jax.numpy as jnp
from jax import lax
from jax.experimental import pallas as pl
from jax.experimental.pallas import tpu as pltpu
from jax.sharding import PartitionSpec as P

HEAD = 128
SCALAR = 168
WINDOW = 1024
BLOCK = 128
WB = WINDOW // BLOCK
SCALE = SCALAR ** (-0.5)
LOG2E = math.log2(math.e)
SMALL = 8 * 1024 * 1024
TOGETHER = 4

NT = (((1,), (1,)), ((), ()))
NN = (((1,), (0,)), ((), ()))
TN = (((0,), (0,)), ((), ()))


def dot(a, b, dims):
    return lax.dot_general(a, b, dims, preferred_element_type=jnp.float32)


def run_copies(pairs, sems):
    copies = [pltpu.make_async_copy(x, y, sems.at[n]) for n, (x, y) in enumerate(pairs)]
    for copy in copies:
        copy.start()
    for copy in copies:
        copy.wait()


def pack_kernel(a_ref, b_ref, out_ref, slabs, in_sems, out_sems):
    heads = out_ref.shape[0]
    width = out_ref.shape[2] // 2
    reads = [
        [
            pltpu.make_async_copy(
                ref.at[:, pl.ds(h * width, width)],
                slabs.at[h, :, pl.ds(n * width, width)],
                in_sems.at[2 * h + n],
            )
            for n, ref in enumerate((a_ref, b_ref))
        ]
        for h in range(heads)
    ]
    writes = [
        pltpu.make_async_copy(slabs.at[h], out_ref.at[h], out_sems.at[h]) for h in range(heads)
    ]
    for pair in reads:
        for copy in pair:
            copy.start()
    for pair, write in zip(reads, writes):
        for copy in pair:
            copy.wait()
        write.start()
    for write in writes:
        write.wait()


def pack(a, b, heads):
    tokens, cols = a.shape
    hbm = pl.BlockSpec(memory_space=pl.ANY)
    shape = (heads, tokens, 2 * cols // heads)
    return pl.pallas_call(
        pack_kernel,
        in_specs=[hbm] * 2,
        out_specs=hbm,
        out_shape=jax.ShapeDtypeStruct(shape, a.dtype),
        scratch_shapes=[
            pltpu.VMEM(shape, a.dtype),
            pltpu.SemaphoreType.DMA((2 * heads,)),
            pltpu.SemaphoreType.DMA((heads,)),
        ],
    )(a, b)


def unpack_kernel(in_ref, *refs):
    out_refs, sems = refs[:-1], refs[-1]
    width = in_ref.shape[2] // len(out_refs)
    run_copies(
        [
            (in_ref.at[h, :, pl.ds(n * width, width)], ref.at[:, pl.ds(h * width, width)])
            for h in range(in_ref.shape[0])
            for n, ref in enumerate(out_refs)
        ],
        sems,
    )


def unpack(value, outputs):
    heads, tokens, width = value.shape
    shape = jax.ShapeDtypeStruct((tokens, heads * width // outputs), value.dtype)
    return pl.pallas_call(
        unpack_kernel,
        in_specs=[pl.BlockSpec(memory_space=pltpu.VMEM)],
        out_specs=[pl.BlockSpec(memory_space=pl.ANY)] * outputs,
        out_shape=[shape] * outputs,
        scratch_shapes=[pltpu.SemaphoreType.DMA((outputs * heads,))],
        compiler_params=pltpu.CompilerParams(vmem_limit_bytes=SMALL),
    )(value)


def attend_kernel(
    chunk_ref, doc_ref, band_ref, qd_ref, own_ref, halo_ref,
    dq_ref, dkv_own_ref, dkv_halo_ref,
    keys, values, dk, dv,
):
    chunk = own_ref.shape[0] * BLOCK
    blocks = chunk // BLOCK
    q_heads = qd_ref.shape[2] // (2 * HEAD)
    for j in range(blocks):
        rows = slice(j * BLOCK, (j + 1) * BLOCK)
        late = slice(WINDOW + j * BLOCK, WINDOW + (j + 1) * BLOCK)
        keys[rows, :] = halo_ref[j, :, :HEAD]
        values[rows, :] = halo_ref[j, :, HEAD:]
        keys[late, :] = own_ref[j, :, :HEAD]
        values[late, :] = own_ref[j, :, HEAD:]
    dk[...] = jnp.zeros_like(dk)
    dv[...] = jnp.zeros_like(dv)
    first = chunk_ref[0] * blocks

    def reach_of(i):
        index = first + i
        own_band = band_ref[index]
        own_doc = doc_ref[index]
        reach = jnp.int32(0)
        for back in range(1, WB + 1):
            seen = (
                (back <= own_band)
                & (index >= back)
                & (doc_ref[jnp.maximum(index - back, 0)] == own_doc)
            )
            reach = reach + seen.astype(jnp.int32)
        return reach

    rows = q_heads * BLOCK

    def stacked(i, offset):
        return jnp.concatenate(
            [qd_ref[i, :, (offset + h) * HEAD : (offset + h + 1) * HEAD] for h in range(q_heads)],
            axis=0,
        )

    def fold(x, reduce):
        return reduce(x.reshape(BLOCK // 8, 8, rows), axis=0)

    def work(count, members, reaches):
        span = count * BLOCK
        windows = [
            pl.ds(pl.multiple_of((i + WB + 1 - count) * BLOCK, BLOCK), span) for i in members
        ]
        lanes = range(len(members))

        def split(x):
            return [x[b * BLOCK : (b + 1) * BLOCK] for b in range(count)]

        query = [stacked(i, 0) for i in members]
        grad = [stacked(i, q_heads) for i in members]
        scores = [split(dot(keys[windows[n], :], query[n], NT)) for n in lanes]
        key_pos = lax.broadcasted_iota(jnp.int32, (BLOCK, rows), 0)
        query_pos = lax.broadcasted_iota(jnp.int32, (BLOCK, rows), 1) % BLOCK
        causal = key_pos <= query_pos
        probs, probs_b, dprob = {}, {}, {}
        for n in lanes:
            scores[n][-1] = jnp.where(causal, scores[n][-1], -jnp.inf)
            seen = [count - 1 - b <= reaches[n] for b in range(count)]
            tops = [
                jnp.where(seen[b], fold(x, jnp.max), -jnp.inf) for b, x in enumerate(scores[n])
            ]
            top = jnp.max(functools.reduce(jnp.maximum, tops), axis=0, keepdims=True)
            shift = [jnp.where(seen[b], top, jnp.inf) for b in range(count)]
            dprob[n] = split(dot(values[windows[n], :], grad[n], NT))
            expo = [jnp.exp2((x - y) * (SCALE * LOG2E)) for x, y in zip(scores[n], shift)]
            total = functools.reduce(jnp.add, [fold(x, jnp.sum) for x in expo])
            inverse = 1.0 / jnp.sum(total, axis=0, keepdims=True)
            probs[n] = [x * inverse for x in expo]
            probs_b[n] = [x.astype(jnp.bfloat16) for x in probs[n]]
        dscore = {}
        for n in lanes:
            dv[windows[n], :] += dot(jnp.concatenate(probs_b[n], axis=0), grad[n], NN)
            delta = functools.reduce(
                jnp.add,
                [
                    fold(x.astype(jnp.float32) * y, jnp.sum)
                    for x, y in zip(probs_b[n], dprob[n])
                ],
            )
            delta = jnp.sum(delta, axis=0, keepdims=True)
            dscore[n] = jnp.concatenate(
                [
                    (x * (y - delta)).astype(jnp.bfloat16)
                    for x, y in zip(probs[n], dprob[n])
                ],
                axis=0,
            )
        for n, i in enumerate(members):
            dk[windows[n], :] += dot(dscore[n], query[n], NN)
            query_grad = dot(dscore[n], keys[windows[n], :], TN) * SCALE
            for h in range(q_heads):
                dq_ref[i, :, h * HEAD : (h + 1) * HEAD] = query_grad[
                    h * BLOCK : (h + 1) * BLOCK, :
                ].astype(dq_ref.dtype)

    def one_step(step, carry):
        members = [step * TOGETHER + n for n in range(TOGETHER)]
        reaches = [reach_of(i) for i in members]
        widest = functools.reduce(jnp.maximum, reaches) + 1
        for count in range(1, WB + 2):
            pl.when(widest == count)(functools.partial(work, count, members, reaches))
        return carry

    lax.fori_loop(0, blocks // TOGETHER, one_step, 0)
    for j in range(blocks):
        rows = slice(j * BLOCK, (j + 1) * BLOCK)
        late = slice(WINDOW + j * BLOCK, WINDOW + (j + 1) * BLOCK)
        dkv_halo_ref[j, :, :HEAD] = (dk[rows, :] * SCALE).astype(dkv_halo_ref.dtype)
        dkv_halo_ref[j, :, HEAD:] = dv[rows, :].astype(dkv_halo_ref.dtype)
        dkv_own_ref[j, :, :HEAD] = dk[late, :] * SCALE
        dkv_own_ref[j, :, HEAD:] = dv[late, :]


def attend(chunk_index, doc_ids, band, queries_grads, own, halo):
    blocks = own.shape[0]
    total = WINDOW + blocks * BLOCK
    smem = pl.BlockSpec(memory_space=pltpu.SMEM)
    vmem = pl.BlockSpec(memory_space=pltpu.VMEM)
    return pl.pallas_call(
        attend_kernel,
        in_specs=[smem] * 3 + [vmem] * 3,
        out_specs=[vmem] * 3,
        out_shape=[
            jax.ShapeDtypeStruct(
                (blocks, BLOCK, queries_grads.shape[2] // 2), jnp.bfloat16
            ),
            jax.ShapeDtypeStruct(own.shape, jnp.float32),
            jax.ShapeDtypeStruct(own.shape, jnp.bfloat16),
        ],
        scratch_shapes=[
            pltpu.VMEM((total, HEAD), jnp.bfloat16),
            pltpu.VMEM((total, HEAD), jnp.bfloat16),
            pltpu.VMEM((total, HEAD), jnp.float32),
            pltpu.VMEM((total, HEAD), jnp.float32),
        ],
        compiler_params=pltpu.CompilerParams(vmem_limit_bytes=40 * 1024 * 1024),
    )(chunk_index, doc_ids, band, queries_grads, own, halo)


def per_device(queries, keys, values, upstream, doc_ids, band):
    tokens = queries.shape[0]
    parts = WINDOW // tokens
    cores = lax.axis_size("heads")
    spans = lax.axis_size("blk")
    step = parts // cores
    axes = ("blk", "heads")
    groups = [
        [first * parts + member for member in range(parts)] for first in range(spans // step)
    ]

    def exchange(value):
        return lax.all_to_all(
            value, axes, split_axis=0, concat_axis=0, axis_index_groups=groups, tiled=True
        )

    kv = exchange(pack(keys, values, parts))
    halo = lax.ppermute(kv, "blk", [(s, s + step) for s in range(spans - step)])
    qd = exchange(pack(queries, upstream, parts))
    chunk_index = (lax.axis_index("blk") // step).astype(jnp.int32).reshape(1)
    dq, dkv_own, dkv_halo = attend(chunk_index, doc_ids, band, qd, kv, halo)
    spill = lax.ppermute(dkv_halo, "blk", [(s + step, s) for s in range(spans - step)])
    query_out = exchange(dq)
    dkv = exchange((dkv_own + spill.astype(jnp.float32)).astype(jnp.bfloat16))

    return (*unpack(query_out, 1), *unpack(dkv, 2))


def solution(mesh):
    sharded = P(("groups", "blk", "heads"), None)
    return jax.shard_map(
        per_device,
        mesh=mesh,
        in_specs=(sharded,) * 4 + (P("groups"),) * 2,
        out_specs=(sharded,) * 3,
        check_vma=False,
    )
```

profile of v0, /device:TPU:16, one launch (start us, length us, event | category | flops | bytes accessed | tf_op | source)
XLA Modules:
  0.0 76.0 jit_solution(12294642954137235534)
XLA Ops:
  0.6 1.8 %shard_map.86 = bf16[8,128,256]{2,1,0:T(8,128)(2,1)} custom-call(bf16[128,1024]{1,0:T(8,128)(2,1)} %a_ref.3, bf16[128,1024]{1,0:T(8,128)(2,1)} %b_ref.3), custom_call_target="tpu_custom_call" | custom-call | tf_op jit(solution)/shard_map/pallas_call | solution.py:70
  2.5 3.7 %all-to-all-start.1 = ((bf16[8,128,256]{2,1,0:T(8,128)(2,1)}), bf16[8,128,256]{2,1,0:T(8,128)(2,1)S(1)}, u32[]{:S(2)}, u32[]{:S(2)}) async-start(bf16[8,128,256]{2,1,0:T(8,128)(2,1)} %shard_map.86), calls=%async_computation.1 | async-start | bytes 1048576 | tf_op jit(solution)/shard_map/all_to_all | solution.py:266
  6.2 2.1 %shard_map.85 = bf16[8,128,512]{2,1,0:T(8,128)(2,1)} custom-call(bf16[128,2048]{1,0:T(8,128)(2,1)} %a_ref.2, bf16[128,2048]{1,0:T(8,128)(2,1)} %b_ref.2), custom_call_target="tpu_custom_call" | custom-call | tf_op jit(solution)/shard_map/pallas_call | solution.py:70
  8.4 7.6 %all-to-all-done.1.own_ref = bf16[8,128,256]{2,1,0:T(8,128)(2,1)S(1)} async-done(((bf16[8,128,256]{2,1,0:T(8,128)(2,1)}), bf16[8,128,256]{2,1,0:T(8,128)(2,1)S(1)}, u32[]{:S(2)}, u32[]{:S(2)}) %all-to-all-start.1) | async-done | bytes 524320 | tf_op jit(solution)/shard_map/all_to_all | solution.py:266
  16.0 3.6 %all-to-all-start = ((bf16[8,128,512]{2,1,0:T(8,128)(2,1)}), bf16[8,128,512]{2,1,0:T(8,128)(2,1)S(1)}, u32[]{:S(2)}, u32[]{:S(2)}) async-start(bf16[8,128,512]{2,1,0:T(8,128)(2,1)} %shard_map.85), calls=%async_computation | async-start | bytes 2097152 | tf_op jit(solution)/shard_map/all_to_all | solution.py:266
  19.5 3.5 %collective-permute-start = (bf16[8,128,256]{2,1,0:T(8,128)(2,1)S(1)}, bf16[8,128,256]{2,1,0:T(8,128)(2,1)S(1)}, u32[]{:S(2)}, u32[]{:S(2)}) collective-permute-start(bf16[8,128,256]{2,1,0:T(8,128)(2,1)S(1)} %all-to-all-done.1.own_ref), channel_id=1, source_target_pairs={{0,8},{2,10},{4,12},{6,14},{8,16},{10,18},{12,20},{14,22},{16,24},... | collective-permute-start | bytes 1572872 | tf_op jit(solution)/shard_map/ppermute | solution.py:271
  23.1 0.0 copy-start
  23.1 0.0 copy-start.1
  23.1 11.8 %all-to-all-done.qd_ref = bf16[8,128,512]{2,1,0:T(8,128)(2,1)S(1)} async-done(((bf16[8,128,512]{2,1,0:T(8,128)(2,1)}), bf16[8,128,512]{2,1,0:T(8,128)(2,1)S(1)}, u32[]{:S(2)}, u32[]{:S(2)}) %all-to-all-start) | async-done | bytes 1048608 | tf_op jit(solution)/shard_map/all_to_all | solution.py:266
  34.9 0.8 %collective-permute-done.halo_ref = bf16[8,128,256]{2,1,0:T(8,128)(2,1)S(1)} collective-permute-done((bf16[8,128,256]{2,1,0:T(8,128)(2,1)S(1)}, bf16[8,128,256]{2,1,0:T(8,128)(2,1)S(1)}, u32[]{:S(2)}, u32[]{:S(2)}) %collective-permute-start) | collective-permute-done | bytes 524320 | tf_op jit(solution)/shard_map/ppermute | solution.py:271
  35.6 0.0 copy-done
  35.7 0.0 copy-done.1
  35.7 9.6 %shard_map.87 = (bf16[8,128,256]{2,1,0:T(8,128)(2,1)}, f32[8,128,256]{2,1,0:T(8,128)S(1)}, bf16[8,128,256]{2,1,0:T(8,128)(2,1)}) custom-call(s32[1]{0:T(128)} %bitcast.chunk_ref, s32[32]{0:T(128)S(1)} %copy-done, s32[32]{0:T(128)S(1)} %copy-done.1, bf16[8,128,512]{2,1,0:T(8,128)(2,1)S(1)} %all-to-all-done.qd_ref, ...), custom_call_target="tpu_custom_call" | custom-call | tf_op jit(solution)/shard_map/pallas_call | solution.py:233
  45.3 1.9 %collective-permute-start.1 = (bf16[8,128,256]{2,1,0:T(8,128)(2,1)}, bf16[8,128,256]{2,1,0:T(8,128)(2,1)S(1)}, u32[]{:S(2)}, u32[]{:S(2)}) collective-permute-start(bf16[8,128,256]{2,1,0:T(8,128)(2,1)} %get-tuple-element.10), channel_id=1, source_target_pairs={{8,0},{10,2},{12,4},{14,6},{16,8},{18,10},{20,12},{22,14},{24,16},... | collective-permute-start | bytes 1572872 | tf_op jit(solution)/shard_map/ppermute | solution.py:275
  47.2 3.9 %all-to-all-start.2 = ((bf16[8,128,256]{2,1,0:T(8,128)(2,1)}), bf16[8,128,256]{2,1,0:T(8,128)(2,1)S(1)}, u32[]{:S(2)}, u32[]{:S(2)}) async-start(bf16[8,128,256]{2,1,0:T(8,128)(2,1)} %get-tuple-element.8), calls=%async_computation.2 | async-start | bytes 1048576 | tf_op jit(solution)/shard_map/all_to_all | solution.py:266
  51.1 9.7 %collective-permute-done.1 = bf16[8,128,256]{2,1,0:T(8,128)(2,1)S(1)} collective-permute-done((bf16[8,128,256]{2,1,0:T(8,128)(2,1)}, bf16[8,128,256]{2,1,0:T(8,128)(2,1)S(1)}, u32[]{:S(2)}, u32[]{:S(2)}) %collective-permute-start.1) | collective-permute-done | bytes 524320 | tf_op jit(solution)/shard_map/ppermute | solution.py:275
  60.8 0.9 %add_convert_fusion = bf16[8,128,256]{2,1,0:T(8,128)(2,1)} fusion(f32[8,128,256]{2,1,0:T(8,128)S(1)} %get-tuple-element.9, bf16[8,128,256]{2,1,0:T(8,128)(2,1)S(1)} %collective-permute-done.1), kind=kLoop, calls=%fused_computation | loop fusion | flops 786432 | bytes 2097152 | tf_op jit(solution)/shard_map/convert_element_type | solution.py:277
  61.7 0.0 all-to-all-done.2.in_ref
  61.7 3.6 %all-to-all-start.3 = ((bf16[8,128,256]{2,1,0:T(8,128)(2,1)}), bf16[8,128,256]{2,1,0:T(8,128)(2,1)S(1)}, u32[]{:S(2)}, u32[]{:S(2)}) async-start(bf16[8,128,256]{2,1,0:T(8,128)(2,1)} %add_convert_fusion), calls=%async_computation.3 | async-start | bytes 1048576 | tf_op jit(solution)/shard_map/all_to_all | solution.py:266
  65.3 0.8 %shard_map.88 = bf16[128,2048]{1,0:T(8,128)(2,1)} custom-call(bf16[8,128,256]{2,1,0:T(8,128)(2,1)S(1)} %all-to-all-done.2.in_ref), custom_call_target="tpu_custom_call" | custom-call | tf_op jit(solution)/shard_map/pallas_call | solution.py:99
  66.2 8.9 %all-to-all-done.3.in_ref = bf16[8,128,256]{2,1,0:T(8,128)(2,1)S(1)} async-done(((bf16[8,128,256]{2,1,0:T(8,128)(2,1)}), bf16[8,128,256]{2,1,0:T(8,128)(2,1)S(1)}, u32[]{:S(2)}, u32[]{:S(2)}) %all-to-all-start.3) | async-done | bytes 524320 | tf_op jit(solution)/shard_map/all_to_all | solution.py:266
  75.1 0.9 %shard_map.89 = (bf16[128,1024]{1,0:T(8,128)(2,1)}, bf16[128,1024]{1,0:T(8,128)(2,1)}) custom-call(bf16[8,128,256]{2,1,0:T(8,128)(2,1)S(1)} %all-to-all-done.3.in_ref), custom_call_target="tpu_custom_call" | custom-call | tf_op jit(solution)/shard_map/pallas_call | solution.py:99
Async XLA Ops:
  2.5 13.5 %all-to-all-start.1 = ((bf16[8,128,256]{2,1,0:T(8,128)(2,1)}), bf16[8,128,256]{2,1,0:T(8,128)(2,1)S(1)}, u32[]{:S(2)}, u32[]{:S(2)}) async-start(bf16[8,128,256]{2,1,0:T(8,128)(2,1)} %shard_map.86), calls=%async_computation.1 | async-start | bytes 1048576 | tf_op jit(solution)/shard_map/all_to_all | solution.py:266
  16.0 18.9 %all-to-all-start = ((bf16[8,128,512]{2,1,0:T(8,128)(2,1)}), bf16[8,128,512]{2,1,0:T(8,128)(2,1)S(1)}, u32[]{:S(2)}, u32[]{:S(2)}) async-start(bf16[8,128,512]{2,1,0:T(8,128)(2,1)} %shard_map.85), calls=%async_computation | async-start | bytes 2097152 | tf_op jit(solution)/shard_map/all_to_all | solution.py:266
  19.5 16.1 %collective-permute-start = (bf16[8,128,256]{2,1,0:T(8,128)(2,1)S(1)}, bf16[8,128,256]{2,1,0:T(8,128)(2,1)S(1)}, u32[]{:S(2)}, u32[]{:S(2)}) collective-permute-start(bf16[8,128,256]{2,1,0:T(8,128)(2,1)S(1)} %all-to-all-done.1.own_ref), channel_id=1, source_target_pairs={{0,8},{2,10},{4,12},{6,14},{8,16},{10,18},{12,20},{14,22},{16,24},... | collective-permute-start | bytes 1572872 | tf_op jit(solution)/shard_map/ppermute | solution.py:271
  23.1 12.6 %copy-start = (s32[32]{0:T(128)S(1)}, s32[32]{0:T(128)}, u32[]{:S(2)}) copy-start(s32[32]{0:T(128)} %doc_ref.1) | copy-start | bytes 388
  23.1 12.6 %copy-start.1 = (s32[32]{0:T(128)S(1)}, s32[32]{0:T(128)}, u32[]{:S(2)}) copy-start(s32[32]{0:T(128)} %band_ref.1) | copy-start | bytes 388
  45.3 15.5 %collective-permute-start.1 = (bf16[8,128,256]{2,1,0:T(8,128)(2,1)}, bf16[8,128,256]{2,1,0:T(8,128)(2,1)S(1)}, u32[]{:S(2)}, u32[]{:S(2)}) collective-permute-start(bf16[8,128,256]{2,1,0:T(8,128)(2,1)} %get-tuple-element.10), channel_id=1, source_target_pairs={{8,0},{10,2},{12,4},{14,6},{16,8},{18,10},{20,12},{22,14},{24,16},... | collective-permute-start | bytes 1572872 | tf_op jit(solution)/shard_map/ppermute | solution.py:275
  47.2 14.5 %all-to-all-start.2 = ((bf16[8,128,256]{2,1,0:T(8,128)(2,1)}), bf16[8,128,256]{2,1,0:T(8,128)(2,1)S(1)}, u32[]{:S(2)}, u32[]{:S(2)}) async-start(bf16[8,128,256]{2,1,0:T(8,128)(2,1)} %get-tuple-element.8), calls=%async_computation.2 | async-start | bytes 1048576 | tf_op jit(solution)/shard_map/all_to_all | solution.py:266
  61.7 13.4 %all-to-all-start.3 = ((bf16[8,128,256]{2,1,0:T(8,128)(2,1)}), bf16[8,128,256]{2,1,0:T(8,128)(2,1)S(1)}, u32[]{:S(2)}, u32[]{:S(2)}) async-start(bf16[8,128,256]{2,1,0:T(8,128)(2,1)} %add_convert_fusion), calls=%async_computation.3 | async-start | bytes 1048576 | tf_op jit(solution)/shard_map/all_to_all | solution.py:266
where the time goes:
time: 76.7 us; the launch traced here: 76 us
  waiting for transfers between devices  38.7 us (50%)
  starting transfers between devices  20.2 us (26%)
  Pallas kernels  15.4 us (20%)
  other arithmetic  0.92 us (1%)
    all_to_all x4, waiting for transfers between devices, exchange(): lax.all_to_all(value, axes, split_axis=0, concat_axis=0, axis_index_group...  28.3 us
    all_to_all x4, starting transfers between devices, exchange(): lax.all_to_all(value, axes, split_axis=0, concat_axis=0, axis_index_group...  14.8 us
    ppermute x1, waiting for transfers between devices, per_device(): lax.ppermute(dkv_halo, 'blk', [(s + step, s) for s in range(spans - step)])  9.68 us
    pallas_call x1, Pallas kernels, attend(): pl.pallas_call(attend_kernel, in_specs=[smem] * 3 + [vmem] * 3, out_specs...  9.64 us
    pallas_call x2, Pallas kernels, pack(): pl.pallas_call(pack_kernel, in_specs=[hbm] * 2, out_specs=hbm, out_shape=...  3.98 us
    ppermute x1, starting transfers between devices, per_device(): halo = lax.ppermute(kv, 'blk', [(s, s + step) for s in range(spans - step)])  3.52 us
    ppermute x1, starting transfers between devices, per_device(): lax.ppermute(dkv_halo, 'blk', [(s + step, s) for s in range(spans - step)])  1.91 us
    pallas_call x2, Pallas kernels, unpack(): pl.pallas_call(unpack_kernel, in_specs=[pl.BlockSpec(memory_space=pltpu.V...  1.76 us
  transfers between devices with their start and end apart: 6, of which 5 were waited for; matrix products, arithmetic and copies ran while one was open for 1% of the time, Pallas kernels for 4%

commit v1 on v0

--- a/solution.py
+++ b/solution.py
@@ -16,11 +16,10 @@
 SCALE = SCALAR ** (-0.5)
 LOG2E = math.log2(math.e)
 SMALL = 8 * 1024 * 1024
-TOGETHER = 4
+TOGETHER = 2
 
 NT = (((1,), (1,)), ((), ()))
 NN = (((1,), (0,)), ((), ()))
-TN = (((0,), (0,)), ((), ()))
 
 
 def dot(a, b, dims):
@@ -109,7 +108,7 @@
 def attend_kernel(
     chunk_ref, doc_ref, band_ref, qd_ref, own_ref, halo_ref,
     dq_ref, dkv_own_ref, dkv_halo_ref,
-    keys, values, dk, dv,
+    keys, keys_t, values, dk, dv, order, counts,
 ):
     chunk = own_ref.shape[0] * BLOCK
     blocks = chunk // BLOCK
@@ -120,24 +119,31 @@
         keys[rows, :] = halo_ref[j, :, :HEAD]
         values[rows, :] = halo_ref[j, :, HEAD:]
         keys[late, :] = own_ref[j, :, :HEAD]
+        keys_t[:, rows] = halo_ref[j, :, :HEAD].T
+        keys_t[:, late] = own_ref[j, :, :HEAD].T
         values[late, :] = own_ref[j, :, HEAD:]
     dk[...] = jnp.zeros_like(dk)
     dv[...] = jnp.zeros_like(dv)
     first = chunk_ref[0] * blocks
 
-    def reach_of(i):
-        index = first + i
-        own_band = band_ref[index]
-        own_doc = doc_ref[index]
-        reach = jnp.int32(0)
-        for back in range(1, WB + 1):
-            seen = (
-                (back <= own_band)
-                & (index >= back)
-                & (doc_ref[jnp.maximum(index - back, 0)] == own_doc)
-            )
-            reach = reach + seen.astype(jnp.int32)
-        return reach
+    length = jnp.int32(0)
+    for back in range(1, WB + 1):
+        same = (first >= back) & (doc_ref[jnp.maximum(first - back, 0)] == doc_ref[first])
+        length = length + same.astype(jnp.int32)
+    seen = []
+    for i in range(blocks):
+        if i > 0:
+            same = doc_ref[first + i] == doc_ref[first + i - 1]
+            length = jnp.where(same, length + 1, 0)
+        seen.append(jnp.minimum(band_ref[first + i], length) + 1)
+    for i in range(blocks):
+        rank = jnp.int32(0)
+        for j in range(blocks):
+            if j != i:
+                below = seen[j] <= seen[i] if j < i else seen[j] < seen[i]
+                rank = rank + below.astype(jnp.int32)
+        order[rank] = i
+        counts[rank] = seen[i]
 
     rows = q_heads * BLOCK
 
@@ -150,7 +156,7 @@
     def fold(x, reduce):
         return reduce(x.reshape(BLOCK // 8, 8, rows), axis=0)
 
-    def work(count, members, reaches):
+    def work(count, members, sizes):
         span = count * BLOCK
         windows = [
             pl.ds(pl.multiple_of((i + WB + 1 - count) * BLOCK, BLOCK), span) for i in members
@@ -166,10 +172,10 @@
         key_pos = lax.broadcasted_iota(jnp.int32, (BLOCK, rows), 0)
         query_pos = lax.broadcasted_iota(jnp.int32, (BLOCK, rows), 1) % BLOCK
         causal = key_pos <= query_pos
-        probs, probs_b, dprob = {}, {}, {}
+        probs_b, dprob = {}, {}
         for n in lanes:
             scores[n][-1] = jnp.where(causal, scores[n][-1], -jnp.inf)
-            seen = [count - 1 - b <= reaches[n] for b in range(count)]
+            seen = [count - b <= sizes[n] for b in range(count)]
             tops = [
                 jnp.where(seen[b], fold(x, jnp.max), -jnp.inf) for b, x in enumerate(scores[n])
             ]
@@ -179,8 +185,7 @@
             expo = [jnp.exp2((x - y) * (SCALE * LOG2E)) for x, y in zip(scores[n], shift)]
             total = functools.reduce(jnp.add, [fold(x, jnp.sum) for x in expo])
             inverse = 1.0 / jnp.sum(total, axis=0, keepdims=True)
-            probs[n] = [x * inverse for x in expo]
-            probs_b[n] = [x.astype(jnp.bfloat16) for x in probs[n]]
+            probs_b[n] = [(x * inverse).astype(jnp.bfloat16) for x in expo]
         dscore = {}
         for n in lanes:
             dv[windows[n], :] += dot(jnp.concatenate(probs_b[n], axis=0), grad[n], NN)
@@ -194,25 +199,24 @@
             delta = jnp.sum(delta, axis=0, keepdims=True)
             dscore[n] = jnp.concatenate(
                 [
-                    (x * (y - delta)).astype(jnp.bfloat16)
-                    for x, y in zip(probs[n], dprob[n])
+                    (x.astype(jnp.float32) * (y - delta)).astype(jnp.bfloat16)
+                    for x, y in zip(probs_b[n], dprob[n])
                 ],
                 axis=0,
             )
         for n, i in enumerate(members):
             dk[windows[n], :] += dot(dscore[n], query[n], NN)
-            query_grad = dot(dscore[n], keys[windows[n], :], TN) * SCALE
+            query_grad = dot(keys_t[:, windows[n]], dscore[n], NN) * SCALE
             for h in range(q_heads):
                 dq_ref[i, :, h * HEAD : (h + 1) * HEAD] = query_grad[
-                    h * BLOCK : (h + 1) * BLOCK, :
-                ].astype(dq_ref.dtype)
+                    :, h * BLOCK : (h + 1) * BLOCK
+                ].T.astype(dq_ref.dtype)
 
     def one_step(step, carry):
-        members = [step * TOGETHER + n for n in range(TOGETHER)]
-        reaches = [reach_of(i) for i in members]
-        widest = functools.reduce(jnp.maximum, reaches) + 1
+        members = [order[step * TOGETHER + n] for n in range(TOGETHER)]
+        sizes = [counts[step * TOGETHER + n] for n in range(TOGETHER)]
         for count in range(1, WB + 2):
-            pl.when(widest == count)(functools.partial(work, count, members, reaches))
+            pl.when(sizes[-1] == count)(functools.partial(work, count, members, sizes))
         return carry
 
     lax.fori_loop(0, blocks // TOGETHER, one_step, 0)
@@ -243,12 +247,39 @@
         ],
         scratch_shapes=[
             pltpu.VMEM((total, HEAD), jnp.bfloat16),
+            pltpu.VMEM((HEAD, total), jnp.bfloat16),
             pltpu.VMEM((total, HEAD), jnp.bfloat16),
             pltpu.VMEM((total, HEAD), jnp.float32),
             pltpu.VMEM((total, HEAD), jnp.float32),
+            pltpu.SMEM((blocks,), jnp.int32),
+            pltpu.SMEM((blocks,), jnp.int32),
         ],
         compiler_params=pltpu.CompilerParams(vmem_limit_bytes=40 * 1024 * 1024),
     )(chunk_index, doc_ids, band, queries_grads, own, halo)
+
+
+def add_kernel(own_ref, spill_ref, out_ref, slabs, sems):
+    copies = []
+    for j in range(out_ref.shape[0]):
+        slabs[j] = (own_ref[j] + spill_ref[j].astype(jnp.float32)).astype(slabs.dtype)
+        copies.append(pltpu.make_async_copy(slabs.at[j], out_ref.at[j], sems.at[j]))
+        copies[j].start()
+    for copy in copies:
+        copy.wait()
+
+
+def add_spill(own, spill):
+    return pl.pallas_call(
+        add_kernel,
+        in_specs=[pl.BlockSpec(memory_space=pltpu.VMEM)] * 2,
+        out_specs=pl.BlockSpec(memory_space=pl.ANY),
+        out_shape=jax.ShapeDtypeStruct(spill.shape, spill.dtype),
+        scratch_shapes=[
+            pltpu.VMEM(spill.shape, spill.dtype),
+            pltpu.SemaphoreType.DMA((spill.shape[0],)),
+        ],
+        compiler_params=pltpu.CompilerParams(vmem_limit_bytes=SMALL),
+    )(own, spill)
 
 
 def per_device(queries, keys, values, upstream, doc_ids, band):
@@ -274,7 +305,7 @@
     dq, dkv_own, dkv_halo = attend(chunk_index, doc_ids, band, qd, kv, halo)
     spill = lax.ppermute(dkv_halo, "blk", [(s + step, s) for s in range(spans - step)])
     query_out = exchange(dq)
-    dkv = exchange((dkv_own + spill.astype(jnp.float32)).astype(jnp.bfloat16))
+    dkv = exchange(add_spill(dkv_own, spill))
 
     return (*unpack(query_out, 1), *unpack(dkv, 2))
 

time: 76.7 us -> 77 us (level)
  the two profiles are of different devices: /device:TPU:16 before, /device:TPU:0 now
where the time goes in v1:
time: 77 us; the launch traced here: 75.7 us
  waiting for transfers between devices  41.7 us (54%)
  starting transfers between devices  21 us (27%)
  Pallas kernels  12.2 us (16%)
    all_to_all x4, waiting for transfers between devices, exchange(): lax.all_to_all(value, axes, split_axis=0, concat_axis=0, axis_index_group...  28.3 us
    all_to_all x4, starting transfers between devices, exchange(): lax.all_to_all(value, axes, split_axis=0, concat_axis=0, axis_index_group...  16.1 us
    ppermute x1, waiting for transfers between devices, per_device(): lax.ppermute(dkv_halo, 'blk', [(s + step, s) for s in range(spans - step)])  13.5 us
    pallas_call x1, Pallas kernels, attend(): pl.pallas_call(attend_kernel, in_specs=[smem] * 3 + [vmem] * 3, out_specs...  5.6 us
    pallas_call x2, Pallas kernels, pack(): pl.pallas_call(pack_kernel, in_specs=[hbm] * 2, out_specs=hbm, out_shape=...  3.98 us
    ppermute x1, starting transfers between devices, per_device(): halo = lax.ppermute(kv, 'blk', [(s, s + step) for s in range(spans - step)])  3.54 us
    pallas_call x2, Pallas kernels, unpack(): pl.pallas_call(unpack_kernel, in_specs=[pl.BlockSpec(memory_space=pltpu.V...  1.76 us
  transfers between devices with their start and end apart: 6, of which 4 were waited for; matrix products, arithmetic and copies ran while one was open for 0% of the time, Pallas kernels for 5%

profile of v1, /device:TPU:0, one launch (start us, length us, event | category | flops | bytes accessed | tf_op | source)
XLA Modules:
  0.0 75.7 jit_solution(17021751787873840366)
XLA Ops:
  0.6 1.8 %shard_map.86 = bf16[8,128,256]{2,1,0:T(8,128)(2,1)} custom-call(bf16[128,1024]{1,0:T(8,128)(2,1)} %a_ref.3, bf16[128,1024]{1,0:T(8,128)(2,1)} %b_ref.3), custom_call_target="tpu_custom_call" | custom-call | tf_op jit(solution)/shard_map/pallas_call | solution.py:69
  2.5 5.2 %all-to-all-start.1 = ((bf16[8,128,256]{2,1,0:T(8,128)(2,1)}), bf16[8,128,256]{2,1,0:T(8,128)(2,1)S(1)}, u32[]{:S(2)}, u32[]{:S(2)}) async-start(bf16[8,128,256]{2,1,0:T(8,128)(2,1)} %shard_map.86), calls=%async_computation.1 | async-start | bytes 1048576 | tf_op jit(solution)/shard_map/all_to_all | solution.py:297
  7.7 2.1 %shard_map.85 = bf16[8,128,512]{2,1,0:T(8,128)(2,1)} custom-call(bf16[128,2048]{1,0:T(8,128)(2,1)} %a_ref.2, bf16[128,2048]{1,0:T(8,128)(2,1)} %b_ref.2), custom_call_target="tpu_custom_call" | custom-call | tf_op jit(solution)/shard_map/pallas_call | solution.py:69
  9.8 7.6 %all-to-all-done.1.own_ref = bf16[8,128,256]{2,1,0:T(8,128)(2,1)S(1)} async-done(((bf16[8,128,256]{2,1,0:T(8,128)(2,1)}), bf16[8,128,256]{2,1,0:T(8,128)(2,1)S(1)}, u32[]{:S(2)}, u32[]{:S(2)}) %all-to-all-start.1) | async-done | bytes 524320 | tf_op jit(solution)/shard_map/all_to_all | solution.py:297
  17.4 3.6 %all-to-all-start = ((bf16[8,128,512]{2,1,0:T(8,128)(2,1)}), bf16[8,128,512]{2,1,0:T(8,128)(2,1)S(1)}, u32[]{:S(2)}, u32[]{:S(2)}) async-start(bf16[8,128,512]{2,1,0:T(8,128)(2,1)} %shard_map.85), calls=%async_computation | async-start | bytes 2097152 | tf_op jit(solution)/shard_map/all_to_all | solution.py:297
  21.0 3.5 %collective-permute-start = (bf16[8,128,256]{2,1,0:T(8,128)(2,1)S(1)}, bf16[8,128,256]{2,1,0:T(8,128)(2,1)S(1)}, u32[]{:S(2)}, u32[]{:S(2)}) collective-permute-start(bf16[8,128,256]{2,1,0:T(8,128)(2,1)S(1)} %all-to-all-done.1.own_ref), channel_id=1, source_target_pairs={{0,8},{2,10},{4,12},{6,14},{8,16},{10,18},{12,20},{14,22},{16,24},... | collective-permute-start | bytes 1572872 | tf_op jit(solution)/shard_map/ppermute | solution.py:302
  24.5 0.0 copy-start
  24.6 0.0 copy-start.1
  24.6 11.7 %all-to-all-done.qd_ref = bf16[8,128,512]{2,1,0:T(8,128)(2,1)S(1)} async-done(((bf16[8,128,512]{2,1,0:T(8,128)(2,1)}), bf16[8,128,512]{2,1,0:T(8,128)(2,1)S(1)}, u32[]{:S(2)}, u32[]{:S(2)}) %all-to-all-start) | async-done | bytes 1048608 | tf_op jit(solution)/shard_map/all_to_all | solution.py:297
  36.3 0.0 collective-permute-done.halo_ref
  36.3 0.0 copy-done
  36.3 0.0 copy-done.1
  36.3 5.6 %shard_map.87 = (bf16[8,128,256]{2,1,0:T(8,128)(2,1)}, f32[8,128,256]{2,1,0:T(8,128)S(1)}, bf16[8,128,256]{2,1,0:T(8,128)(2,1)}) custom-call(s32[1]{0:T(128)} %bitcast.chunk_ref, s32[32]{0:T(128)S(1)} %copy-done, s32[32]{0:T(128)S(1)} %copy-done.1, bf16[8,128,512]{2,1,0:T(8,128)(2,1)S(1)} %all-to-all-done.qd_ref, ...), custom_call_target="tpu_custom_call" | custom-call | tf_op jit(solution)/shard_map/pallas_call | solution.py:237
  41.9 1.3 %collective-permute-start.1 = (bf16[8,128,256]{2,1,0:T(8,128)(2,1)}, bf16[8,128,256]{2,1,0:T(8,128)(2,1)S(1)}, u32[]{:S(2)}, u32[]{:S(2)}) collective-permute-start(bf16[8,128,256]{2,1,0:T(8,128)(2,1)} %get-tuple-element.10), channel_id=1, source_target_pairs={{8,0},{10,2},{12,4},{14,6},{16,8},{18,10},{20,12},{22,14},{24,16},... | collective-permute-start | bytes 1572872 | tf_op jit(solution)/shard_map/ppermute | solution.py:306
  43.2 3.7 %all-to-all-start.2 = ((bf16[8,128,256]{2,1,0:T(8,128)(2,1)}), bf16[8,128,256]{2,1,0:T(8,128)(2,1)S(1)}, u32[]{:S(2)}, u32[]{:S(2)}) async-start(bf16[8,128,256]{2,1,0:T(8,128)(2,1)} %get-tuple-element.8), calls=%async_computation.2 | async-start | bytes 1048576 | tf_op jit(solution)/shard_map/all_to_all | solution.py:297
  47.0 13.5 %collective-permute-done.1.spill_ref = bf16[8,128,256]{2,1,0:T(8,128)(2,1)S(1)} collective-permute-done((bf16[8,128,256]{2,1,0:T(8,128)(2,1)}, bf16[8,128,256]{2,1,0:T(8,128)(2,1)S(1)}, u32[]{:S(2)}, u32[]{:S(2)}) %collective-permute-start.1) | collective-permute-done | bytes 524320 | tf_op jit(solution)/shard_map/ppermute | solution.py:306
  60.5 0.9 %shard_map.89 = bf16[8,128,256]{2,1,0:T(8,128)(2,1)} custom-call(f32[8,128,256]{2,1,0:T(8,128)S(1)} %get-tuple-element.9.own_ref, bf16[8,128,256]{2,1,0:T(8,128)(2,1)S(1)} %collective-permute-done.1.spill_ref), custom_call_target="tpu_custom_call" | custom-call | tf_op jit(solution)/shard_map/pallas_call | solution.py:272
  61.3 0.0 all-to-all-done.2.in_ref
  61.4 3.6 %all-to-all-start.3 = ((bf16[8,128,256]{2,1,0:T(8,128)(2,1)}), bf16[8,128,256]{2,1,0:T(8,128)(2,1)S(1)}, u32[]{:S(2)}, u32[]{:S(2)}) async-start(bf16[8,128,256]{2,1,0:T(8,128)(2,1)} %shard_map.89), calls=%async_computation.3 | async-start | bytes 1048576 | tf_op jit(solution)/shard_map/all_to_all | solution.py:297
  65.0 0.8 %shard_map.88 = bf16[128,2048]{1,0:T(8,128)(2,1)} custom-call(bf16[8,128,256]{2,1,0:T(8,128)(2,1)S(1)} %all-to-all-done.2.in_ref), custom_call_target="tpu_custom_call" | custom-call | tf_op jit(solution)/shard_map/pallas_call | solution.py:98
  65.9 8.9 %all-to-all-done.3.in_ref = bf16[8,128,256]{2,1,0:T(8,128)(2,1)S(1)} async-done(((bf16[8,128,256]{2,1,0:T(8,128)(2,1)}), bf16[8,128,256]{2,1,0:T(8,128)(2,1)S(1)}, u32[]{:S(2)}, u32[]{:S(2)}) %all-to-all-start.3) | async-done | bytes 524320 | tf_op jit(solution)/shard_map/all_to_all | solution.py:297
  74.8 0.9 %shard_map.90 = (bf16[128,1024]{1,0:T(8,128)(2,1)}, bf16[128,1024]{1,0:T(8,128)(2,1)}) custom-call(bf16[8,128,256]{2,1,0:T(8,128)(2,1)S(1)} %all-to-all-done.3.in_ref), custom_call_target="tpu_custom_call" | custom-call | tf_op jit(solution)/shard_map/pallas_call | solution.py:98
Async XLA Ops:
  2.5 14.9 %all-to-all-start.1 = ((bf16[8,128,256]{2,1,0:T(8,128)(2,1)}), bf16[8,128,256]{2,1,0:T(8,128)(2,1)S(1)}, u32[]{:S(2)}, u32[]{:S(2)}) async-start(bf16[8,128,256]{2,1,0:T(8,128)(2,1)} %shard_map.86), calls=%async_computation.1 | async-start | bytes 1048576 | tf_op jit(solution)/shard_map/all_to_all | solution.py:297
  17.4 18.9 %all-to-all-start = ((bf16[8,128,512]{2,1,0:T(8,128)(2,1)}), bf16[8,128,512]{2,1,0:T(8,128)(2,1)S(1)}, u32[]{:S(2)}, u32[]{:S(2)}) async-start(bf16[8,128,512]{2,1,0:T(8,128)(2,1)} %shard_map.85), calls=%async_computation | async-start | bytes 2097152 | tf_op jit(solution)/shard_map/all_to_all | solution.py:297
  21.0 15.3 %collective-permute-start = (bf16[8,128,256]{2,1,0:T(8,128)(2,1)S(1)}, bf16[8,128,256]{2,1,0:T(8,128)(2,1)S(1)}, u32[]{:S(2)}, u32[]{:S(2)}) collective-permute-start(bf16[8,128,256]{2,1,0:T(8,128)(2,1)S(1)} %all-to-all-done.1.own_ref), channel_id=1, source_target_pairs={{0,8},{2,10},{4,12},{6,14},{8,16},{10,18},{12,20},{14,22},{16,24},... | collective-permute-start | bytes 1572872 | tf_op jit(solution)/shard_map/ppermute | solution.py:302
  24.5 11.8 %copy-start = (s32[32]{0:T(128)S(1)}, s32[32]{0:T(128)}, u32[]{:S(2)}) copy-start(s32[32]{0:T(128)} %doc_ref.1) | copy-start | bytes 388
  24.6 11.8 %copy-start.1 = (s32[32]{0:T(128)S(1)}, s32[32]{0:T(128)}, u32[]{:S(2)}) copy-start(s32[32]{0:T(128)} %band_ref.1) | copy-start | bytes 388
  41.9 18.5 %collective-permute-start.1 = (bf16[8,128,256]{2,1,0:T(8,128)(2,1)}, bf16[8,128,256]{2,1,0:T(8,128)(2,1)S(1)}, u32[]{:S(2)}, u32[]{:S(2)}) collective-permute-start(bf16[8,128,256]{2,1,0:T(8,128)(2,1)} %get-tuple-element.10), channel_id=1, source_target_pairs={{8,0},{10,2},{12,4},{14,6},{16,8},{18,10},{20,12},{22,14},{24,16},... | collective-permute-start | bytes 1572872 | tf_op jit(solution)/shard_map/ppermute | solution.py:306
  43.2 18.1 %all-to-all-start.2 = ((bf16[8,128,256]{2,1,0:T(8,128)(2,1)}), bf16[8,128,256]{2,1,0:T(8,128)(2,1)S(1)}, u32[]{:S(2)}, u32[]{:S(2)}) async-start(bf16[8,128,256]{2,1,0:T(8,128)(2,1)} %get-tuple-element.8), calls=%async_computation.2 | async-start | bytes 1048576 | tf_op jit(solution)/shard_map/all_to_all | solution.py:297
  61.4 13.4 %all-to-all-start.3 = ((bf16[8,128,256]{2,1,0:T(8,128)(2,1)}), bf16[8,128,256]{2,1,0:T(8,128)(2,1)S(1)}, u32[]{:S(2)}, u32[]{:S(2)}) async-start(bf16[8,128,256]{2,1,0:T(8,128)(2,1)} %shard_map.89), calls=%async_computation.3 | async-start | bytes 1048576 | tf_op jit(solution)/shard_map/all_to_all | solution.py:297

commit v2 on v1

--- a/solution.py
+++ b/solution.py
@@ -34,48 +34,27 @@
         copy.wait()
 
 
-def pack_kernel(a_ref, b_ref, out_ref, slabs, in_sems, out_sems):
-    heads = out_ref.shape[0]
+def pack_kernel(a_ref, b_ref, out_ref, sems):
     width = out_ref.shape[2] // 2
-    reads = [
+    run_copies(
         [
-            pltpu.make_async_copy(
-                ref.at[:, pl.ds(h * width, width)],
-                slabs.at[h, :, pl.ds(n * width, width)],
-                in_sems.at[2 * h + n],
-            )
+            (ref.at[:, pl.ds(h * width, width)], out_ref.at[h, :, pl.ds(n * width, width)])
+            for h in range(out_ref.shape[0])
             for n, ref in enumerate((a_ref, b_ref))
-        ]
-        for h in range(heads)
-    ]
-    writes = [
-        pltpu.make_async_copy(slabs.at[h], out_ref.at[h], out_sems.at[h]) for h in range(heads)
-    ]
-    for pair in reads:
-        for copy in pair:
-            copy.start()
-    for pair, write in zip(reads, writes):
-        for copy in pair:
-            copy.wait()
-        write.start()
-    for write in writes:
-        write.wait()
+        ],
+        sems,
+    )
 
 
 def pack(a, b, heads):
     tokens, cols = a.shape
-    hbm = pl.BlockSpec(memory_space=pl.ANY)
-    shape = (heads, tokens, 2 * cols // heads)
     return pl.pallas_call(
         pack_kernel,
-        in_specs=[hbm] * 2,
-        out_specs=hbm,
-        out_shape=jax.ShapeDtypeStruct(shape, a.dtype),
-        scratch_shapes=[
-            pltpu.VMEM(shape, a.dtype),
-            pltpu.SemaphoreType.DMA((2 * heads,)),
-            pltpu.SemaphoreType.DMA((heads,)),
-        ],
+        in_specs=[pl.BlockSpec(memory_space=pltpu.VMEM)] * 2,
+        out_specs=pl.BlockSpec(memory_space=pl.ANY),
+        out_shape=jax.ShapeDtypeStruct((heads, tokens, 2 * cols // heads), a.dtype),
+        scratch_shapes=[pltpu.SemaphoreType.DMA((2 * heads,))],
+        compiler_params=pltpu.CompilerParams(vmem_limit_bytes=SMALL),
     )(a, b)
 
 
@@ -105,27 +84,11 @@
     )(value)
 
 
-def attend_kernel(
-    chunk_ref, doc_ref, band_ref, qd_ref, own_ref, halo_ref,
-    dq_ref, dkv_own_ref, dkv_halo_ref,
-    keys, keys_t, values, dk, dv, order, counts,
-):
-    chunk = own_ref.shape[0] * BLOCK
-    blocks = chunk // BLOCK
-    q_heads = qd_ref.shape[2] // (2 * HEAD)
-    for j in range(blocks):
-        rows = slice(j * BLOCK, (j + 1) * BLOCK)
-        late = slice(WINDOW + j * BLOCK, WINDOW + (j + 1) * BLOCK)
-        keys[rows, :] = halo_ref[j, :, :HEAD]
-        values[rows, :] = halo_ref[j, :, HEAD:]
-        keys[late, :] = own_ref[j, :, :HEAD]
-        keys_t[:, rows] = halo_ref[j, :, :HEAD].T
-        keys_t[:, late] = own_ref[j, :, :HEAD].T
-        values[late, :] = own_ref[j, :, HEAD:]
-    dk[...] = jnp.zeros_like(dk)
-    dv[...] = jnp.zeros_like(dv)
+def prepare_kernel(chunk_ref, doc_ref, band_ref, own_ref, order, counts, keys_t_ref):
+    blocks = own_ref.shape[0]
+    for j in range(blocks):
+        keys_t_ref[:, j * BLOCK : (j + 1) * BLOCK] = own_ref[j, :, :HEAD].T
     first = chunk_ref[0] * blocks
-
     length = jnp.int32(0)
     for back in range(1, WB + 1):
         same = (first >= back) & (doc_ref[jnp.maximum(first - back, 0)] == doc_ref[first])
@@ -145,6 +108,46 @@
         order[rank] = i
         counts[rank] = seen[i]
 
+
+def prepare(chunk_index, doc_ids, band, own):
+    blocks = own.shape[0]
+    smem = pl.BlockSpec(memory_space=pltpu.SMEM)
+    vmem = pl.BlockSpec(memory_space=pltpu.VMEM)
+    return pl.pallas_call(
+        prepare_kernel,
+        in_specs=[smem] * 3 + [vmem],
+        out_specs=[smem] * 2 + [vmem],
+        out_shape=[jax.ShapeDtypeStruct((blocks,), jnp.int32)] * 2
+        + [jax.ShapeDtypeStruct((HEAD, blocks * BLOCK), own.dtype)],
+        compiler_params=pltpu.CompilerParams(vmem_limit_bytes=SMALL),
+    )(chunk_index, doc_ids, band, own)
+
+
+def attend_kernel(
+    order, counts, qd_ref, own_ref, keys_t_ref, halo_ref,
+    dq_ref, dkv_own_ref, dkv_halo_ref,
+    keys, keys_t, values, dk, dv, dq_slabs, halo_slabs, dq_sems, halo_sems,
+):
+    blocks = own_ref.shape[0]
+    q_heads = qd_ref.shape[2] // (2 * HEAD)
+    for j in range(blocks):
+        early = slice(j * BLOCK, (j + 1) * BLOCK)
+        late = slice(WINDOW + j * BLOCK, WINDOW + (j + 1) * BLOCK)
+        keys[early, :] = halo_ref[j, :, :HEAD]
+        values[early, :] = halo_ref[j, :, HEAD:]
+        keys[late, :] = own_ref[j, :, :HEAD]
+        values[late, :] = own_ref[j, :, HEAD:]
+        keys_t[:, early] = halo_ref[j, :, :HEAD].T
+        keys_t[:, late] = keys_t_ref[:, early]
+    dk[...] = jnp.zeros_like(dk)
+    dv[...] = jnp.zeros_like(dv)
+
+    def dq_copy(i):
+        return pltpu.make_async_copy(dq_slabs.at[i], dq_ref.at[i], dq_sems.at[i])
+
+    def halo_copy(j):
+        return pltpu.make_async_copy(halo_slabs.at[j], dkv_halo_ref.at[j], halo_sems.at[j])
+
     rows = q_heads * BLOCK
 
     def stacked(i, offset):
@@ -172,7 +175,7 @@
         key_pos = lax.broadcasted_iota(jnp.int32, (BLOCK, rows), 0)
         query_pos = lax.broadcasted_iota(jnp.int32, (BLOCK, rows), 1) % BLOCK
         causal = key_pos <= query_pos
-        probs_b, dprob = {}, {}
+        probs, probs_b, dprob = {}, {}, {}
         for n in lanes:
             scores[n][-1] = jnp.where(causal, scores[n][-1], -jnp.inf)
             seen = [count - b <= sizes[n] for b in range(count)]
@@ -185,7 +188,8 @@
             expo = [jnp.exp2((x - y) * (SCALE * LOG2E)) for x, y in zip(scores[n], shift)]
             total = functools.reduce(jnp.add, [fold(x, jnp.sum) for x in expo])
             inverse = 1.0 / jnp.sum(total, axis=0, keepdims=True)
-            probs_b[n] = [(x * inverse).astype(jnp.bfloat16) for x in expo]
+            probs[n] = [x * inverse for x in expo]
+            probs_b[n] = [x.astype(jnp.bfloat16) for x in probs[n]]
         dscore = {}
         for n in lanes:
             dv[windows[n], :] += dot(jnp.concatenate(probs_b[n], axis=0), grad[n], NN)
@@ -199,8 +203,8 @@
             delta = jnp.sum(delta, axis=0, keepdims=True)
             dscore[n] = jnp.concatenate(
                 [
-                    (x.astype(jnp.float32) * (y - delta)).astype(jnp.bfloat16)
-                    for x, y in zip(probs_b[n], dprob[n])
+                    (x * (y - delta)).astype(jnp.bfloat16)
+                    for x, y in zip(probs[n], dprob[n])
                 ],
                 axis=0,
             )
@@ -208,9 +212,10 @@
             dk[windows[n], :] += dot(dscore[n], query[n], NN)
             query_grad = dot(keys_t[:, windows[n]], dscore[n], NN) * SCALE
             for h in range(q_heads):
-                dq_ref[i, :, h * HEAD : (h + 1) * HEAD] = query_grad[
+                dq_slabs[i, :, h * HEAD : (h + 1) * HEAD] = query_grad[
                     :, h * BLOCK : (h + 1) * BLOCK
                 ].T.astype(dq_ref.dtype)
+            dq_copy(i).start()
 
     def one_step(step, carry):
         members = [order[step * TOGETHER + n] for n in range(TOGETHER)]
@@ -221,12 +226,18 @@
 
     lax.fori_loop(0, blocks // TOGETHER, one_step, 0)
     for j in range(blocks):
-        rows = slice(j * BLOCK, (j + 1) * BLOCK)
+        early = slice(j * BLOCK, (j + 1) * BLOCK)
+        halo_slabs[j, :, :HEAD] = (dk[early, :] * SCALE).astype(halo_slabs.dtype)
+        halo_slabs[j, :, HEAD:] = dv[early, :].astype(halo_slabs.dtype)
+        halo_copy(j).start()
+    for j in range(blocks):
         late = slice(WINDOW + j * BLOCK, WINDOW + (j + 1) * BLOCK)
-        dkv_halo_ref[j, :, :HEAD] = (dk[rows, :] * SCALE).astype(dkv_halo_ref.dtype)
-        dkv_halo_ref[j, :, HEAD:] = dv[rows, :].astype(dkv_halo_ref.dtype)
         dkv_own_ref[j, :, :HEAD] = dk[late, :] * SCALE
         dkv_own_ref[j, :, HEAD:] = dv[late, :]
+    for i in range(blocks):
+        dq_copy(i).wait()
+    for j in range(blocks):
+        halo_copy(j).wait()
 
 
 def attend(chunk_index, doc_ids, band, queries_grads, own, halo):
@@ -234,14 +245,15 @@
     total = WINDOW + blocks * BLOCK
     smem = pl.BlockSpec(memory_space=pltpu.SMEM)
     vmem = pl.BlockSpec(memory_space=pltpu.VMEM)
+    hbm = pl.BlockSpec(memory_space=pl.ANY)
+    order, counts, keys_t = prepare(chunk_index, doc_ids, band, own)
+    dq = jax.ShapeDtypeStruct((blocks, BLOCK, queries_grads.shape[2] // 2), jnp.bfloat16)
     return pl.pallas_call(
         attend_kernel,
-        in_specs=[smem] * 3 + [vmem] * 3,
-        out_specs=[vmem] * 3,
+        in_specs=[smem] * 2 + [vmem] * 4,
+        out_specs=[hbm, vmem, hbm],
         out_shape=[
-            jax.ShapeDtypeStruct(
-                (blocks, BLOCK, queries_grads.shape[2] // 2), jnp.bfloat16
-            ),
+            dq,
             jax.ShapeDtypeStruct(own.shape, jnp.float32),
             jax.ShapeDtypeStruct(own.shape, jnp.bfloat16),
         ],
@@ -251,11 +263,13 @@
             pltpu.VMEM((total, HEAD), jnp.bfloat16),
             pltpu.VMEM((total, HEAD), jnp.float32),
             pltpu.VMEM((total, HEAD), jnp.float32),
-            pltpu.SMEM((blocks,), jnp.int32),
-            pltpu.SMEM((blocks,), jnp.int32),
+            pltpu.VMEM(dq.shape, dq.dtype),
+            pltpu.VMEM(own.shape, jnp.bfloat16),
+            pltpu.SemaphoreType.DMA((blocks,)),
+            pltpu.SemaphoreType.DMA((blocks,)),
         ],
         compiler_params=pltpu.CompilerParams(vmem_limit_bytes=40 * 1024 * 1024),
-    )(chunk_index, doc_ids, band, queries_grads, own, halo)
+    )(order, counts, queries_grads, own, keys_t, halo)
 
 
 def add_kernel(own_ref, spill_ref, out_ref, slabs, sems):

time: 77 us -> 76.7 us (level)
  local copies, waits for them, and re-layouts: 0.01 us -> 2.56 us
  waiting for transfers between devices: 41.7 us -> 39.7 us
    unnamed x4 -> x12, local copies, waits for them, and re-layouts: 0.01 us -> 2.56 us
    ppermute x1, waiting for transfers between devices: 13.5 us -> 12.4 us  [per_device(): lax.ppermute(dkv_halo, 'blk', [(s + step, s) for s in range(spans - step)])]
    all_to_all x4, waiting for transfers between devices: 28.3 us -> 27.3 us  [exchange(): lax.all_to_all(value, axes, split_axis=0, concat_axis=0, axis_index_group...]
    pallas_call x3 -> x4, Pallas kernels: 9.57 us -> 8.87 us  [the longest x1 5.54 us: attend(): pl.pallas_call(attend_kernel, in_specs=[smem] * 2 + [vmem] * 4, out_specs...]
where the time goes in v2:
time: 76.7 us; the launch traced here: 75.6 us
  waiting for transfers between devices  39.7 us (52%)
  starting transfers between devices  21.1 us (28%)
  Pallas kernels  11.5 us (15%)
  local copies, waits for them, and re-layouts  2.56 us (3%)
  between operations  0.78 us (1%)
    all_to_all x4, waiting for transfers between devices, exchange(): lax.all_to_all(value, axes, split_axis=0, concat_axis=0, axis_index_group...  27.3 us
    all_to_all x4, starting transfers between devices, exchange(): lax.all_to_all(value, axes, split_axis=0, concat_axis=0, axis_index_group...  16.3 us
    ppermute x1, waiting for transfers between devices, per_device(): lax.ppermute(dkv_halo, 'blk', [(s + step, s) for s in range(spans - step)])  12.4 us
    pallas_call x1, Pallas kernels, attend(): pl.pallas_call(attend_kernel, in_specs=[smem] * 2 + [vmem] * 4, out_specs...  5.54 us
    ppermute x1, starting transfers between devices, per_device(): halo = lax.ppermute(kv, 'blk', [(s, s + step) for s in range(spans - step)])  3.54 us
    unnamed x12, local copies, waits for them, and re-layouts  2.56 us
    pallas_call x2, Pallas kernels, pack(): pl.pallas_call(pack_kernel, in_specs=[pl.BlockSpec(memory_space=pltpu.VME...  2.05 us
    pallas_call x2, Pallas kernels, unpack(): pl.pallas_call(unpack_kernel, in_specs=[pl.BlockSpec(memory_space=pltpu.V...  1.76 us
  transfers between devices with their start and end apart: 6, of which 4 were waited for; matrix products, arithmetic and copies ran while one was open for 0% of the time, Pallas kernels for 5%

profile of v2, /device:TPU:0, one launch (start us, length us, event | category | flops | bytes accessed | tf_op | source)
XLA Modules:
  0.0 75.6 jit_solution(9312325202116134129)
XLA Ops:
  0.6 0.0 copy-start.2
  0.6 0.9 %copy-done.2 = bf16[128,1024]{1,0:T(8,128)(2,1)S(1)} copy-done((bf16[128,1024]{1,0:T(8,128)(2,1)S(1)}, bf16[128,1024]{1,0:T(8,128)(2,1)}, u32[]{:S(2)}) %copy-start.2) | copy-done | bytes 262168
  1.6 0.0 copy-start.3
  1.6 0.9 %copy-done.3 = bf16[128,1024]{1,0:T(8,128)(2,1)S(1)} copy-done((bf16[128,1024]{1,0:T(8,128)(2,1)S(1)}, bf16[128,1024]{1,0:T(8,128)(2,1)}, u32[]{:S(2)}) %copy-start.3) | copy-done | bytes 262168
  2.5 0.9 %shard_map.85 = bf16[8,128,256]{2,1,0:T(8,128)(2,1)} custom-call(bf16[128,1024]{1,0:T(8,128)(2,1)S(1)} %copy-done.2, bf16[128,1024]{1,0:T(8,128)(2,1)S(1)} %copy-done.3), custom_call_target="tpu_custom_call" | custom-call | tf_op jit(solution)/shard_map/pallas_call | solution.py:51
  3.5 0.0 copy-start
  3.5 0.0 copy-start.1
  3.5 5.3 %all-to-all-start = ((bf16[8,128,256]{2,1,0:T(8,128)(2,1)}), bf16[8,128,256]{2,1,0:T(8,128)(2,1)S(1)}, u32[]{:S(2)}, u32[]{:S(2)}) async-start(bf16[8,128,256]{2,1,0:T(8,128)(2,1)} %shard_map.85), calls=%async_computation | async-start | bytes 1048576 | tf_op jit(solution)/shard_map/all_to_all | solution.py:311
  8.8 0.0 copy-done
  8.8 0.0 copy-done.1
  8.8 1.1 %shard_map.87 = bf16[8,128,512]{2,1,0:T(8,128)(2,1)} custom-call(bf16[128,2048]{1,0:T(8,128)(2,1)S(1)} %copy-done, bf16[128,2048]{1,0:T(8,128)(2,1)S(1)} %copy-done.1), custom_call_target="tpu_custom_call" | custom-call | tf_op jit(solution)/shard_map/pallas_call | solution.py:51
  10.0 8.6 %all-to-all-done.own_ref = bf16[8,128,256]{2,1,0:T(8,128)(2,1)S(1)} async-done(((bf16[8,128,256]{2,1,0:T(8,128)(2,1)}), bf16[8,128,256]{2,1,0:T(8,128)(2,1)S(1)}, u32[]{:S(2)}, u32[]{:S(2)}) %all-to-all-start) | async-done | bytes 524320 | tf_op jit(solution)/shard_map/all_to_all | solution.py:311
  18.5 3.6 %all-to-all-start.1 = ((bf16[8,128,512]{2,1,0:T(8,128)(2,1)}), bf16[8,128,512]{2,1,0:T(8,128)(2,1)S(1)}, u32[]{:S(2)}, u32[]{:S(2)}) async-start(bf16[8,128,512]{2,1,0:T(8,128)(2,1)} %shard_map.87), calls=%async_computation.1 | async-start | bytes 2097152 | tf_op jit(solution)/shard_map/all_to_all | solution.py:311
  22.1 3.5 %collective-permute-start = (bf16[8,128,256]{2,1,0:T(8,128)(2,1)S(1)}, bf16[8,128,256]{2,1,0:T(8,128)(2,1)S(1)}, u32[]{:S(2)}, u32[]{:S(2)}) collective-permute-start(bf16[8,128,256]{2,1,0:T(8,128)(2,1)S(1)} %all-to-all-done.own_ref), channel_id=1, source_target_pairs={{0,8},{2,10},{4,12},{6,14},{8,16},{10,18},{12,20},{14,22},{16,24},... | collective-permute-start | bytes 1572872 | tf_op jit(solution)/shard_map/ppermute | solution.py:316
  25.7 0.0 copy-start.4
  25.7 0.0 copy-start.5
  25.7 0.6 copy-done.4
  26.3 0.0 copy-done.5
  26.3 1.3 %shard_map.86 = (s32[8]{0:T(128)S(1)}, s32[8]{0:T(128)S(1)}, bf16[128,1024]{1,0:T(8,128)(2,1)S(1)}) custom-call(s32[1]{0:T(128)} %bitcast.chunk_ref, s32[32]{0:T(128)S(1)} %copy-done.4, s32[32]{0:T(128)S(1)} %copy-done.5, bf16[8,128,256]{2,1,0:T(8,128)(2,1)S(1)} %all-to-all-done.own_ref), custom_call_target="tpu_custom_call" | custom-call | tf_op jit(solution)/shard_map/pallas_call | solution.py:116
  27.6 9.8 %all-to-all-done.1.qd_ref = bf16[8,128,512]{2,1,0:T(8,128)(2,1)S(1)} async-done(((bf16[8,128,512]{2,1,0:T(8,128)(2,1)}), bf16[8,128,512]{2,1,0:T(8,128)(2,1)S(1)}, u32[]{:S(2)}, u32[]{:S(2)}) %all-to-all-start.1) | async-done | bytes 1048608 | tf_op jit(solution)/shard_map/all_to_all | solution.py:311
  37.4 0.0 collective-permute-done.halo_ref
  37.4 5.5 %shard_map.88 = (bf16[8,128,256]{2,1,0:T(8,128)(2,1)}, f32[8,128,256]{2,1,0:T(8,128)S(1)}, bf16[8,128,256]{2,1,0:T(8,128)(2,1)}) custom-call(s32[8]{0:T(128)S(1)} %get-tuple-element.11.order, s32[8]{0:T(128)S(1)} %get-tuple-element.12.counts, bf16[8,128,512]{2,1,0:T(8,128)(2,1)S(1)} %all-to-all-done.1.qd_ref, bf16[8,128,256]{2,1,0:T(8,128)(2,1)S(1)} %all-to-all-done.own_ref, ...), custom_call_target="tpu_custom_call" | custom-call | tf_op jit(solution)/shard_map/pallas_call | solution.py:251
  43.0 1.3 %collective-permute-start.1 = (bf16[8,128,256]{2,1,0:T(8,128)(2,1)}, bf16[8,128,256]{2,1,0:T(8,128)(2,1)S(1)}, u32[]{:S(2)}, u32[]{:S(2)}) collective-permute-start(bf16[8,128,256]{2,1,0:T(8,128)(2,1)} %get-tuple-element.16), channel_id=1, source_target_pairs={{8,0},{10,2},{12,4},{14,6},{16,8},{18,10},{20,12},{22,14},{24,16},... | collective-permute-start | bytes 1572872 | tf_op jit(solution)/shard_map/ppermute | solution.py:320
  44.3 3.8 %all-to-all-start.2 = ((bf16[8,128,256]{2,1,0:T(8,128)(2,1)}), bf16[8,128,256]{2,1,0:T(8,128)(2,1)S(1)}, u32[]{:S(2)}, u32[]{:S(2)}) async-start(bf16[8,128,256]{2,1,0:T(8,128)(2,1)} %get-tuple-element.14), calls=%async_computation.2 | async-start | bytes 1048576 | tf_op jit(solution)/shard_map/all_to_all | solution.py:311
  48.1 12.4 %collective-permute-done.1.spill_ref = bf16[8,128,256]{2,1,0:T(8,128)(2,1)S(1)} collective-permute-done((bf16[8,128,256]{2,1,0:T(8,128)(2,1)}, bf16[8,128,256]{2,1,0:T(8,128)(2,1)S(1)}, u32[]{:S(2)}, u32[]{:S(2)}) %collective-permute-start.1) | collective-permute-done | bytes 524320 | tf_op jit(solution)/shard_map/ppermute | solution.py:320
  60.4 0.9 %shard_map.90 = bf16[8,128,256]{2,1,0:T(8,128)(2,1)} custom-call(f32[8,128,256]{2,1,0:T(8,128)S(1)} %get-tuple-element.15.own_ref, bf16[8,128,256]{2,1,0:T(8,128)(2,1)S(1)} %collective-permute-done.1.spill_ref), custom_call_target="tpu_custom_call" | custom-call | tf_op jit(solution)/shard_map/pallas_call | solution.py:286
  61.3 0.0 all-to-all-done.2.in_ref
  61.3 3.6 %all-to-all-start.3 = ((bf16[8,128,256]{2,1,0:T(8,128)(2,1)}), bf16[8,128,256]{2,1,0:T(8,128)(2,1)S(1)}, u32[]{:S(2)}, u32[]{:S(2)}) async-start(bf16[8,128,256]{2,1,0:T(8,128)(2,1)} %shard_map.90), calls=%async_computation.3 | async-start | bytes 1048576 | tf_op jit(solution)/shard_map/all_to_all | solution.py:311
  65.0 0.8 %shard_map.89 = bf16[128,2048]{1,0:T(8,128)(2,1)} custom-call(bf16[8,128,256]{2,1,0:T(8,128)(2,1)S(1)} %all-to-all-done.2.in_ref), custom_call_target="tpu_custom_call" | custom-call | tf_op jit(solution)/shard_map/pallas_call | solution.py:77
  65.8 8.9 %all-to-all-done.3.in_ref = bf16[8,128,256]{2,1,0:T(8,128)(2,1)S(1)} async-done(((bf16[8,128,256]{2,1,0:T(8,128)(2,1)}), bf16[8,128,256]{2,1,0:T(8,128)(2,1)S(1)}, u32[]{:S(2)}, u32[]{:S(2)}) %all-to-all-start.3) | async-done | bytes 524320 | tf_op jit(solution)/shard_map/all_to_all | solution.py:311
  74.7 0.9 %shard_map.91 = (bf16[128,1024]{1,0:T(8,128)(2,1)}, bf16[128,1024]{1,0:T(8,128)(2,1)}) custom-call(bf16[8,128,256]{2,1,0:T(8,128)(2,1)S(1)} %all-to-all-done.3.in_ref), custom_call_target="tpu_custom_call" | custom-call | tf_op jit(solution)/shard_map/pallas_call | solution.py:77
Async XLA Ops:
  0.6 1.0 %copy-start.2 = (bf16[128,1024]{1,0:T(8,128)(2,1)S(1)}, bf16[128,1024]{1,0:T(8,128)(2,1)}, u32[]{:S(2)}) copy-start(bf16[128,1024]{1,0:T(8,128)(2,1)} %a_ref.2) | copy-start | bytes 786436
  1.6 0.9 %copy-start.3 = (bf16[128,1024]{1,0:T(8,128)(2,1)S(1)}, bf16[128,1024]{1,0:T(8,128)(2,1)}, u32[]{:S(2)}) copy-start(bf16[128,1024]{1,0:T(8,128)(2,1)} %b_ref.2) | copy-start | bytes 786436
  3.5 5.3 %copy-start = (bf16[128,2048]{1,0:T(8,128)(2,1)S(1)}, bf16[128,2048]{1,0:T(8,128)(2,1)}, u32[]{:S(2)}) copy-start(bf16[128,2048]{1,0:T(8,128)(2,1)} %a_ref.3) | copy-start | bytes 1572868
  3.5 5.3 %copy-start.1 = (bf16[128,2048]{1,0:T(8,128)(2,1)S(1)}, bf16[128,2048]{1,0:T(8,128)(2,1)}, u32[]{:S(2)}) copy-start(bf16[128,2048]{1,0:T(8,128)(2,1)} %b_ref.3) | copy-start | bytes 1572868
  3.5 15.1 %all-to-all-start = ((bf16[8,128,256]{2,1,0:T(8,128)(2,1)}), bf16[8,128,256]{2,1,0:T(8,128)(2,1)S(1)}, u32[]{:S(2)}, u32[]{:S(2)}) async-start(bf16[8,128,256]{2,1,0:T(8,128)(2,1)} %shard_map.85), calls=%async_computation | async-start | bytes 1048576 | tf_op jit(solution)/shard_map/all_to_all | solution.py:311
  18.5 18.9 %all-to-all-start.1 = ((bf16[8,128,512]{2,1,0:T(8,128)(2,1)}), bf16[8,128,512]{2,1,0:T(8,128)(2,1)S(1)}, u32[]{:S(2)}, u32[]{:S(2)}) async-start(bf16[8,128,512]{2,1,0:T(8,128)(2,1)} %shard_map.87), calls=%async_computation.1 | async-start | bytes 2097152 | tf_op jit(solution)/shard_map/all_to_all | solution.py:311
  22.1 15.3 %collective-permute-start = (bf16[8,128,256]{2,1,0:T(8,128)(2,1)S(1)}, bf16[8,128,256]{2,1,0:T(8,128)(2,1)S(1)}, u32[]{:S(2)}, u32[]{:S(2)}) collective-permute-start(bf16[8,128,256]{2,1,0:T(8,128)(2,1)S(1)} %all-to-all-done.own_ref), channel_id=1, source_target_pairs={{0,8},{2,10},{4,12},{6,14},{8,16},{10,18},{12,20},{14,22},{16,24},... | collective-permute-start | bytes 1572872 | tf_op jit(solution)/shard_map/ppermute | solution.py:316
  25.7 0.7 copy-start.4
  25.7 0.7 copy-start.5
  43.0 17.4 %collective-permute-start.1 = (bf16[8,128,256]{2,1,0:T(8,128)(2,1)}, bf16[8,128,256]{2,1,0:T(8,128)(2,1)S(1)}, u32[]{:S(2)}, u32[]{:S(2)}) collective-permute-start(bf16[8,128,256]{2,1,0:T(8,128)(2,1)} %get-tuple-element.16), channel_id=1, source_target_pairs={{8,0},{10,2},{12,4},{14,6},{16,8},{18,10},{20,12},{22,14},{24,16},... | collective-permute-start | bytes 1572872 | tf_op jit(solution)/shard_map/ppermute | solution.py:320
  44.3 17.0 %all-to-all-start.2 = ((bf16[8,128,256]{2,1,0:T(8,128)(2,1)}), bf16[8,128,256]{2,1,0:T(8,128)(2,1)S(1)}, u32[]{:S(2)}, u32[]{:S(2)}) async-start(bf16[8,128,256]{2,1,0:T(8,128)(2,1)} %get-tuple-element.14), calls=%async_computation.2 | async-start | bytes 1048576 | tf_op jit(solution)/shard_map/all_to_all | solution.py:311
  61.3 13.4 %all-to-all-start.3 = ((bf16[8,128,256]{2,1,0:T(8,128)(2,1)}), bf16[8,128,256]{2,1,0:T(8,128)(2,1)S(1)}, u32[]{:S(2)}, u32[]{:S(2)}) async-start(bf16[8,128,256]{2,1,0:T(8,128)(2,1)} %shard_map.90), calls=%async_computation.3 | async-start | bytes 1048576 | tf_op jit(solution)/shard_map/all_to_all | solution.py:311

commit v3 on v2

--- a/solution.py
+++ b/solution.py
@@ -34,27 +34,48 @@
         copy.wait()
 
 
-def pack_kernel(a_ref, b_ref, out_ref, sems):
+def pack_kernel(a_ref, b_ref, out_ref, slabs, in_sems, out_sems):
+    heads = out_ref.shape[0]
     width = out_ref.shape[2] // 2
-    run_copies(
+    reads = [
         [
-            (ref.at[:, pl.ds(h * width, width)], out_ref.at[h, :, pl.ds(n * width, width)])
-            for h in range(out_ref.shape[0])
+            pltpu.make_async_copy(
+                ref.at[:, pl.ds(h * width, width)],
+                slabs.at[h, :, pl.ds(n * width, width)],
+                in_sems.at[2 * h + n],
+            )
             for n, ref in enumerate((a_ref, b_ref))
-        ],
-        sems,
-    )
+        ]
+        for h in range(heads)
+    ]
+    writes = [
+        pltpu.make_async_copy(slabs.at[h], out_ref.at[h], out_sems.at[h]) for h in range(heads)
+    ]
+    for pair in reads:
+        for copy in pair:
+            copy.start()
+    for pair, write in zip(reads, writes):
+        for copy in pair:
+            copy.wait()
+        write.start()
+    for write in writes:
+        write.wait()
 
 
 def pack(a, b, heads):
     tokens, cols = a.shape
+    hbm = pl.BlockSpec(memory_space=pl.ANY)
+    shape = (heads, tokens, 2 * cols // heads)
     return pl.pallas_call(
         pack_kernel,
-        in_specs=[pl.BlockSpec(memory_space=pltpu.VMEM)] * 2,
-        out_specs=pl.BlockSpec(memory_space=pl.ANY),
-        out_shape=jax.ShapeDtypeStruct((heads, tokens, 2 * cols // heads), a.dtype),
-        scratch_shapes=[pltpu.SemaphoreType.DMA((2 * heads,))],
-        compiler_params=pltpu.CompilerParams(vmem_limit_bytes=SMALL),
+        in_specs=[hbm] * 2,
+        out_specs=hbm,
+        out_shape=jax.ShapeDtypeStruct(shape, a.dtype),
+        scratch_shapes=[
+            pltpu.VMEM(shape, a.dtype),
+            pltpu.SemaphoreType.DMA((2 * heads,)),
+            pltpu.SemaphoreType.DMA((heads,)),
+        ],
     )(a, b)
 
 
@@ -126,17 +147,15 @@
 def attend_kernel(
     order, counts, qd_ref, own_ref, keys_t_ref, halo_ref,
     dq_ref, dkv_own_ref, dkv_halo_ref,
-    keys, keys_t, values, dk, dv, dq_slabs, halo_slabs, dq_sems, halo_sems,
+    kv, keys_t, dk, dv, dq_slabs, halo_slabs, dq_sems, halo_sems,
 ):
     blocks = own_ref.shape[0]
     q_heads = qd_ref.shape[2] // (2 * HEAD)
     for j in range(blocks):
         early = slice(j * BLOCK, (j + 1) * BLOCK)
         late = slice(WINDOW + j * BLOCK, WINDOW + (j + 1) * BLOCK)
-        keys[early, :] = halo_ref[j, :, :HEAD]
-        values[early, :] = halo_ref[j, :, HEAD:]
-        keys[late, :] = own_ref[j, :, :HEAD]
-        values[late, :] = own_ref[j, :, HEAD:]
+        kv[early, :] = halo_ref[j]
+        kv[late, :] = own_ref[j]
         keys_t[:, early] = halo_ref[j, :, :HEAD].T
         keys_t[:, late] = keys_t_ref[:, early]
     dk[...] = jnp.zeros_like(dk)
@@ -171,11 +190,23 @@
 
         query = [stacked(i, 0) for i in members]
         grad = [stacked(i, q_heads) for i in members]
-        scores = [split(dot(keys[windows[n], :], query[n], NT)) for n in lanes]
+        both = []
+        for n in lanes:
+            blank = jnp.zeros_like(query[n])
+            weights = jnp.concatenate(
+                [
+                    jnp.concatenate([query[n], blank], axis=1),
+                    jnp.concatenate([blank, grad[n]], axis=1),
+                ],
+                axis=0,
+            )
+            both.append(dot(kv[windows[n], :], weights, NT))
+        scores = [split(x[:, :rows]) for x in both]
+        dprob = [split(x[:, rows:]) for x in both]
         key_pos = lax.broadcasted_iota(jnp.int32, (BLOCK, rows), 0)
         query_pos = lax.broadcasted_iota(jnp.int32, (BLOCK, rows), 1) % BLOCK
         causal = key_pos <= query_pos
-        probs, probs_b, dprob = {}, {}, {}
+        probs, probs_b = {}, {}
         for n in lanes:
             scores[n][-1] = jnp.where(causal, scores[n][-1], -jnp.inf)
             seen = [count - b <= sizes[n] for b in range(count)]
@@ -184,7 +215,6 @@
             ]
             top = jnp.max(functools.reduce(jnp.maximum, tops), axis=0, keepdims=True)
             shift = [jnp.where(seen[b], top, jnp.inf) for b in range(count)]
-            dprob[n] = split(dot(values[windows[n], :], grad[n], NT))
             expo = [jnp.exp2((x - y) * (SCALE * LOG2E)) for x, y in zip(scores[n], shift)]
             total = functools.reduce(jnp.add, [fold(x, jnp.sum) for x in expo])
             inverse = 1.0 / jnp.sum(total, axis=0, keepdims=True)
@@ -258,9 +288,8 @@
             jax.ShapeDtypeStruct(own.shape, jnp.bfloat16),
         ],
         scratch_shapes=[
-            pltpu.VMEM((total, HEAD), jnp.bfloat16),
+            pltpu.VMEM((total, 2 * HEAD), jnp.bfloat16),
             pltpu.VMEM((HEAD, total), jnp.bfloat16),
-            pltpu.VMEM((total, HEAD), jnp.bfloat16),
             pltpu.VMEM((total, HEAD), jnp.float32),
             pltpu.VMEM((total, HEAD), jnp.float32),
             pltpu.VMEM(dq.shape, dq.dtype),

time: 76.7 us -> 76.1 us (level); the launches traced: 75.6 us -> 76.5 us
  Pallas kernels: 11.5 us -> 14.3 us
  local copies, waits for them, and re-layouts: 2.56 us -> 0.66 us
    pallas_call x2, Pallas kernels: 2.05 us -> 3.99 us  [pack(): pl.pallas_call(pack_kernel, in_specs=[hbm] * 2, out_specs=hbm, out_shape=...]
    unnamed x12 -> x4, local copies, waits for them, and re-layouts: 2.56 us -> 0.66 us
    ppermute x1, waiting for transfers between devices: 12.4 us -> 13.6 us  [per_device(): lax.ppermute(dkv_halo, 'blk', [(s + step, s) for s in range(spans - step)])]
    all_to_all x4, waiting for transfers between devices: 27.3 us -> 26.3 us  [exchange(): lax.all_to_all(value, axes, split_axis=0, concat_axis=0, axis_index_group...]
    pallas_call x1, Pallas kernels: 5.54 us -> 6.37 us  [attend(): pl.pallas_call(attend_kernel, in_specs=[smem] * 2 + [vmem] * 4, out_specs...]
  transfers between devices with their start and end apart: 6 -> 6, of which waited for: 4 -> 4; matrix products, arithmetic and copies ran while one was open for 0% -> 0% of each run, Pallas kernels for 5% -> 7%
where the time goes in v3:
time: 76.1 us; the launch traced here: 76.5 us
  waiting for transfers between devices  39.9 us (52%)
  starting transfers between devices  21 us (28%)
  Pallas kernels  14.3 us (19%)
    all_to_all x4, waiting for transfers between devices, exchange(): lax.all_to_all(value, axes, split_axis=0, concat_axis=0, axis_index_group...  26.3 us
    all_to_all x4, starting transfers between devices, exchange(): lax.all_to_all(value, axes, split_axis=0, concat_axis=0, axis_index_group...  16.1 us
    ppermute x1, waiting for transfers between devices, per_device(): lax.ppermute(dkv_halo, 'blk', [(s + step, s) for s in range(spans - step)])  13.6 us
    pallas_call x1, Pallas kernels, attend(): pl.pallas_call(attend_kernel, in_specs=[smem] * 2 + [vmem] * 4, out_specs...  6.37 us
    pallas_call x2, Pallas kernels, pack(): pl.pallas_call(pack_kernel, in_specs=[hbm] * 2, out_specs=hbm, out_shape=...  3.99 us
    ppermute x1, starting transfers between devices, per_device(): halo = lax.ppermute(kv, 'blk', [(s, s + step) for s in range(spans - step)])  3.54 us
    pallas_call x2, Pallas kernels, unpack(): pl.pallas_call(unpack_kernel, in_specs=[pl.BlockSpec(memory_space=pltpu.V...  1.76 us
  transfers between devices with their start and end apart: 6, of which 4 were waited for; matrix products, arithmetic and copies ran while one was open for 0% of the time, Pallas kernels for 7%

profile of v3, /device:TPU:0, one launch (start us, length us, event | category | flops | bytes accessed | tf_op | source)
XLA Modules:
  0.0 76.5 jit_solution(10419260171575818905)
XLA Ops:
  0.6 1.8 %shard_map.85 = bf16[8,128,256]{2,1,0:T(8,128)(2,1)} custom-call(bf16[128,1024]{1,0:T(8,128)(2,1)} %a_ref.2, bf16[128,1024]{1,0:T(8,128)(2,1)} %b_ref.2), custom_call_target="tpu_custom_call" | custom-call | tf_op jit(solution)/shard_map/pallas_call | solution.py:69
  2.5 5.2 %all-to-all-start = ((bf16[8,128,256]{2,1,0:T(8,128)(2,1)}), bf16[8,128,256]{2,1,0:T(8,128)(2,1)S(1)}, u32[]{:S(2)}, u32[]{:S(2)}) async-start(bf16[8,128,256]{2,1,0:T(8,128)(2,1)} %shard_map.85), calls=%async_computation | async-start | bytes 1048576 | tf_op jit(solution)/shard_map/all_to_all | solution.py:340
  7.7 2.1 %shard_map.87 = bf16[8,128,512]{2,1,0:T(8,128)(2,1)} custom-call(bf16[128,2048]{1,0:T(8,128)(2,1)} %a_ref.3, bf16[128,2048]{1,0:T(8,128)(2,1)} %b_ref.3), custom_call_target="tpu_custom_call" | custom-call | tf_op jit(solution)/shard_map/pallas_call | solution.py:69
  9.8 7.6 %all-to-all-done.own_ref = bf16[8,128,256]{2,1,0:T(8,128)(2,1)S(1)} async-done(((bf16[8,128,256]{2,1,0:T(8,128)(2,1)}), bf16[8,128,256]{2,1,0:T(8,128)(2,1)S(1)}, u32[]{:S(2)}, u32[]{:S(2)}) %all-to-all-start) | async-done | bytes 524320 | tf_op jit(solution)/shard_map/all_to_all | solution.py:340
  17.4 3.6 %all-to-all-start.1 = ((bf16[8,128,512]{2,1,0:T(8,128)(2,1)}), bf16[8,128,512]{2,1,0:T(8,128)(2,1)S(1)}, u32[]{:S(2)}, u32[]{:S(2)}) async-start(bf16[8,128,512]{2,1,0:T(8,128)(2,1)} %shard_map.87), calls=%async_computation.1 | async-start | bytes 2097152 | tf_op jit(solution)/shard_map/all_to_all | solution.py:340
  21.0 3.5 %collective-permute-start = (bf16[8,128,256]{2,1,0:T(8,128)(2,1)S(1)}, bf16[8,128,256]{2,1,0:T(8,128)(2,1)S(1)}, u32[]{:S(2)}, u32[]{:S(2)}) collective-permute-start(bf16[8,128,256]{2,1,0:T(8,128)(2,1)S(1)} %all-to-all-done.own_ref), channel_id=1, source_target_pairs={{0,8},{2,10},{4,12},{6,14},{8,16},{10,18},{12,20},{14,22},{16,24},... | collective-permute-start | bytes 1572872 | tf_op jit(solution)/shard_map/ppermute | solution.py:345
  24.5 0.0 copy-start
  24.6 0.0 copy-start.1
  24.6 0.6 copy-done
  25.2 0.0 copy-done.1
  25.2 1.3 %shard_map.86 = (s32[8]{0:T(128)S(1)}, s32[8]{0:T(128)S(1)}, bf16[128,1024]{1,0:T(8,128)(2,1)S(1)}) custom-call(s32[1]{0:T(128)} %bitcast.chunk_ref, s32[32]{0:T(128)S(1)} %copy-done, s32[32]{0:T(128)S(1)} %copy-done.1, bf16[8,128,256]{2,1,0:T(8,128)(2,1)S(1)} %all-to-all-done.own_ref), custom_call_target="tpu_custom_call" | custom-call | tf_op jit(solution)/shard_map/pallas_call | solution.py:137
  26.5 9.8 %all-to-all-done.1.qd_ref = bf16[8,128,512]{2,1,0:T(8,128)(2,1)S(1)} async-done(((bf16[8,128,512]{2,1,0:T(8,128)(2,1)}), bf16[8,128,512]{2,1,0:T(8,128)(2,1)S(1)}, u32[]{:S(2)}, u32[]{:S(2)}) %all-to-all-start.1) | async-done | bytes 1048608 | tf_op jit(solution)/shard_map/all_to_all | solution.py:340
  36.3 0.0 collective-permute-done.halo_ref
  36.3 6.4 %shard_map.88 = (bf16[8,128,256]{2,1,0:T(8,128)(2,1)}, f32[8,128,256]{2,1,0:T(8,128)S(1)}, bf16[8,128,256]{2,1,0:T(8,128)(2,1)}) custom-call(s32[8]{0:T(128)S(1)} %get-tuple-element.11.order, s32[8]{0:T(128)S(1)} %get-tuple-element.12.counts, bf16[8,128,512]{2,1,0:T(8,128)(2,1)S(1)} %all-to-all-done.1.qd_ref, bf16[8,128,256]{2,1,0:T(8,128)(2,1)S(1)} %all-to-all-done.own_ref, ...), custom_call_target="tpu_custom_call" | custom-call | tf_op jit(solution)/shard_map/pallas_call | solution.py:281
  42.7 1.3 %collective-permute-start.1 = (bf16[8,128,256]{2,1,0:T(8,128)(2,1)}, bf16[8,128,256]{2,1,0:T(8,128)(2,1)S(1)}, u32[]{:S(2)}, u32[]{:S(2)}) collective-permute-start(bf16[8,128,256]{2,1,0:T(8,128)(2,1)} %get-tuple-element.16), channel_id=1, source_target_pairs={{8,0},{10,2},{12,4},{14,6},{16,8},{18,10},{20,12},{22,14},{24,16},... | collective-permute-start | bytes 1572872 | tf_op jit(solution)/shard_map/ppermute | solution.py:349
  44.0 3.8 %all-to-all-start.2 = ((bf16[8,128,256]{2,1,0:T(8,128)(2,1)}), bf16[8,128,256]{2,1,0:T(8,128)(2,1)S(1)}, u32[]{:S(2)}, u32[]{:S(2)}) async-start(bf16[8,128,256]{2,1,0:T(8,128)(2,1)} %get-tuple-element.14), calls=%async_computation.2 | async-start | bytes 1048576 | tf_op jit(solution)/shard_map/all_to_all | solution.py:340
  47.8 13.6 %collective-permute-done.1.spill_ref = bf16[8,128,256]{2,1,0:T(8,128)(2,1)S(1)} collective-permute-done((bf16[8,128,256]{2,1,0:T(8,128)(2,1)}, bf16[8,128,256]{2,1,0:T(8,128)(2,1)S(1)}, u32[]{:S(2)}, u32[]{:S(2)}) %collective-permute-start.1) | collective-permute-done | bytes 524320 | tf_op jit(solution)/shard_map/ppermute | solution.py:349
  61.3 0.9 %shard_map.90 = bf16[8,128,256]{2,1,0:T(8,128)(2,1)} custom-call(f32[8,128,256]{2,1,0:T(8,128)S(1)} %get-tuple-element.15.own_ref, bf16[8,128,256]{2,1,0:T(8,128)(2,1)S(1)} %collective-permute-done.1.spill_ref), custom_call_target="tpu_custom_call" | custom-call | tf_op jit(solution)/shard_map/pallas_call | solution.py:315
  62.2 0.0 all-to-all-done.2.in_ref
  62.2 3.7 %all-to-all-start.3 = ((bf16[8,128,256]{2,1,0:T(8,128)(2,1)}), bf16[8,128,256]{2,1,0:T(8,128)(2,1)S(1)}, u32[]{:S(2)}, u32[]{:S(2)}) async-start(bf16[8,128,256]{2,1,0:T(8,128)(2,1)} %shard_map.90), calls=%async_computation.3 | async-start | bytes 1048576 | tf_op jit(solution)/shard_map/all_to_all | solution.py:340
  65.9 0.8 %shard_map.89 = bf16[128,2048]{1,0:T(8,128)(2,1)} custom-call(bf16[8,128,256]{2,1,0:T(8,128)(2,1)S(1)} %all-to-all-done.2.in_ref), custom_call_target="tpu_custom_call" | custom-call | tf_op jit(solution)/shard_map/pallas_call | solution.py:98
  66.7 8.9 %all-to-all-done.3.in_ref = bf16[8,128,256]{2,1,0:T(8,128)(2,1)S(1)} async-done(((bf16[8,128,256]{2,1,0:T(8,128)(2,1)}), bf16[8,128,256]{2,1,0:T(8,128)(2,1)S(1)}, u32[]{:S(2)}, u32[]{:S(2)}) %all-to-all-start.3) | async-done | bytes 524320 | tf_op jit(solution)/shard_map/all_to_all | solution.py:340
  75.6 0.9 %shard_map.91 = (bf16[128,1024]{1,0:T(8,128)(2,1)}, bf16[128,1024]{1,0:T(8,128)(2,1)}) custom-call(bf16[8,128,256]{2,1,0:T(8,128)(2,1)S(1)} %all-to-all-done.3.in_ref), custom_call_target="tpu_custom_call" | custom-call | tf_op jit(solution)/shard_map/pallas_call | solution.py:98
Async XLA Ops:
  2.5 14.9 %all-to-all-start = ((bf16[8,128,256]{2,1,0:T(8,128)(2,1)}), bf16[8,128,256]{2,1,0:T(8,128)(2,1)S(1)}, u32[]{:S(2)}, u32[]{:S(2)}) async-start(bf16[8,128,256]{2,1,0:T(8,128)(2,1)} %shard_map.85), calls=%async_computation | async-start | bytes 1048576 | tf_op jit(solution)/shard_map/all_to_all | solution.py:340
  17.4 18.9 %all-to-all-start.1 = ((bf16[8,128,512]{2,1,0:T(8,128)(2,1)}), bf16[8,128,512]{2,1,0:T(8,128)(2,1)S(1)}, u32[]{:S(2)}, u32[]{:S(2)}) async-start(bf16[8,128,512]{2,1,0:T(8,128)(2,1)} %shard_map.87), calls=%async_computation.1 | async-start | bytes 2097152 | tf_op jit(solution)/shard_map/all_to_all | solution.py:340
  21.0 15.3 %collective-permute-start = (bf16[8,128,256]{2,1,0:T(8,128)(2,1)S(1)}, bf16[8,128,256]{2,1,0:T(8,128)(2,1)S(1)}, u32[]{:S(2)}, u32[]{:S(2)}) collective-permute-start(bf16[8,128,256]{2,1,0:T(8,128)(2,1)S(1)} %all-to-all-done.own_ref), channel_id=1, source_target_pairs={{0,8},{2,10},{4,12},{6,14},{8,16},{10,18},{12,20},{14,22},{16,24},... | collective-permute-start | bytes 1572872 | tf_op jit(solution)/shard_map/ppermute | solution.py:345
  24.5 0.7 copy-start
  24.6 0.7 copy-start.1
  42.7 18.6 %collective-permute-start.1 = (bf16[8,128,256]{2,1,0:T(8,128)(2,1)}, bf16[8,128,256]{2,1,0:T(8,128)(2,1)S(1)}, u32[]{:S(2)}, u32[]{:S(2)}) collective-permute-start(bf16[8,128,256]{2,1,0:T(8,128)(2,1)} %get-tuple-element.16), channel_id=1, source_target_pairs={{8,0},{10,2},{12,4},{14,6},{16,8},{18,10},{20,12},{22,14},{24,16},... | collective-permute-start | bytes 1572872 | tf_op jit(solution)/shard_map/ppermute | solution.py:349
  44.0 18.2 %all-to-all-start.2 = ((bf16[8,128,256]{2,1,0:T(8,128)(2,1)}), bf16[8,128,256]{2,1,0:T(8,128)(2,1)S(1)}, u32[]{:S(2)}, u32[]{:S(2)}) async-start(bf16[8,128,256]{2,1,0:T(8,128)(2,1)} %get-tuple-element.14), calls=%async_computation.2 | async-start | bytes 1048576 | tf_op jit(solution)/shard_map/all_to_all | solution.py:340
  62.2 13.4 %all-to-all-start.3 = ((bf16[8,128,256]{2,1,0:T(8,128)(2,1)}), bf16[8,128,256]{2,1,0:T(8,128)(2,1)S(1)}, u32[]{:S(2)}, u32[]{:S(2)}) async-start(bf16[8,128,256]{2,1,0:T(8,128)(2,1)} %shard_map.90), calls=%async_computation.3 | async-start | bytes 1048576 | tf_op jit(solution)/shard_map/all_to_all | solution.py:340

commit v4 on v1

--- a/solution.py
+++ b/solution.py
@@ -16,6 +16,7 @@
 SCALE = SCALAR ** (-0.5)
 LOG2E = math.log2(math.e)
 SMALL = 8 * 1024 * 1024
+LARGE = 40 * 1024 * 1024
 TOGETHER = 2
 
 NT = (((1,), (1,)), ((), ()))
@@ -105,27 +106,11 @@
     )(value)
 
 
-def attend_kernel(
-    chunk_ref, doc_ref, band_ref, qd_ref, own_ref, halo_ref,
-    dq_ref, dkv_own_ref, dkv_halo_ref,
-    keys, keys_t, values, dk, dv, order, counts,
-):
-    chunk = own_ref.shape[0] * BLOCK
-    blocks = chunk // BLOCK
-    q_heads = qd_ref.shape[2] // (2 * HEAD)
+def prepare_kernel(chunk_ref, doc_ref, band_ref, own_ref, order, counts, own_t_ref):
+    blocks = own_ref.shape[0]
     for j in range(blocks):
-        rows = slice(j * BLOCK, (j + 1) * BLOCK)
-        late = slice(WINDOW + j * BLOCK, WINDOW + (j + 1) * BLOCK)
-        keys[rows, :] = halo_ref[j, :, :HEAD]
-        values[rows, :] = halo_ref[j, :, HEAD:]
-        keys[late, :] = own_ref[j, :, :HEAD]
-        keys_t[:, rows] = halo_ref[j, :, :HEAD].T
-        keys_t[:, late] = own_ref[j, :, :HEAD].T
-        values[late, :] = own_ref[j, :, HEAD:]
-    dk[...] = jnp.zeros_like(dk)
-    dv[...] = jnp.zeros_like(dv)
+        own_t_ref[:, j * BLOCK : (j + 1) * BLOCK] = own_ref[j, :, :HEAD].T
     first = chunk_ref[0] * blocks
-
     length = jnp.int32(0)
     for back in range(1, WB + 1):
         same = (first >= back) & (doc_ref[jnp.maximum(first - back, 0)] == doc_ref[first])
@@ -136,15 +121,112 @@
             same = doc_ref[first + i] == doc_ref[first + i - 1]
             length = jnp.where(same, length + 1, 0)
         seen.append(jnp.minimum(band_ref[first + i], length) + 1)
+    far = [(seen[i] > i + 1).astype(jnp.int32) for i in range(blocks)]
+    place = [seen[i] + 2 * WB * far[i] for i in range(blocks)]
     for i in range(blocks):
         rank = jnp.int32(0)
         for j in range(blocks):
             if j != i:
-                below = seen[j] <= seen[i] if j < i else seen[j] < seen[i]
+                below = place[j] <= place[i] if j < i else place[j] < place[i]
                 rank = rank + below.astype(jnp.int32)
         order[rank] = i
         counts[rank] = seen[i]
-
+    near = blocks - functools.reduce(jnp.add, far)
+    counts[blocks] = near // TOGETHER
+    counts[blocks + 1] = functools.reduce(
+        jnp.minimum, [jnp.minimum(i + WB + 1 - seen[i], WB) for i in range(blocks)]
+    )
+
+
+def prepare(chunk_index, doc_ids, band, own):
+    blocks = own.shape[0]
+    smem = pl.BlockSpec(memory_space=pltpu.SMEM)
+    vmem = pl.BlockSpec(memory_space=pltpu.VMEM)
+    return pl.pallas_call(
+        prepare_kernel,
+        in_specs=[smem] * 3 + [vmem],
+        out_specs=[smem] * 2 + [vmem],
+        out_shape=[
+            jax.ShapeDtypeStruct((blocks,), jnp.int32),
+            jax.ShapeDtypeStruct((blocks + 2,), jnp.int32),
+            jax.ShapeDtypeStruct((HEAD, blocks * BLOCK), own.dtype),
+        ],
+        compiler_params=pltpu.CompilerParams(vmem_limit_bytes=SMALL),
+    )(chunk_index, doc_ids, band, own)
+
+
+def place_own(own_ref, own_t_ref, kv, keys_t):
+    for j in range(own_ref.shape[0]):
+        late = slice(WINDOW + j * BLOCK, WINDOW + (j + 1) * BLOCK)
+        kv[late, :] = own_ref[j]
+        keys_t[:, late] = own_t_ref[:, j * BLOCK : (j + 1) * BLOCK]
+
+
+def near_kernel(order, counts, qd_ref, own_ref, own_t_ref, dq_ref, sums_ref, kv, keys_t, sums):
+    kv[:WINDOW, :] = jnp.zeros((WINDOW, 2 * HEAD), kv.dtype)
+    keys_t[:, :WINDOW] = jnp.zeros((HEAD, WINDOW), keys_t.dtype)
+    place_own(own_ref, own_t_ref, kv, keys_t)
+    sums[...] = jnp.zeros_like(sums)
+    last = counts[order.shape[0]]
+    attend(0, last, order, counts, qd_ref, kv, keys_t, dq_ref, sums, lambda i: None)
+    sums_ref[...] = sums[WINDOW:, :]
+
+
+def far_kernel(
+    order, counts, qd_ref, own_ref, own_t_ref, halo_ref, dq_near_ref, sums_near_ref, room_ref,
+    dq_ref, sums_ref, spill_ref, kv, keys_t, sums, dq_slabs, spill_slabs, dq_sems, spill_sems,
+):
+    del room_ref
+    sums[:WINDOW, :] = jnp.zeros((WINDOW, 2 * HEAD), sums.dtype)
+    sums[WINDOW:, :] = sums_near_ref[...]
+    blocks = order.shape[0]
+    steps = counts[blocks]
+
+    def dq_copy(slabs, i):
+        return pltpu.make_async_copy(slabs.at[i], dq_ref.at[i], dq_sems.at[i])
+
+    def pass_on(m, carry):
+        dq_copy(dq_near_ref, order[m]).start()
+        return carry
+
+    def fill(j, carry):
+        rows = pl.ds(pl.multiple_of(j * BLOCK, BLOCK), BLOCK)
+        kv[rows, :] = halo_ref[j]
+        keys_t[:, rows] = halo_ref[j, :, :HEAD].T
+        return carry
+
+    def blank(j, carry):
+        rows = pl.ds(pl.multiple_of(j * BLOCK, BLOCK), BLOCK)
+        kv[rows, :] = jnp.zeros((BLOCK, 2 * HEAD), kv.dtype)
+        keys_t[:, rows] = jnp.zeros((HEAD, BLOCK), keys_t.dtype)
+        return carry
+
+    lax.fori_loop(0, steps * TOGETHER, pass_on, 0)
+    lax.fori_loop(0, counts[blocks + 1], blank, 0)
+    lax.fori_loop(counts[blocks + 1], WB, fill, 0)
+    place_own(own_ref, own_t_ref, kv, keys_t)
+    attend(
+        steps, blocks // TOGETHER, order, counts, qd_ref, kv, keys_t, dq_slabs, sums,
+        lambda i: dq_copy(dq_slabs, i).start(),
+    )
+    copies = []
+    for j in range(WB):
+        rows = slice(j * BLOCK, (j + 1) * BLOCK)
+        spill_slabs[j, :, :HEAD] = (sums[rows, :HEAD] * SCALE).astype(spill_slabs.dtype)
+        spill_slabs[j, :, HEAD:] = sums[rows, HEAD:].astype(spill_slabs.dtype)
+        copies.append(
+            pltpu.make_async_copy(spill_slabs.at[j], spill_ref.at[j], spill_sems.at[j])
+        )
+        copies[j].start()
+    sums_ref[...] = sums[WINDOW:, :]
+    for i in range(blocks):
+        dq_copy(dq_slabs, i).wait()
+    for copy in copies:
+        copy.wait()
+
+
+def attend(first_step, last_step, order, counts, qd_ref, kv, keys_t, dq_slabs, sums, ready):
+    q_heads = qd_ref.shape[2] // (2 * HEAD)
     rows = q_heads * BLOCK
 
     def stacked(i, offset):
@@ -168,11 +250,11 @@
 
         query = [stacked(i, 0) for i in members]
         grad = [stacked(i, q_heads) for i in members]
-        scores = [split(dot(keys[windows[n], :], query[n], NT)) for n in lanes]
+        scores = [split(dot(kv[windows[n], :HEAD], query[n], NT)) for n in lanes]
         key_pos = lax.broadcasted_iota(jnp.int32, (BLOCK, rows), 0)
         query_pos = lax.broadcasted_iota(jnp.int32, (BLOCK, rows), 1) % BLOCK
         causal = key_pos <= query_pos
-        probs_b, dprob = {}, {}
+        probs, probs_b, dprob = {}, {}, {}
         for n in lanes:
             scores[n][-1] = jnp.where(causal, scores[n][-1], -jnp.inf)
             seen = [count - b <= sizes[n] for b in range(count)]
@@ -181,14 +263,15 @@
             ]
             top = jnp.max(functools.reduce(jnp.maximum, tops), axis=0, keepdims=True)
             shift = [jnp.where(seen[b], top, jnp.inf) for b in range(count)]
-            dprob[n] = split(dot(values[windows[n], :], grad[n], NT))
+            dprob[n] = split(dot(kv[windows[n], HEAD:], grad[n], NT))
             expo = [jnp.exp2((x - y) * (SCALE * LOG2E)) for x, y in zip(scores[n], shift)]
             total = functools.reduce(jnp.add, [fold(x, jnp.sum) for x in expo])
             inverse = 1.0 / jnp.sum(total, axis=0, keepdims=True)
-            probs_b[n] = [(x * inverse).astype(jnp.bfloat16) for x in expo]
+            probs[n] = [x * inverse for x in expo]
+            probs_b[n] = [x.astype(jnp.bfloat16) for x in probs[n]]
         dscore = {}
         for n in lanes:
-            dv[windows[n], :] += dot(jnp.concatenate(probs_b[n], axis=0), grad[n], NN)
+            sums[windows[n], HEAD:] += dot(jnp.concatenate(probs_b[n], axis=0), grad[n], NN)
             delta = functools.reduce(
                 jnp.add,
                 [
@@ -199,76 +282,92 @@
             delta = jnp.sum(delta, axis=0, keepdims=True)
             dscore[n] = jnp.concatenate(
                 [
-                    (x.astype(jnp.float32) * (y - delta)).astype(jnp.bfloat16)
-                    for x, y in zip(probs_b[n], dprob[n])
+                    (x * (y - delta)).astype(jnp.bfloat16)
+                    for x, y in zip(probs[n], dprob[n])
                 ],
                 axis=0,
             )
         for n, i in enumerate(members):
-            dk[windows[n], :] += dot(dscore[n], query[n], NN)
+            sums[windows[n], :HEAD] += dot(dscore[n], query[n], NN)
             query_grad = dot(keys_t[:, windows[n]], dscore[n], NN) * SCALE
             for h in range(q_heads):
-                dq_ref[i, :, h * HEAD : (h + 1) * HEAD] = query_grad[
+                dq_slabs[i, :, h * HEAD : (h + 1) * HEAD] = query_grad[
                     :, h * BLOCK : (h + 1) * BLOCK
-                ].T.astype(dq_ref.dtype)
+                ].T.astype(dq_slabs.dtype)
+            ready(i)
 
     def one_step(step, carry):
         members = [order[step * TOGETHER + n] for n in range(TOGETHER)]
         sizes = [counts[step * TOGETHER + n] for n in range(TOGETHER)]
+        widest = functools.reduce(jnp.maximum, sizes)
         for count in range(1, WB + 2):
-            pl.when(sizes[-1] == count)(functools.partial(work, count, members, sizes))
+            pl.when(widest == count)(functools.partial(work, count, members, sizes))
         return carry
 
-    lax.fori_loop(0, blocks // TOGETHER, one_step, 0)
-    for j in range(blocks):
-        rows = slice(j * BLOCK, (j + 1) * BLOCK)
-        late = slice(WINDOW + j * BLOCK, WINDOW + (j + 1) * BLOCK)
-        dkv_halo_ref[j, :, :HEAD] = (dk[rows, :] * SCALE).astype(dkv_halo_ref.dtype)
-        dkv_halo_ref[j, :, HEAD:] = dv[rows, :].astype(dkv_halo_ref.dtype)
-        dkv_own_ref[j, :, :HEAD] = dk[late, :] * SCALE
-        dkv_own_ref[j, :, HEAD:] = dv[late, :]
-
-
-def attend(chunk_index, doc_ids, band, queries_grads, own, halo):
-    blocks = own.shape[0]
-    total = WINDOW + blocks * BLOCK
+    lax.fori_loop(first_step, last_step, one_step, 0)
+
+
+def attend_near(order, counts, qd, own, own_t):
+    total = WINDOW + own_t.shape[1]
     smem = pl.BlockSpec(memory_space=pltpu.SMEM)
     vmem = pl.BlockSpec(memory_space=pltpu.VMEM)
     return pl.pallas_call(
-        attend_kernel,
-        in_specs=[smem] * 3 + [vmem] * 3,
-        out_specs=[vmem] * 3,
+        near_kernel,
+        in_specs=[smem] * 2 + [vmem] * 3,
+        out_specs=[vmem] * 2,
         out_shape=[
-            jax.ShapeDtypeStruct(
-                (blocks, BLOCK, queries_grads.shape[2] // 2), jnp.bfloat16
-            ),
-            jax.ShapeDtypeStruct(own.shape, jnp.float32),
-            jax.ShapeDtypeStruct(own.shape, jnp.bfloat16),
+            jax.ShapeDtypeStruct((*qd.shape[:2], qd.shape[2] // 2), qd.dtype),
+            jax.ShapeDtypeStruct((own_t.shape[1], 2 * HEAD), jnp.float32),
         ],
         scratch_shapes=[
-            pltpu.VMEM((total, HEAD), jnp.bfloat16),
-            pltpu.VMEM((HEAD, total), jnp.bfloat16),
-            pltpu.VMEM((total, HEAD), jnp.bfloat16),
-            pltpu.VMEM((total, HEAD), jnp.float32),
-            pltpu.VMEM((total, HEAD), jnp.float32),
-            pltpu.SMEM((blocks,), jnp.int32),
-            pltpu.SMEM((blocks,), jnp.int32),
-        ],
-        compiler_params=pltpu.CompilerParams(vmem_limit_bytes=40 * 1024 * 1024),
-    )(chunk_index, doc_ids, band, queries_grads, own, halo)
-
-
-def add_kernel(own_ref, spill_ref, out_ref, slabs, sems):
+            pltpu.VMEM((total, 2 * HEAD), own.dtype),
+            pltpu.VMEM((HEAD, total), own.dtype),
+            pltpu.VMEM((total, 2 * HEAD), jnp.float32),
+        ],
+        compiler_params=pltpu.CompilerParams(vmem_limit_bytes=LARGE),
+    )(order, counts, qd, own, own_t)
+
+
+def attend_far(order, counts, qd, own, own_t, halo, dq, sums, room):
+    total = WINDOW + own_t.shape[1]
+    smem = pl.BlockSpec(memory_space=pltpu.SMEM)
+    vmem = pl.BlockSpec(memory_space=pltpu.VMEM)
+    hbm = pl.BlockSpec(memory_space=pl.ANY)
+    return pl.pallas_call(
+        far_kernel,
+        in_specs=[smem] * 2 + [vmem] * 6 + [hbm],
+        out_specs=[hbm, vmem, hbm],
+        out_shape=[jax.ShapeDtypeStruct(x.shape, x.dtype) for x in (dq, sums, halo)],
+        input_output_aliases={8: 0},
+        scratch_shapes=[
+            pltpu.VMEM((total, 2 * HEAD), own.dtype),
+            pltpu.VMEM((HEAD, total), own.dtype),
+            pltpu.VMEM((total, 2 * HEAD), jnp.float32),
+            pltpu.VMEM(dq.shape, dq.dtype),
+            pltpu.VMEM(halo.shape, halo.dtype),
+            pltpu.SemaphoreType.DMA(dq.shape[:1]),
+            pltpu.SemaphoreType.DMA(halo.shape[:1]),
+        ],
+        compiler_params=pltpu.CompilerParams(vmem_limit_bytes=LARGE),
+    )(order, counts, qd, own, own_t, halo, dq, sums, room)
+
+
+def add_kernel(sums_ref, spill_ref, out_ref, slabs, sems):
     copies = []
     for j in range(out_ref.shape[0]):
-        slabs[j] = (own_ref[j] + spill_ref[j].astype(jnp.float32)).astype(slabs.dtype)
+        late = slice(j * BLOCK, (j + 1) * BLOCK)
+        for half, scale in ((slice(0, HEAD), SCALE), (slice(HEAD, 2 * HEAD), 1.0)):
+            own = sums_ref[late, half] * scale
+            slabs[j, :, half] = (own + spill_ref[j, :, half].astype(jnp.float32)).astype(
+                slabs.dtype
+            )
         copies.append(pltpu.make_async_copy(slabs.at[j], out_ref.at[j], sems.at[j]))
         copies[j].start()
     for copy in copies:
         copy.wait()
 
 
-def add_spill(own, spill):
+def add_spill(sums, spill):
     return pl.pallas_call(
         add_kernel,
         in_specs=[pl.BlockSpec(memory_space=pltpu.VMEM)] * 2,
@@ -279,7 +378,7 @@
             pltpu.SemaphoreType.DMA((spill.shape[0],)),
         ],
         compiler_params=pltpu.CompilerParams(vmem_limit_bytes=SMALL),
-    )(own, spill)
+    )(sums, spill)
 
 
 def per_device(queries, keys, values, upstream, doc_ids, band):
@@ -298,14 +397,17 @@
             value, axes, split_axis=0, concat_axis=0, axis_index_groups=groups, tiled=True
         )
 
-    kv = exchange(pack(keys, values, parts))
+    kv_packed = pack(keys, values, parts)
+    kv = exchange(kv_packed)
     halo = lax.ppermute(kv, "blk", [(s, s + step) for s in range(spans - step)])
     qd = exchange(pack(queries, upstream, parts))
     chunk_index = (lax.axis_index("blk") // step).astype(jnp.int32).reshape(1)
-    dq, dkv_own, dkv_halo = attend(chunk_index, doc_ids, band, qd, kv, halo)
-    spill = lax.ppermute(dkv_halo, "blk", [(s + step, s) for s in range(spans - step)])
+    order, counts, own_t = prepare(chunk_index, doc_ids, band, kv)
+    dq, sums = attend_near(order, counts, qd, kv, own_t)
+    dq, sums, spill = attend_far(order, counts, qd, kv, own_t, halo, dq, sums, kv_packed)
+    spill = lax.ppermute(spill, "blk", [(s + step, s) for s in range(spans - step)])
     query_out = exchange(dq)
-    dkv = exchange(add_spill(dkv_own, spill))
+    dkv = exchange(add_spill(sums, spill))
 
     return (*unpack(query_out, 1), *unpack(dkv, 2))
 

time: 77 us -> 75.5 us (0.981)
  waiting for transfers between devices: 41.7 us -> 36.7 us
  Pallas kernels: 12.2 us -> 14.1 us
  starting transfers between devices: 21 us -> 22 us
    ppermute x1, waiting for transfers between devices: 13.5 us -> 10.4 us  [per_device(): lax.ppermute(spill, 'blk', [(s + step, s) for s in range(spans - step)])]
    all_to_all x4, waiting for transfers between devices: 28.3 us -> 26.3 us  [exchange(): lax.all_to_all(value, axes, split_axis=0, concat_axis=0, axis_index_group...]
    pallas_call x1 -> x3, Pallas kernels: 5.6 us -> 7.46 us  [the longest x1 4.17 us: attend_near(): pl.pallas_call(near_kernel, in_specs=[smem] * 2 + [vmem] * 3, out_specs=[...]
    all_to_all x4, starting transfers between devices: 16.1 us -> 17.1 us  [exchange(): lax.all_to_all(value, axes, split_axis=0, concat_axis=0, axis_index_group...]
  transfers between devices with their start and end apart: 6 -> 6, of which waited for: 4 -> 4; matrix products, arithmetic and copies ran while one was open for 0% -> 0% of each run, Pallas kernels for 5% -> 13%
where the time goes in v4:
time: 75.5 us; the launch traced here: 74.3 us
  waiting for transfers between devices  36.7 us (49%)
  starting transfers between devices  22 us (29%)
  Pallas kernels  14.1 us (19%)
  between operations  0.93 us (1%)
    all_to_all x4, waiting for transfers between devices, exchange(): lax.all_to_all(value, axes, split_axis=0, concat_axis=0, axis_index_group...  26.3 us
    all_to_all x4, starting transfers between devices, exchange(): lax.all_to_all(value, axes, split_axis=0, concat_axis=0, axis_index_group...  17.1 us
    ppermute x1, waiting for transfers between devices, per_device(): lax.ppermute(spill, 'blk', [(s + step, s) for s in range(spans - step)])  10.4 us
    pallas_call x1, Pallas kernels, attend_near(): pl.pallas_call(near_kernel, in_specs=[smem] * 2 + [vmem] * 3, out_specs=[...  4.17 us
    pallas_call x2, Pallas kernels, pack(): pl.pallas_call(pack_kernel, in_specs=[hbm] * 2, out_specs=hbm, out_shape=...  3.98 us
    ppermute x1, starting transfers between devices, per_device(): halo = lax.ppermute(kv, 'blk', [(s, s + step) for s in range(spans - step)])  3.54 us
    pallas_call x1, Pallas kernels, attend_far(): pl.pallas_call(far_kernel, in_specs=[smem] * 2 + [vmem] * 6 + [hbm], out_...  1.98 us
    pallas_call x2, Pallas kernels, unpack(): pl.pallas_call(unpack_kernel, in_specs=[pl.BlockSpec(memory_space=pltpu.V...  1.76 us
  transfers between devices with their start and end apart: 6, of which 4 were waited for; matrix products, arithmetic and copies ran while one was open for 0% of the time, Pallas kernels for 13%

profile of v4, /device:TPU:0, one launch (start us, length us, event | category | flops | bytes accessed | tf_op | source)
XLA Modules:
  0.0 74.3 jit_solution(7091869136307692442)
XLA Ops:
  0.6 1.8 %shard_map.85.room_ref = bf16[8,128,256]{2,1,0:T(8,128)(2,1)} custom-call(bf16[128,1024]{1,0:T(8,128)(2,1)} %a_ref.2, bf16[128,1024]{1,0:T(8,128)(2,1)} %b_ref.2), custom_call_target="tpu_custom_call" | custom-call | tf_op jit(solution)/shard_map/pallas_call | solution.py:70
  2.5 5.2 %all-to-all-start = ((bf16[8,128,256]{2,1,0:T(8,128)(2,1)}), bf16[8,128,256]{2,1,0:T(8,128)(2,1)S(1)}, u32[]{:S(2)}, u32[]{:S(2)}) async-start(bf16[8,128,256]{2,1,0:T(8,128)(2,1)} %shard_map.85.room_ref), calls=%async_computation | async-start | bytes 1048576 | tf_op jit(solution)/shard_map/all_to_all | solution.py:396
  7.7 2.1 %shard_map.87 = bf16[8,128,512]{2,1,0:T(8,128)(2,1)} custom-call(bf16[128,2048]{1,0:T(8,128)(2,1)} %a_ref.3, bf16[128,2048]{1,0:T(8,128)(2,1)} %b_ref.3), custom_call_target="tpu_custom_call" | custom-call | tf_op jit(solution)/shard_map/pallas_call | solution.py:70
  9.8 7.6 %all-to-all-done.own_ref = bf16[8,128,256]{2,1,0:T(8,128)(2,1)S(1)} async-done(((bf16[8,128,256]{2,1,0:T(8,128)(2,1)}), bf16[8,128,256]{2,1,0:T(8,128)(2,1)S(1)}, u32[]{:S(2)}, u32[]{:S(2)}) %all-to-all-start) | async-done | bytes 524320 | tf_op jit(solution)/shard_map/all_to_all | solution.py:396
  17.4 3.6 %all-to-all-start.1 = ((bf16[8,128,512]{2,1,0:T(8,128)(2,1)}), bf16[8,128,512]{2,1,0:T(8,128)(2,1)S(1)}, u32[]{:S(2)}, u32[]{:S(2)}) async-start(bf16[8,128,512]{2,1,0:T(8,128)(2,1)} %shard_map.87), calls=%async_computation.1 | async-start | bytes 2097152 | tf_op jit(solution)/shard_map/all_to_all | solution.py:396
  21.0 3.5 %collective-permute-start = (bf16[8,128,256]{2,1,0:T(8,128)(2,1)S(1)}, bf16[8,128,256]{2,1,0:T(8,128)(2,1)S(1)}, u32[]{:S(2)}, u32[]{:S(2)}) collective-permute-start(bf16[8,128,256]{2,1,0:T(8,128)(2,1)S(1)} %all-to-all-done.own_ref), channel_id=1, source_target_pairs={{0,8},{2,10},{4,12},{6,14},{8,16},{10,18},{12,20},{14,22},{16,24},... | collective-permute-start | bytes 1572872 | tf_op jit(solution)/shard_map/ppermute | solution.py:402
  24.5 0.0 copy-start
  24.6 0.0 copy-start.1
  24.6 0.6 copy-done
  25.2 0.0 copy-done.1
  25.2 1.3 %shard_map.86 = (s32[8]{0:T(128)S(1)}, s32[10]{0:T(128)S(1)}, bf16[128,1024]{1,0:T(8,128)(2,1)S(1)}) custom-call(s32[1]{0:T(128)} %bitcast.chunk_ref, s32[32]{0:T(128)S(1)} %copy-done, s32[32]{0:T(128)S(1)} %copy-done.1, bf16[8,128,256]{2,1,0:T(8,128)(2,1)S(1)} %all-to-all-done.own_ref), custom_call_target="tpu_custom_call" | custom-call | tf_op jit(solution)/shard_map/pallas_call | solution.py:145
  26.5 9.8 %all-to-all-done.1.qd_ref = bf16[8,128,512]{2,1,0:T(8,128)(2,1)S(1)} async-done(((bf16[8,128,512]{2,1,0:T(8,128)(2,1)}), bf16[8,128,512]{2,1,0:T(8,128)(2,1)S(1)}, u32[]{:S(2)}, u32[]{:S(2)}) %all-to-all-start.1) | async-done | bytes 1048608 | tf_op jit(solution)/shard_map/all_to_all | solution.py:396
  36.3 4.2 %shard_map.88 = (bf16[8,128,256]{2,1,0:T(8,128)(2,1)S(1)}, f32[1024,256]{1,0:T(8,128)S(1)}) custom-call(s32[8]{0:T(128)S(1)} %get-tuple-element.13.order, s32[10]{0:T(128)S(1)} %get-tuple-element.14.counts, bf16[8,128,512]{2,1,0:T(8,128)(2,1)S(1)} %all-to-all-done.1.qd_ref, bf16[8,128,256]{2,1,0:T(8,128)(2,1)S(1)} %all-to-all-done.own_ref, ...), custom_call_target="tpu_custom_call" | custom-call | tf_op jit(solution)/shard_map/pallas_call | solution.py:314
  40.5 0.0 collective-permute-done.halo_ref
  40.5 2.0 %shard_map.89 = (bf16[8,128,256]{2,1,0:T(8,128)(2,1)}, f32[1024,256]{1,0:T(8,128)S(1)}, bf16[8,128,256]{2,1,0:T(8,128)(2,1)}) custom-call(s32[8]{0:T(128)S(1)} %get-tuple-element.13.order, s32[10]{0:T(128)S(1)} %get-tuple-element.14.counts, bf16[8,128,512]{2,1,0:T(8,128)(2,1)S(1)} %all-to-all-done.1.qd_ref, ...), custom_call_target="tpu_custom_call", output_to_operand_aliasing={{0}: (8, {})} | custom-call | tf_op jit(solution)/shard_map/pallas_call | solution.py:336
  42.5 1.3 %collective-permute-start.1 = (bf16[8,128,256]{2,1,0:T(8,128)(2,1)}, bf16[8,128,256]{2,1,0:T(8,128)(2,1)S(1)}, u32[]{:S(2)}, u32[]{:S(2)}) collective-permute-start(bf16[8,128,256]{2,1,0:T(8,128)(2,1)} %get-tuple-element.20), channel_id=1, source_target_pairs={{8,0},{10,2},{12,4},{14,6},{16,8},{18,10},{20,12},{22,14},{24,16},... | collective-permute-start | bytes 1572872 | tf_op jit(solution)/shard_map/ppermute | solution.py:408
  43.8 3.5 %all-to-all-start.2 = ((bf16[8,128,256]{2,1,0:T(8,128)(2,1)}), bf16[8,128,256]{2,1,0:T(8,128)(2,1)S(1)}, u32[]{:S(2)}, u32[]{:S(2)}) async-start(bf16[8,128,256]{2,1,0:T(8,128)(2,1)} %get-tuple-element.18), calls=%async_computation.2 | async-start | bytes 1048576 | tf_op jit(solution)/shard_map/all_to_all | solution.py:396
  47.3 10.4 %collective-permute-done.1.spill_ref = bf16[8,128,256]{2,1,0:T(8,128)(2,1)S(1)} collective-permute-done((bf16[8,128,256]{2,1,0:T(8,128)(2,1)}, bf16[8,128,256]{2,1,0:T(8,128)(2,1)S(1)}, u32[]{:S(2)}, u32[]{:S(2)}) %collective-permute-start.1) | collective-permute-done | bytes 524320 | tf_op jit(solution)/shard_map/ppermute | solution.py:408
  57.7 0.9 %shard_map.91 = bf16[8,128,256]{2,1,0:T(8,128)(2,1)} custom-call(f32[1024,256]{1,0:T(8,128)S(1)} %get-tuple-element.19.sums_ref, bf16[8,128,256]{2,1,0:T(8,128)(2,1)S(1)} %collective-permute-done.1.spill_ref), custom_call_target="tpu_custom_call" | custom-call | tf_op jit(solution)/shard_map/pallas_call | solution.py:371
  58.6 0.0 all-to-all-done.2.in_ref
  58.6 4.9 %all-to-all-start.3 = ((bf16[8,128,256]{2,1,0:T(8,128)(2,1)}), bf16[8,128,256]{2,1,0:T(8,128)(2,1)S(1)}, u32[]{:S(2)}, u32[]{:S(2)}) async-start(bf16[8,128,256]{2,1,0:T(8,128)(2,1)} %shard_map.91), calls=%async_computation.3 | async-start | bytes 1048576 | tf_op jit(solution)/shard_map/all_to_all | solution.py:396
  63.5 0.8 %shard_map.90 = bf16[128,2048]{1,0:T(8,128)(2,1)} custom-call(bf16[8,128,256]{2,1,0:T(8,128)(2,1)S(1)} %all-to-all-done.2.in_ref), custom_call_target="tpu_custom_call" | custom-call | tf_op jit(solution)/shard_map/pallas_call | solution.py:99
  64.3 8.9 %all-to-all-done.3.in_ref = bf16[8,128,256]{2,1,0:T(8,128)(2,1)S(1)} async-done(((bf16[8,128,256]{2,1,0:T(8,128)(2,1)}), bf16[8,128,256]{2,1,0:T(8,128)(2,1)S(1)}, u32[]{:S(2)}, u32[]{:S(2)}) %all-to-all-start.3) | async-done | bytes 524320 | tf_op jit(solution)/shard_map/all_to_all | solution.py:396
  73.2 0.9 %shard_map.92 = (bf16[128,1024]{1,0:T(8,128)(2,1)}, bf16[128,1024]{1,0:T(8,128)(2,1)}) custom-call(bf16[8,128,256]{2,1,0:T(8,128)(2,1)S(1)} %all-to-all-done.3.in_ref), custom_call_target="tpu_custom_call" | custom-call | tf_op jit(solution)/shard_map/pallas_call | solution.py:99
Async XLA Ops:
  2.5 14.9 %all-to-all-start = ((bf16[8,128,256]{2,1,0:T(8,128)(2,1)}), bf16[8,128,256]{2,1,0:T(8,128)(2,1)S(1)}, u32[]{:S(2)}, u32[]{:S(2)}) async-start(bf16[8,128,256]{2,1,0:T(8,128)(2,1)} %shard_map.85.room_ref), calls=%async_computation | async-start | bytes 1048576 | tf_op jit(solution)/shard_map/all_to_all | solution.py:396
  17.4 18.9 %all-to-all-start.1 = ((bf16[8,128,512]{2,1,0:T(8,128)(2,1)}), bf16[8,128,512]{2,1,0:T(8,128)(2,1)S(1)}, u32[]{:S(2)}, u32[]{:S(2)}) async-start(bf16[8,128,512]{2,1,0:T(8,128)(2,1)} %shard_map.87), calls=%async_computation.1 | async-start | bytes 2097152 | tf_op jit(solution)/shard_map/all_to_all | solution.py:396
  21.0 19.5 %collective-permute-start = (bf16[8,128,256]{2,1,0:T(8,128)(2,1)S(1)}, bf16[8,128,256]{2,1,0:T(8,128)(2,1)S(1)}, u32[]{:S(2)}, u32[]{:S(2)}) collective-permute-start(bf16[8,128,256]{2,1,0:T(8,128)(2,1)S(1)} %all-to-all-done.own_ref), channel_id=1, source_target_pairs={{0,8},{2,10},{4,12},{6,14},{8,16},{10,18},{12,20},{14,22},{16,24},... | collective-permute-start | bytes 1572872 | tf_op jit(solution)/shard_map/ppermute | solution.py:402
  24.5 0.7 copy-start
  24.6 0.7 copy-start.1
  42.5 15.2 %collective-permute-start.1 = (bf16[8,128,256]{2,1,0:T(8,128)(2,1)}, bf16[8,128,256]{2,1,0:T(8,128)(2,1)S(1)}, u32[]{:S(2)}, u32[]{:S(2)}) collective-permute-start(bf16[8,128,256]{2,1,0:T(8,128)(2,1)} %get-tuple-element.20), channel_id=1, source_target_pairs={{8,0},{10,2},{12,4},{14,6},{16,8},{18,10},{20,12},{22,14},{24,16},... | collective-permute-start | bytes 1572872 | tf_op jit(solution)/shard_map/ppermute | solution.py:408
  43.8 14.8 %all-to-all-start.2 = ((bf16[8,128,256]{2,1,0:T(8,128)(2,1)}), bf16[8,128,256]{2,1,0:T(8,128)(2,1)S(1)}, u32[]{:S(2)}, u32[]{:S(2)}) async-start(bf16[8,128,256]{2,1,0:T(8,128)(2,1)} %get-tuple-element.18), calls=%async_computation.2 | async-start | bytes 1048576 | tf_op jit(solution)/shard_map/all_to_all | solution.py:396
  58.6 14.6 %all-to-all-start.3 = ((bf16[8,128,256]{2,1,0:T(8,128)(2,1)}), bf16[8,128,256]{2,1,0:T(8,128)(2,1)S(1)}, u32[]{:S(2)}, u32[]{:S(2)}) async-start(bf16[8,128,256]{2,1,0:T(8,128)(2,1)} %shard_map.91), calls=%async_computation.3 | async-start | bytes 1048576 | tf_op jit(solution)/shard_map/all_to_all | solution.py:396

commit v5 on v4

--- a/solution.py
+++ b/solution.py
@@ -162,23 +162,22 @@
         keys_t[:, late] = own_t_ref[:, j * BLOCK : (j + 1) * BLOCK]
 
 
-def near_kernel(order, counts, qd_ref, own_ref, own_t_ref, dq_ref, sums_ref, kv, keys_t, sums):
+def near_kernel(order, counts, qd_ref, own_ref, own_t_ref, dq_ref, sums, kv, keys_t):
     kv[:WINDOW, :] = jnp.zeros((WINDOW, 2 * HEAD), kv.dtype)
     keys_t[:, :WINDOW] = jnp.zeros((HEAD, WINDOW), keys_t.dtype)
     place_own(own_ref, own_t_ref, kv, keys_t)
     sums[...] = jnp.zeros_like(sums)
     last = counts[order.shape[0]]
     attend(0, last, order, counts, qd_ref, kv, keys_t, dq_ref, sums, lambda i: None)
-    sums_ref[...] = sums[WINDOW:, :]
 
 
 def far_kernel(
     order, counts, qd_ref, own_ref, own_t_ref, halo_ref, dq_near_ref, sums_near_ref, room_ref,
-    dq_ref, sums_ref, spill_ref, kv, keys_t, sums, dq_slabs, spill_slabs, dq_sems, spill_sems,
+    dq_ref, sums_ref, spill_ref, kv, keys_t, sums, dq_slabs, dq_sems,
 ):
     del room_ref
     sums[:WINDOW, :] = jnp.zeros((WINDOW, 2 * HEAD), sums.dtype)
-    sums[WINDOW:, :] = sums_near_ref[...]
+    sums[WINDOW:, :] = sums_near_ref[WINDOW:, :]
     blocks = order.shape[0]
     steps = counts[blocks]
 
@@ -209,20 +208,13 @@
         steps, blocks // TOGETHER, order, counts, qd_ref, kv, keys_t, dq_slabs, sums,
         lambda i: dq_copy(dq_slabs, i).start(),
     )
-    copies = []
     for j in range(WB):
         rows = slice(j * BLOCK, (j + 1) * BLOCK)
-        spill_slabs[j, :, :HEAD] = (sums[rows, :HEAD] * SCALE).astype(spill_slabs.dtype)
-        spill_slabs[j, :, HEAD:] = sums[rows, HEAD:].astype(spill_slabs.dtype)
-        copies.append(
-            pltpu.make_async_copy(spill_slabs.at[j], spill_ref.at[j], spill_sems.at[j])
-        )
-        copies[j].start()
+        spill_ref[j, :, :HEAD] = (sums[rows, :HEAD] * SCALE).astype(spill_ref.dtype)
+        spill_ref[j, :, HEAD:] = sums[rows, HEAD:].astype(spill_ref.dtype)
     sums_ref[...] = sums[WINDOW:, :]
     for i in range(blocks):
         dq_copy(dq_slabs, i).wait()
-    for copy in copies:
-        copy.wait()
 
 
 def attend(first_step, last_step, order, counts, qd_ref, kv, keys_t, dq_slabs, sums, ready):
@@ -317,12 +309,11 @@
         out_specs=[vmem] * 2,
         out_shape=[
             jax.ShapeDtypeStruct((*qd.shape[:2], qd.shape[2] // 2), qd.dtype),
-            jax.ShapeDtypeStruct((own_t.shape[1], 2 * HEAD), jnp.float32),
+            jax.ShapeDtypeStruct((total, 2 * HEAD), jnp.float32),
         ],
         scratch_shapes=[
             pltpu.VMEM((total, 2 * HEAD), own.dtype),
             pltpu.VMEM((HEAD, total), own.dtype),
-            pltpu.VMEM((total, 2 * HEAD), jnp.float32),
         ],
         compiler_params=pltpu.CompilerParams(vmem_limit_bytes=LARGE),
     )(order, counts, qd, own, own_t)
@@ -336,17 +327,19 @@
     return pl.pallas_call(
         far_kernel,
         in_specs=[smem] * 2 + [vmem] * 6 + [hbm],
-        out_specs=[hbm, vmem, hbm],
-        out_shape=[jax.ShapeDtypeStruct(x.shape, x.dtype) for x in (dq, sums, halo)],
-        input_output_aliases={8: 0},
+        out_specs=[hbm, vmem, vmem],
+        out_shape=[
+            jax.ShapeDtypeStruct(dq.shape, dq.dtype),
+            jax.ShapeDtypeStruct((own_t.shape[1], 2 * HEAD), sums.dtype),
+            jax.ShapeDtypeStruct(halo.shape, halo.dtype),
+        ],
+        input_output_aliases={8: 0, 5: 2},
         scratch_shapes=[
             pltpu.VMEM((total, 2 * HEAD), own.dtype),
             pltpu.VMEM((HEAD, total), own.dtype),
-            pltpu.VMEM((total, 2 * HEAD), jnp.float32),
+            pltpu.VMEM(sums.shape, sums.dtype),
             pltpu.VMEM(dq.shape, dq.dtype),
-            pltpu.VMEM(halo.shape, halo.dtype),
             pltpu.SemaphoreType.DMA(dq.shape[:1]),
-            pltpu.SemaphoreType.DMA(halo.shape[:1]),
         ],
         compiler_params=pltpu.CompilerParams(vmem_limit_bytes=LARGE),
     )(order, counts, qd, own, own_t, halo, dq, sums, room)

time: 75.5 us -> 75.1 us (level)
  the two profiles are of different devices: /device:TPU:0 before, /device:TPU:16 now
where the time goes in v5:
time: 75.1 us; the launch traced here: 75.2 us
  waiting for transfers between devices  38.2 us (51%)
  starting transfers between devices  21.4 us (28%)
  Pallas kernels  14.6 us (19%)
  between operations  0.94 us (1%)
    all_to_all x4, waiting for transfers between devices, exchange(): lax.all_to_all(value, axes, split_axis=0, concat_axis=0, axis_index_group...  26.9 us
    all_to_all x4, starting transfers between devices, exchange(): lax.all_to_all(value, axes, split_axis=0, concat_axis=0, axis_index_group...  14.4 us
    ppermute x1, waiting for transfers between devices, per_device(): lax.ppermute(spill, 'blk', [(s + step, s) for s in range(spans - step)])  11.3 us
    pallas_call x1, Pallas kernels, attend_near(): pl.pallas_call(near_kernel, in_specs=[smem] * 2 + [vmem] * 3, out_specs=[...  5.15 us
    pallas_call x2, Pallas kernels, pack(): pl.pallas_call(pack_kernel, in_specs=[hbm] * 2, out_specs=hbm, out_shape=...  4 us
    ppermute x1, starting transfers between devices, per_device(): halo = lax.ppermute(kv, 'blk', [(s, s + step) for s in range(spans - step)])  3.52 us
    ppermute x1, starting transfers between devices, per_device(): lax.ppermute(spill, 'blk', [(s + step, s) for s in range(spans - step)])  3.44 us
    pallas_call x2, Pallas kernels, unpack(): pl.pallas_call(unpack_kernel, in_specs=[pl.BlockSpec(memory_space=pltpu.V...  1.76 us
  transfers between devices with their start and end apart: 6, of which 4 were waited for; matrix products, arithmetic and copies ran while one was open for 0% of the time, Pallas kernels for 14%

profile of v5, /device:TPU:16, one launch (start us, length us, event | category | flops | bytes accessed | tf_op | source)
XLA Modules:
  0.0 75.2 jit_solution(17499484219785418994)
XLA Ops:
  0.6 1.8 %shard_map.85.room_ref = bf16[8,128,256]{2,1,0:T(8,128)(2,1)} custom-call(bf16[128,1024]{1,0:T(8,128)(2,1)} %a_ref.2, bf16[128,1024]{1,0:T(8,128)(2,1)} %b_ref.2), custom_call_target="tpu_custom_call" | custom-call | tf_op jit(solution)/shard_map/pallas_call | solution.py:70
  2.5 3.7 %all-to-all-start = ((bf16[8,128,256]{2,1,0:T(8,128)(2,1)}), bf16[8,128,256]{2,1,0:T(8,128)(2,1)S(1)}, u32[]{:S(2)}, u32[]{:S(2)}) async-start(bf16[8,128,256]{2,1,0:T(8,128)(2,1)} %shard_map.85.room_ref), calls=%async_computation | async-start | bytes 1048576 | tf_op jit(solution)/shard_map/all_to_all | solution.py:389
  6.2 0.0 copy-start
  6.2 0.0 copy-start.1
  6.2 2.1 %shard_map.87 = bf16[8,128,512]{2,1,0:T(8,128)(2,1)} custom-call(bf16[128,2048]{1,0:T(8,128)(2,1)} %a_ref.3, bf16[128,2048]{1,0:T(8,128)(2,1)} %b_ref.3), custom_call_target="tpu_custom_call" | custom-call | tf_op jit(solution)/shard_map/pallas_call | solution.py:70
  8.4 7.6 %all-to-all-done.own_ref = bf16[8,128,256]{2,1,0:T(8,128)(2,1)S(1)} async-done(((bf16[8,128,256]{2,1,0:T(8,128)(2,1)}), bf16[8,128,256]{2,1,0:T(8,128)(2,1)S(1)}, u32[]{:S(2)}, u32[]{:S(2)}) %all-to-all-start) | async-done | bytes 524320 | tf_op jit(solution)/shard_map/all_to_all | solution.py:389
  16.0 3.6 %all-to-all-start.1 = ((bf16[8,128,512]{2,1,0:T(8,128)(2,1)}), bf16[8,128,512]{2,1,0:T(8,128)(2,1)S(1)}, u32[]{:S(2)}, u32[]{:S(2)}) async-start(bf16[8,128,512]{2,1,0:T(8,128)(2,1)} %shard_map.87), calls=%async_computation.1 | async-start | bytes 2097152 | tf_op jit(solution)/shard_map/all_to_all | solution.py:389
  19.5 3.5 %collective-permute-start = (bf16[8,128,256]{2,1,0:T(8,128)(2,1)S(1)}, bf16[8,128,256]{2,1,0:T(8,128)(2,1)S(1)}, u32[]{:S(2)}, u32[]{:S(2)}) collective-permute-start(bf16[8,128,256]{2,1,0:T(8,128)(2,1)S(1)} %all-to-all-done.own_ref), channel_id=1, source_target_pairs={{0,8},{2,10},{4,12},{6,14},{8,16},{10,18},{12,20},{14,22},{16,24},... | collective-permute-start | bytes 1572872 | tf_op jit(solution)/shard_map/ppermute | solution.py:395
  23.1 0.0 copy-done
  23.1 0.0 copy-done.1
  23.1 1.3 %shard_map.86 = (s32[8]{0:T(128)S(1)}, s32[10]{0:T(128)S(1)}, bf16[128,1024]{1,0:T(8,128)(2,1)S(1)}) custom-call(s32[1]{0:T(128)} %bitcast.chunk_ref, s32[32]{0:T(128)S(1)} %copy-done, s32[32]{0:T(128)S(1)} %copy-done.1, bf16[8,128,256]{2,1,0:T(8,128)(2,1)S(1)} %all-to-all-done.own_ref), custom_call_target="tpu_custom_call" | custom-call | tf_op jit(solution)/shard_map/pallas_call | solution.py:145
  24.4 10.5 %all-to-all-done.1.qd_ref = bf16[8,128,512]{2,1,0:T(8,128)(2,1)S(1)} async-done(((bf16[8,128,512]{2,1,0:T(8,128)(2,1)}), bf16[8,128,512]{2,1,0:T(8,128)(2,1)S(1)}, u32[]{:S(2)}, u32[]{:S(2)}) %all-to-all-start.1) | async-done | bytes 1048608 | tf_op jit(solution)/shard_map/all_to_all | solution.py:389
  34.9 5.2 %shard_map.88 = (bf16[8,128,256]{2,1,0:T(8,128)(2,1)S(1)}, f32[2048,256]{1,0:T(8,128)S(1)}) custom-call(s32[8]{0:T(128)S(1)} %get-tuple-element.13.order, s32[10]{0:T(128)S(1)} %get-tuple-element.14.counts, bf16[8,128,512]{2,1,0:T(8,128)(2,1)S(1)} %all-to-all-done.1.qd_ref, bf16[8,128,256]{2,1,0:T(8,128)(2,1)S(1)} %all-to-all-done.own_ref, ...), custom_call_target="tpu_custom_call" | custom-call | tf_op jit(solution)/shard_map/pallas_call | solution.py:306
  40.0 0.0 collective-permute-done.halo_ref
  40.0 1.5 %shard_map.89 = (bf16[8,128,256]{2,1,0:T(8,128)(2,1)}, f32[1024,256]{1,0:T(8,128)S(1)}, bf16[8,128,256]{2,1,0:T(8,128)(2,1)S(1)}) custom-call(s32[8]{0:T(128)S(1)} %get-tuple-element.13.order, s32[10]{0:T(128)S(1)} %get-tuple-element.14.counts, bf16[8,128,512]{2,1,0:T(8,128)(2,1)S(1)} %all-to-all-done.1.qd_ref, ...), custom_call_target="tpu_custom_call", output_to_operand_aliasing={{0}: (8, {}), {2}: (5, {})} | custom-call | tf_op jit(solution)/shard_map/pallas_call | solution.py:327
  41.6 3.4 %collective-permute-start.1 = (bf16[8,128,256]{2,1,0:T(8,128)(2,1)S(1)}, bf16[8,128,256]{2,1,0:T(8,128)(2,1)S(1)}, u32[]{:S(2)}, u32[]{:S(2)}) collective-permute-start(bf16[8,128,256]{2,1,0:T(8,128)(2,1)S(1)} %get-tuple-element.20), channel_id=1, source_target_pairs={{8,0},{10,2},{12,4},{14,6},{16,8},{18,10},{20,12},{22,14},{24,16},... | collective-permute-start | bytes 1572872 | tf_op jit(solution)/shard_map/ppermute | solution.py:401
  45.0 3.5 %all-to-all-start.2 = ((bf16[8,128,256]{2,1,0:T(8,128)(2,1)}), bf16[8,128,256]{2,1,0:T(8,128)(2,1)S(1)}, u32[]{:S(2)}, u32[]{:S(2)}) async-start(bf16[8,128,256]{2,1,0:T(8,128)(2,1)} %get-tuple-element.18), calls=%async_computation.2 | async-start | bytes 1048576 | tf_op jit(solution)/shard_map/all_to_all | solution.py:389
  48.6 11.3 %collective-permute-done.1.spill_ref = bf16[8,128,256]{2,1,0:T(8,128)(2,1)S(1)} collective-permute-done((bf16[8,128,256]{2,1,0:T(8,128)(2,1)S(1)}, bf16[8,128,256]{2,1,0:T(8,128)(2,1)S(1)}, u32[]{:S(2)}, u32[]{:S(2)}) %collective-permute-start.1) | collective-permute-done | bytes 524320 | tf_op jit(solution)/shard_map/ppermute | solution.py:401
  59.8 0.9 %shard_map.91 = bf16[8,128,256]{2,1,0:T(8,128)(2,1)} custom-call(f32[1024,256]{1,0:T(8,128)S(1)} %get-tuple-element.19.sums_ref, bf16[8,128,256]{2,1,0:T(8,128)(2,1)S(1)} %collective-permute-done.1.spill_ref), custom_call_target="tpu_custom_call" | custom-call | tf_op jit(solution)/shard_map/pallas_call | solution.py:364
  60.7 0.0 all-to-all-done.2.in_ref
  60.7 3.6 %all-to-all-start.3 = ((bf16[8,128,256]{2,1,0:T(8,128)(2,1)}), bf16[8,128,256]{2,1,0:T(8,128)(2,1)S(1)}, u32[]{:S(2)}, u32[]{:S(2)}) async-start(bf16[8,128,256]{2,1,0:T(8,128)(2,1)} %shard_map.91), calls=%async_computation.3 | async-start | bytes 1048576 | tf_op jit(solution)/shard_map/all_to_all | solution.py:389
  64.4 0.8 %shard_map.90 = bf16[128,2048]{1,0:T(8,128)(2,1)} custom-call(bf16[8,128,256]{2,1,0:T(8,128)(2,1)S(1)} %all-to-all-done.2.in_ref), custom_call_target="tpu_custom_call" | custom-call | tf_op jit(solution)/shard_map/pallas_call | solution.py:99
  65.2 8.9 %all-to-all-done.3.in_ref = bf16[8,128,256]{2,1,0:T(8,128)(2,1)S(1)} async-done(((bf16[8,128,256]{2,1,0:T(8,128)(2,1)}), bf16[8,128,256]{2,1,0:T(8,128)(2,1)S(1)}, u32[]{:S(2)}, u32[]{:S(2)}) %all-to-all-start.3) | async-done | bytes 524320 | tf_op jit(solution)/shard_map/all_to_all | solution.py:389
  74.1 0.9 %shard_map.92 = (bf16[128,1024]{1,0:T(8,128)(2,1)}, bf16[128,1024]{1,0:T(8,128)(2,1)}) custom-call(bf16[8,128,256]{2,1,0:T(8,128)(2,1)S(1)} %all-to-all-done.3.in_ref), custom_call_target="tpu_custom_call" | custom-call | tf_op jit(solution)/shard_map/pallas_call | solution.py:99
Async XLA Ops:
  2.5 13.5 %all-to-all-start = ((bf16[8,128,256]{2,1,0:T(8,128)(2,1)}), bf16[8,128,256]{2,1,0:T(8,128)(2,1)S(1)}, u32[]{:S(2)}, u32[]{:S(2)}) async-start(bf16[8,128,256]{2,1,0:T(8,128)(2,1)} %shard_map.85.room_ref), calls=%async_computation | async-start | bytes 1048576 | tf_op jit(solution)/shard_map/all_to_all | solution.py:389
  6.2 16.9 %copy-start = (s32[32]{0:T(128)S(1)}, s32[32]{0:T(128)}, u32[]{:S(2)}) copy-start(s32[32]{0:T(128)} %doc_ref.1) | copy-start | bytes 388
  6.2 16.9 %copy-start.1 = (s32[32]{0:T(128)S(1)}, s32[32]{0:T(128)}, u32[]{:S(2)}) copy-start(s32[32]{0:T(128)} %band_ref.1) | copy-start | bytes 388
  16.0 18.9 %all-to-all-start.1 = ((bf16[8,128,512]{2,1,0:T(8,128)(2,1)}), bf16[8,128,512]{2,1,0:T(8,128)(2,1)S(1)}, u32[]{:S(2)}, u32[]{:S(2)}) async-start(bf16[8,128,512]{2,1,0:T(8,128)(2,1)} %shard_map.87), calls=%async_computation.1 | async-start | bytes 2097152 | tf_op jit(solution)/shard_map/all_to_all | solution.py:389
  19.5 20.5 %collective-permute-start = (bf16[8,128,256]{2,1,0:T(8,128)(2,1)S(1)}, bf16[8,128,256]{2,1,0:T(8,128)(2,1)S(1)}, u32[]{:S(2)}, u32[]{:S(2)}) collective-permute-start(bf16[8,128,256]{2,1,0:T(8,128)(2,1)S(1)} %all-to-all-done.own_ref), channel_id=1, source_target_pairs={{0,8},{2,10},{4,12},{6,14},{8,16},{10,18},{12,20},{14,22},{16,24},... | collective-permute-start | bytes 1572872 | tf_op jit(solution)/shard_map/ppermute | solution.py:395
  41.6 18.3 %collective-permute-start.1 = (bf16[8,128,256]{2,1,0:T(8,128)(2,1)S(1)}, bf16[8,128,256]{2,1,0:T(8,128)(2,1)S(1)}, u32[]{:S(2)}, u32[]{:S(2)}) collective-permute-start(bf16[8,128,256]{2,1,0:T(8,128)(2,1)S(1)} %get-tuple-element.20), channel_id=1, source_target_pairs={{8,0},{10,2},{12,4},{14,6},{16,8},{18,10},{20,12},{22,14},{24,16},... | collective-permute-start | bytes 1572872 | tf_op jit(solution)/shard_map/ppermute | solution.py:401
  45.0 15.7 %all-to-all-start.2 = ((bf16[8,128,256]{2,1,0:T(8,128)(2,1)}), bf16[8,128,256]{2,1,0:T(8,128)(2,1)S(1)}, u32[]{:S(2)}, u32[]{:S(2)}) async-start(bf16[8,128,256]{2,1,0:T(8,128)(2,1)} %get-tuple-element.18), calls=%async_computation.2 | async-start | bytes 1048576 | tf_op jit(solution)/shard_map/all_to_all | solution.py:389
  60.7 13.4 %all-to-all-start.3 = ((bf16[8,128,256]{2,1,0:T(8,128)(2,1)}), bf16[8,128,256]{2,1,0:T(8,128)(2,1)S(1)}, u32[]{:S(2)}, u32[]{:S(2)}) async-start(bf16[8,128,256]{2,1,0:T(8,128)(2,1)} %shard_map.91), calls=%async_computation.3 | async-start | bytes 1048576 | tf_op jit(solution)/shard_map/all_to_all | solution.py:389

commit v6 on v5

--- a/solution.py
+++ b/solution.py
@@ -172,12 +172,10 @@
 
 
 def far_kernel(
-    order, counts, qd_ref, own_ref, own_t_ref, halo_ref, dq_near_ref, sums_near_ref, room_ref,
+    order, counts, qd_ref, halo_ref, dq_near_ref, room_ref, kv_in, keys_t_in, sums_in,
     dq_ref, sums_ref, spill_ref, kv, keys_t, sums, dq_slabs, dq_sems,
 ):
-    del room_ref
-    sums[:WINDOW, :] = jnp.zeros((WINDOW, 2 * HEAD), sums.dtype)
-    sums[WINDOW:, :] = sums_near_ref[WINDOW:, :]
+    del room_ref, kv_in, keys_t_in, sums_in
     blocks = order.shape[0]
     steps = counts[blocks]
 
@@ -194,16 +192,8 @@
         keys_t[:, rows] = halo_ref[j, :, :HEAD].T
         return carry
 
-    def blank(j, carry):
-        rows = pl.ds(pl.multiple_of(j * BLOCK, BLOCK), BLOCK)
-        kv[rows, :] = jnp.zeros((BLOCK, 2 * HEAD), kv.dtype)
-        keys_t[:, rows] = jnp.zeros((HEAD, BLOCK), keys_t.dtype)
-        return carry
-
     lax.fori_loop(0, steps * TOGETHER, pass_on, 0)
-    lax.fori_loop(0, counts[blocks + 1], blank, 0)
     lax.fori_loop(counts[blocks + 1], WB, fill, 0)
-    place_own(own_ref, own_t_ref, kv, keys_t)
     attend(
         steps, blocks // TOGETHER, order, counts, qd_ref, kv, keys_t, dq_slabs, sums,
         lambda i: dq_copy(dq_slabs, i).start(),
@@ -306,43 +296,35 @@
     return pl.pallas_call(
         near_kernel,
         in_specs=[smem] * 2 + [vmem] * 3,
-        out_specs=[vmem] * 2,
+        out_specs=[vmem] * 4,
         out_shape=[
             jax.ShapeDtypeStruct((*qd.shape[:2], qd.shape[2] // 2), qd.dtype),
             jax.ShapeDtypeStruct((total, 2 * HEAD), jnp.float32),
-        ],
-        scratch_shapes=[
-            pltpu.VMEM((total, 2 * HEAD), own.dtype),
-            pltpu.VMEM((HEAD, total), own.dtype),
+            jax.ShapeDtypeStruct((total, 2 * HEAD), own.dtype),
+            jax.ShapeDtypeStruct((HEAD, total), own.dtype),
         ],
         compiler_params=pltpu.CompilerParams(vmem_limit_bytes=LARGE),
     )(order, counts, qd, own, own_t)
 
 
-def attend_far(order, counts, qd, own, own_t, halo, dq, sums, room):
-    total = WINDOW + own_t.shape[1]
+def attend_far(order, counts, qd, halo, dq, room, kv, keys_t, sums):
     smem = pl.BlockSpec(memory_space=pltpu.SMEM)
     vmem = pl.BlockSpec(memory_space=pltpu.VMEM)
     hbm = pl.BlockSpec(memory_space=pl.ANY)
+    own_sums = jax.ShapeDtypeStruct((sums.shape[0] - WINDOW, sums.shape[1]), sums.dtype)
+    shapes = [jax.ShapeDtypeStruct(x.shape, x.dtype) for x in (dq, halo, kv, keys_t, sums)]
     return pl.pallas_call(
         far_kernel,
-        in_specs=[smem] * 2 + [vmem] * 6 + [hbm],
-        out_specs=[hbm, vmem, vmem],
-        out_shape=[
-            jax.ShapeDtypeStruct(dq.shape, dq.dtype),
-            jax.ShapeDtypeStruct((own_t.shape[1], 2 * HEAD), sums.dtype),
-            jax.ShapeDtypeStruct(halo.shape, halo.dtype),
-        ],
-        input_output_aliases={8: 0, 5: 2},
+        in_specs=[smem] * 2 + [vmem] * 3 + [hbm] + [vmem] * 3,
+        out_specs=[hbm] + [vmem] * 5,
+        out_shape=[shapes[0], own_sums, *shapes[1:]],
+        input_output_aliases={5: 0, 3: 2, 6: 3, 7: 4, 8: 5},
         scratch_shapes=[
-            pltpu.VMEM((total, 2 * HEAD), own.dtype),
-            pltpu.VMEM((HEAD, total), own.dtype),
-            pltpu.VMEM(sums.shape, sums.dtype),
             pltpu.VMEM(dq.shape, dq.dtype),
             pltpu.SemaphoreType.DMA(dq.shape[:1]),
         ],
         compiler_params=pltpu.CompilerParams(vmem_limit_bytes=LARGE),
-    )(order, counts, qd, own, own_t, halo, dq, sums, room)
+    )(order, counts, qd, halo, dq, room, kv, keys_t, sums)[:3]
 
 
 def add_kernel(sums_ref, spill_ref, out_ref, slabs, sems):
@@ -396,8 +378,8 @@
     qd = exchange(pack(queries, upstream, parts))
     chunk_index = (lax.axis_index("blk") // step).astype(jnp.int32).reshape(1)
     order, counts, own_t = prepare(chunk_index, doc_ids, band, kv)
-    dq, sums = attend_near(order, counts, qd, kv, own_t)
-    dq, sums, spill = attend_far(order, counts, qd, kv, own_t, halo, dq, sums, kv_packed)
+    dq, sums, rows, rows_t = attend_near(order, counts, qd, kv, own_t)
+    dq, sums, spill = attend_far(order, counts, qd, halo, dq, kv_packed, rows, rows_t, sums)
     spill = lax.ppermute(spill, "blk", [(s + step, s) for s in range(spans - step)])
     query_out = exchange(dq)
     dkv = exchange(add_spill(sums, spill))

time: 75.1 us -> 75.5 us (level)
  the two profiles are of different devices: /device:TPU:16 before, /device:TPU:0 now
where the time goes in v6:
time: 75.5 us; the launch traced here: 75.2 us
  waiting for transfers between devices  39.7 us (53%)
  starting transfers between devices  20.7 us (27%)
  Pallas kernels  13.9 us (18%)
  between operations  0.94 us (1%)
    all_to_all x4, waiting for transfers between devices, exchange(): lax.all_to_all(value, axes, split_axis=0, concat_axis=0, axis_index_group...  26.9 us
    all_to_all x4, starting transfers between devices, exchange(): lax.all_to_all(value, axes, split_axis=0, concat_axis=0, axis_index_group...  15.9 us
    ppermute x1, waiting for transfers between devices, per_device(): lax.ppermute(spill, 'blk', [(s + step, s) for s in range(spans - step)])  12.8 us
    pallas_call x1, Pallas kernels, attend_near(): pl.pallas_call(near_kernel, in_specs=[smem] * 2 + [vmem] * 3, out_specs=[...  4.52 us
    pallas_call x2, Pallas kernels, pack(): pl.pallas_call(pack_kernel, in_specs=[hbm] * 2, out_specs=hbm, out_shape=...  4 us
    ppermute x1, starting transfers between devices, per_device(): halo = lax.ppermute(kv, 'blk', [(s, s + step) for s in range(spans - step)])  3.54 us
    pallas_call x2, Pallas kernels, unpack(): pl.pallas_call(unpack_kernel, in_specs=[pl.BlockSpec(memory_space=pltpu.V...  1.76 us
  transfers between devices with their start and end apart: 6, of which 4 were waited for; matrix products, arithmetic and copies ran while one was open for 0% of the time, Pallas kernels for 13%

profile of v6, /device:TPU:0, one launch (start us, length us, event | category | flops | bytes accessed | tf_op | source)
XLA Modules:
  0.0 75.2 jit_solution(7860218787821020702)
XLA Ops:
  0.6 1.8 %shard_map.85.room_ref = bf16[8,128,256]{2,1,0:T(8,128)(2,1)} custom-call(bf16[128,1024]{1,0:T(8,128)(2,1)} %a_ref.2, bf16[128,1024]{1,0:T(8,128)(2,1)} %b_ref.2), custom_call_target="tpu_custom_call" | custom-call | tf_op jit(solution)/shard_map/pallas_call | solution.py:70
  2.5 5.2 %all-to-all-start = ((bf16[8,128,256]{2,1,0:T(8,128)(2,1)}), bf16[8,128,256]{2,1,0:T(8,128)(2,1)S(1)}, u32[]{:S(2)}, u32[]{:S(2)}) async-start(bf16[8,128,256]{2,1,0:T(8,128)(2,1)} %shard_map.85.room_ref), calls=%async_computation | async-start | bytes 1048576 | tf_op jit(solution)/shard_map/all_to_all | solution.py:371
  7.7 0.0 copy-start
  7.7 0.0 copy-start.1
  7.7 2.1 %shard_map.87 = bf16[8,128,512]{2,1,0:T(8,128)(2,1)} custom-call(bf16[128,2048]{1,0:T(8,128)(2,1)} %a_ref.3, bf16[128,2048]{1,0:T(8,128)(2,1)} %b_ref.3), custom_call_target="tpu_custom_call" | custom-call | tf_op jit(solution)/shard_map/pallas_call | solution.py:70
  9.8 7.6 %all-to-all-done.own_ref = bf16[8,128,256]{2,1,0:T(8,128)(2,1)S(1)} async-done(((bf16[8,128,256]{2,1,0:T(8,128)(2,1)}), bf16[8,128,256]{2,1,0:T(8,128)(2,1)S(1)}, u32[]{:S(2)}, u32[]{:S(2)}) %all-to-all-start) | async-done | bytes 524320 | tf_op jit(solution)/shard_map/all_to_all | solution.py:371
  17.4 3.6 %all-to-all-start.1 = ((bf16[8,128,512]{2,1,0:T(8,128)(2,1)}), bf16[8,128,512]{2,1,0:T(8,128)(2,1)S(1)}, u32[]{:S(2)}, u32[]{:S(2)}) async-start(bf16[8,128,512]{2,1,0:T(8,128)(2,1)} %shard_map.87), calls=%async_computation.1 | async-start | bytes 2097152 | tf_op jit(solution)/shard_map/all_to_all | solution.py:371
  21.0 3.5 %collective-permute-start = (bf16[8,128,256]{2,1,0:T(8,128)(2,1)S(1)}, bf16[8,128,256]{2,1,0:T(8,128)(2,1)S(1)}, u32[]{:S(2)}, u32[]{:S(2)}) collective-permute-start(bf16[8,128,256]{2,1,0:T(8,128)(2,1)S(1)} %all-to-all-done.own_ref), channel_id=1, source_target_pairs={{0,8},{2,10},{4,12},{6,14},{8,16},{10,18},{12,20},{14,22},{16,24},... | collective-permute-start | bytes 1572872 | tf_op jit(solution)/shard_map/ppermute | solution.py:377
  24.5 0.0 copy-done
  24.6 0.0 copy-done.1
  24.6 1.3 %shard_map.86 = (s32[8]{0:T(128)S(1)}, s32[10]{0:T(128)S(1)}, bf16[128,1024]{1,0:T(8,128)(2,1)S(1)}) custom-call(s32[1]{0:T(128)} %bitcast.chunk_ref, s32[32]{0:T(128)S(1)} %copy-done, s32[32]{0:T(128)S(1)} %copy-done.1, bf16[8,128,256]{2,1,0:T(8,128)(2,1)S(1)} %all-to-all-done.own_ref), custom_call_target="tpu_custom_call" | custom-call | tf_op jit(solution)/shard_map/pallas_call | solution.py:145
  25.9 10.4 %all-to-all-done.1.qd_ref = bf16[8,128,512]{2,1,0:T(8,128)(2,1)S(1)} async-done(((bf16[8,128,512]{2,1,0:T(8,128)(2,1)}), bf16[8,128,512]{2,1,0:T(8,128)(2,1)S(1)}, u32[]{:S(2)}, u32[]{:S(2)}) %all-to-all-start.1) | async-done | bytes 1048608 | tf_op jit(solution)/shard_map/all_to_all | solution.py:371
  36.3 4.5 %shard_map.88 = (bf16[8,128,256]{2,1,0:T(8,128)(2,1)S(1)}, f32[2048,256]{1,0:T(8,128)S(1)}, bf16[2048,256]{1,0:T(8,128)(2,1)S(1)}, bf16[128,2048]{1,0:T(8,128)(2,1)S(1)}) custom-call(s32[8]{0:T(128)S(1)} %get-tuple-element.15.order, s32[10]{0:T(128)S(1)} %get-tuple-element.16.counts, bf16[8,128,512]{2,1,0:T(8,128)(2,1)S(1)} %all-to-all-done.1.qd_ref, ...), custom_call_target="tpu_custom_call" | custom-call | tf_op jit(solution)/shard_map/pallas_call | solution.py:296
  40.8 0.0 collective-permute-done.halo_ref
  40.9 1.4 %shard_map.89 = (bf16[8,128,256]{2,1,0:T(8,128)(2,1)}, f32[1024,256]{1,0:T(8,128)S(1)}, bf16[8,128,256]{2,1,0:T(8,128)(2,1)S(1)}, bf16[2048,256]{1,0:T(8,128)(2,...) custom-call(s32[8]{0:T(128)S(1)} %get-tuple-element.15.order, ...), custom_call_target="tpu_custom_call", output_to_operand_aliasing={{0}: (5, {}), {2}: (3, {}), {3}: (6, {}), {4}: (7, {}), {5}... | custom-call | tf_op jit(solution)/shard_map/pallas_call | solution.py:316
  42.3 1.3 %collective-permute-start.1 = (bf16[8,128,256]{2,1,0:T(8,128)(2,1)S(1)}, bf16[8,128,256]{2,1,0:T(8,128)(2,1)S(1)}, u32[]{:S(2)}, u32[]{:S(2)}) collective-permute-start(bf16[8,128,256]{2,1,0:T(8,128)(2,1)S(1)} %get-tuple-element.24), channel_id=1, source_target_pairs={{8,0},{10,2},{12,4},{14,6},{16,8},{18,10},{20,12},{22,14},{24,16},... | collective-permute-start | bytes 1572872 | tf_op jit(solution)/shard_map/ppermute | solution.py:383
  43.6 3.5 %all-to-all-start.2 = ((bf16[8,128,256]{2,1,0:T(8,128)(2,1)}), bf16[8,128,256]{2,1,0:T(8,128)(2,1)S(1)}, u32[]{:S(2)}, u32[]{:S(2)}) async-start(bf16[8,128,256]{2,1,0:T(8,128)(2,1)} %get-tuple-element.22), calls=%async_computation.2 | async-start | bytes 1048576 | tf_op jit(solution)/shard_map/all_to_all | solution.py:371
  47.1 12.8 %collective-permute-done.1.spill_ref = bf16[8,128,256]{2,1,0:T(8,128)(2,1)S(1)} collective-permute-done((bf16[8,128,256]{2,1,0:T(8,128)(2,1)S(1)}, bf16[8,128,256]{2,1,0:T(8,128)(2,1)S(1)}, u32[]{:S(2)}, u32[]{:S(2)}) %collective-permute-start.1) | collective-permute-done | bytes 524320 | tf_op jit(solution)/shard_map/ppermute | solution.py:383
  59.9 0.9 %shard_map.91 = bf16[8,128,256]{2,1,0:T(8,128)(2,1)} custom-call(f32[1024,256]{1,0:T(8,128)S(1)} %get-tuple-element.23.sums_ref, bf16[8,128,256]{2,1,0:T(8,128)(2,1)S(1)} %collective-permute-done.1.spill_ref), custom_call_target="tpu_custom_call" | custom-call | tf_op jit(solution)/shard_map/pallas_call | solution.py:346
  60.8 0.0 all-to-all-done.2.in_ref
  60.8 3.6 %all-to-all-start.3 = ((bf16[8,128,256]{2,1,0:T(8,128)(2,1)}), bf16[8,128,256]{2,1,0:T(8,128)(2,1)S(1)}, u32[]{:S(2)}, u32[]{:S(2)}) async-start(bf16[8,128,256]{2,1,0:T(8,128)(2,1)} %shard_map.91), calls=%async_computation.3 | async-start | bytes 1048576 | tf_op jit(solution)/shard_map/all_to_all | solution.py:371
  64.4 0.8 %shard_map.90 = bf16[128,2048]{1,0:T(8,128)(2,1)} custom-call(bf16[8,128,256]{2,1,0:T(8,128)(2,1)S(1)} %all-to-all-done.2.in_ref), custom_call_target="tpu_custom_call" | custom-call | tf_op jit(solution)/shard_map/pallas_call | solution.py:99
  65.3 8.9 %all-to-all-done.3.in_ref = bf16[8,128,256]{2,1,0:T(8,128)(2,1)S(1)} async-done(((bf16[8,128,256]{2,1,0:T(8,128)(2,1)}), bf16[8,128,256]{2,1,0:T(8,128)(2,1)S(1)}, u32[]{:S(2)}, u32[]{:S(2)}) %all-to-all-start.3) | async-done | bytes 524320 | tf_op jit(solution)/shard_map/all_to_all | solution.py:371
  74.2 0.9 %shard_map.92 = (bf16[128,1024]{1,0:T(8,128)(2,1)}, bf16[128,1024]{1,0:T(8,128)(2,1)}) custom-call(bf16[8,128,256]{2,1,0:T(8,128)(2,1)S(1)} %all-to-all-done.3.in_ref), custom_call_target="tpu_custom_call" | custom-call | tf_op jit(solution)/shard_map/pallas_call | solution.py:99
Async XLA Ops:
  2.5 14.9 %all-to-all-start = ((bf16[8,128,256]{2,1,0:T(8,128)(2,1)}), bf16[8,128,256]{2,1,0:T(8,128)(2,1)S(1)}, u32[]{:S(2)}, u32[]{:S(2)}) async-start(bf16[8,128,256]{2,1,0:T(8,128)(2,1)} %shard_map.85.room_ref), calls=%async_computation | async-start | bytes 1048576 | tf_op jit(solution)/shard_map/all_to_all | solution.py:371
  7.7 16.9 %copy-start = (s32[32]{0:T(128)S(1)}, s32[32]{0:T(128)}, u32[]{:S(2)}) copy-start(s32[32]{0:T(128)} %doc_ref.1) | copy-start | bytes 388
  7.7 16.9 %copy-start.1 = (s32[32]{0:T(128)S(1)}, s32[32]{0:T(128)}, u32[]{:S(2)}) copy-start(s32[32]{0:T(128)} %band_ref.1) | copy-start | bytes 388
  17.4 18.9 %all-to-all-start.1 = ((bf16[8,128,512]{2,1,0:T(8,128)(2,1)}), bf16[8,128,512]{2,1,0:T(8,128)(2,1)S(1)}, u32[]{:S(2)}, u32[]{:S(2)}) async-start(bf16[8,128,512]{2,1,0:T(8,128)(2,1)} %shard_map.87), calls=%async_computation.1 | async-start | bytes 2097152 | tf_op jit(solution)/shard_map/all_to_all | solution.py:371
  21.0 19.9 %collective-permute-start = (bf16[8,128,256]{2,1,0:T(8,128)(2,1)S(1)}, bf16[8,128,256]{2,1,0:T(8,128)(2,1)S(1)}, u32[]{:S(2)}, u32[]{:S(2)}) collective-permute-start(bf16[8,128,256]{2,1,0:T(8,128)(2,1)S(1)} %all-to-all-done.own_ref), channel_id=1, source_target_pairs={{0,8},{2,10},{4,12},{6,14},{8,16},{10,18},{12,20},{14,22},{16,24},... | collective-permute-start | bytes 1572872 | tf_op jit(solution)/shard_map/ppermute | solution.py:377
  42.3 17.6 %collective-permute-start.1 = (bf16[8,128,256]{2,1,0:T(8,128)(2,1)S(1)}, bf16[8,128,256]{2,1,0:T(8,128)(2,1)S(1)}, u32[]{:S(2)}, u32[]{:S(2)}) collective-permute-start(bf16[8,128,256]{2,1,0:T(8,128)(2,1)S(1)} %get-tuple-element.24), channel_id=1, source_target_pairs={{8,0},{10,2},{12,4},{14,6},{16,8},{18,10},{20,12},{22,14},{24,16},... | collective-permute-start | bytes 1572872 | tf_op jit(solution)/shard_map/ppermute | solution.py:383
  43.6 17.2 %all-to-all-start.2 = ((bf16[8,128,256]{2,1,0:T(8,128)(2,1)}), bf16[8,128,256]{2,1,0:T(8,128)(2,1)S(1)}, u32[]{:S(2)}, u32[]{:S(2)}) async-start(bf16[8,128,256]{2,1,0:T(8,128)(2,1)} %get-tuple-element.22), calls=%async_computation.2 | async-start | bytes 1048576 | tf_op jit(solution)/shard_map/all_to_all | solution.py:371
  60.8 13.4 %all-to-all-start.3 = ((bf16[8,128,256]{2,1,0:T(8,128)(2,1)}), bf16[8,128,256]{2,1,0:T(8,128)(2,1)S(1)}, u32[]{:S(2)}, u32[]{:S(2)}) async-start(bf16[8,128,256]{2,1,0:T(8,128)(2,1)} %shard_map.91), calls=%async_computation.3 | async-start | bytes 1048576 | tf_op jit(solution)/shard_map/all_to_all | solution.py:371

commit v7 on v6

--- a/solution.py
+++ b/solution.py
@@ -186,14 +186,15 @@
         dq_copy(dq_near_ref, order[m]).start()
         return carry
 
-    def fill(j, carry):
-        rows = pl.ds(pl.multiple_of(j * BLOCK, BLOCK), BLOCK)
-        kv[rows, :] = halo_ref[j]
-        keys_t[:, rows] = halo_ref[j, :, :HEAD].T
-        return carry
-
     lax.fori_loop(0, steps * TOGETHER, pass_on, 0)
-    lax.fori_loop(counts[blocks + 1], WB, fill, 0)
+
+    @pl.when(counts[blocks + 1] < WB)
+    def fill():
+        for j in range(WB):
+            rows = slice(j * BLOCK, (j + 1) * BLOCK)
+            kv[rows, :] = halo_ref[j]
+            keys_t[:, rows] = halo_ref[j, :, :HEAD].T
+
     attend(
         steps, blocks // TOGETHER, order, counts, qd_ref, kv, keys_t, dq_slabs, sums,
         lambda i: dq_copy(dq_slabs, i).start(),

time: 75.5 us -> 74.2 us (0.983)
  waiting for transfers between devices: 39.7 us -> 37 us
  starting transfers between devices: 20.7 us -> 22 us
    ppermute x1, waiting for transfers between devices: 12.8 us -> 10.1 us  [per_device(): lax.ppermute(spill, 'blk', [(s + step, s) for s in range(spans - step)])]
    all_to_all x4, starting transfers between devices: 15.9 us -> 17.1 us  [exchange(): lax.all_to_all(value, axes, split_axis=0, concat_axis=0, axis_index_group...]
where the time goes in v7:
time: 74.2 us; the launch traced here: 73.8 us
  waiting for transfers between devices  37 us (50%)
  starting transfers between devices  22 us (30%)
  Pallas kernels  13.9 us (19%)
  between operations  0.94 us (1%)
    all_to_all x4, waiting for transfers between devices, exchange(): lax.all_to_all(value, axes, split_axis=0, concat_axis=0, axis_index_group...  26.9 us
    all_to_all x4, starting transfers between devices, exchange(): lax.all_to_all(value, axes, split_axis=0, concat_axis=0, axis_index_group...  17.1 us
    ppermute x1, waiting for transfers between devices, per_device(): lax.ppermute(spill, 'blk', [(s + step, s) for s in range(spans - step)])  10.1 us
    pallas_call x1, Pallas kernels, attend_near(): pl.pallas_call(near_kernel, in_specs=[smem] * 2 + [vmem] * 3, out_specs=[...  4.56 us
    pallas_call x2, Pallas kernels, pack(): pl.pallas_call(pack_kernel, in_specs=[hbm] * 2, out_specs=hbm, out_shape=...  4 us
    ppermute x1, starting transfers between devices, per_device(): halo = lax.ppermute(kv, 'blk', [(s, s + step) for s in range(spans - step)])  3.54 us
    pallas_call x2, Pallas kernels, unpack(): pl.pallas_call(unpack_kernel, in_specs=[pl.BlockSpec(memory_space=pltpu.V...  1.76 us
  transfers between devices with their start and end apart: 6, of which 4 were waited for; matrix products, arithmetic and copies ran while one was open for 0% of the time, Pallas kernels for 13%

profile of v7, /device:TPU:0, one launch (start us, length us, event | category | flops | bytes accessed | tf_op | source)
XLA Modules:
  0.0 73.8 jit_solution(12608440518870340657)
XLA Ops:
  0.6 1.8 %shard_map.85.room_ref = bf16[8,128,256]{2,1,0:T(8,128)(2,1)} custom-call(bf16[128,1024]{1,0:T(8,128)(2,1)} %a_ref.2, bf16[128,1024]{1,0:T(8,128)(2,1)} %b_ref.2), custom_call_target="tpu_custom_call" | custom-call | tf_op jit(solution)/shard_map/pallas_call | solution.py:70
  2.5 5.2 %all-to-all-start = ((bf16[8,128,256]{2,1,0:T(8,128)(2,1)}), bf16[8,128,256]{2,1,0:T(8,128)(2,1)S(1)}, u32[]{:S(2)}, u32[]{:S(2)}) async-start(bf16[8,128,256]{2,1,0:T(8,128)(2,1)} %shard_map.85.room_ref), calls=%async_computation | async-start | bytes 1048576 | tf_op jit(solution)/shard_map/all_to_all | solution.py:372
  7.7 0.0 copy-start
  7.7 0.0 copy-start.1
  7.7 2.1 %shard_map.87 = bf16[8,128,512]{2,1,0:T(8,128)(2,1)} custom-call(bf16[128,2048]{1,0:T(8,128)(2,1)} %a_ref.3, bf16[128,2048]{1,0:T(8,128)(2,1)} %b_ref.3), custom_call_target="tpu_custom_call" | custom-call | tf_op jit(solution)/shard_map/pallas_call | solution.py:70
  9.8 7.6 %all-to-all-done.own_ref = bf16[8,128,256]{2,1,0:T(8,128)(2,1)S(1)} async-done(((bf16[8,128,256]{2,1,0:T(8,128)(2,1)}), bf16[8,128,256]{2,1,0:T(8,128)(2,1)S(1)}, u32[]{:S(2)}, u32[]{:S(2)}) %all-to-all-start) | async-done | bytes 524320 | tf_op jit(solution)/shard_map/all_to_all | solution.py:372
  17.4 3.6 %all-to-all-start.1 = ((bf16[8,128,512]{2,1,0:T(8,128)(2,1)}), bf16[8,128,512]{2,1,0:T(8,128)(2,1)S(1)}, u32[]{:S(2)}, u32[]{:S(2)}) async-start(bf16[8,128,512]{2,1,0:T(8,128)(2,1)} %shard_map.87), calls=%async_computation.1 | async-start | bytes 2097152 | tf_op jit(solution)/shard_map/all_to_all | solution.py:372
  21.0 3.5 %collective-permute-start = (bf16[8,128,256]{2,1,0:T(8,128)(2,1)S(1)}, bf16[8,128,256]{2,1,0:T(8,128)(2,1)S(1)}, u32[]{:S(2)}, u32[]{:S(2)}) collective-permute-start(bf16[8,128,256]{2,1,0:T(8,128)(2,1)S(1)} %all-to-all-done.own_ref), channel_id=1, source_target_pairs={{0,8},{2,10},{4,12},{6,14},{8,16},{10,18},{12,20},{14,22},{16,24},... | collective-permute-start | bytes 1572872 | tf_op jit(solution)/shard_map/ppermute | solution.py:378
  24.5 0.0 copy-done
  24.6 0.0 copy-done.1
  24.6 1.3 %shard_map.86 = (s32[8]{0:T(128)S(1)}, s32[10]{0:T(128)S(1)}, bf16[128,1024]{1,0:T(8,128)(2,1)S(1)}) custom-call(s32[1]{0:T(128)} %bitcast.chunk_ref, s32[32]{0:T(128)S(1)} %copy-done, s32[32]{0:T(128)S(1)} %copy-done.1, bf16[8,128,256]{2,1,0:T(8,128)(2,1)S(1)} %all-to-all-done.own_ref), custom_call_target="tpu_custom_call" | custom-call | tf_op jit(solution)/shard_map/pallas_call | solution.py:145
  25.9 10.4 %all-to-all-done.1.qd_ref = bf16[8,128,512]{2,1,0:T(8,128)(2,1)S(1)} async-done(((bf16[8,128,512]{2,1,0:T(8,128)(2,1)}), bf16[8,128,512]{2,1,0:T(8,128)(2,1)S(1)}, u32[]{:S(2)}, u32[]{:S(2)}) %all-to-all-start.1) | async-done | bytes 1048608 | tf_op jit(solution)/shard_map/all_to_all | solution.py:372
  36.3 4.6 %shard_map.88 = (bf16[8,128,256]{2,1,0:T(8,128)(2,1)S(1)}, f32[2048,256]{1,0:T(8,128)S(1)}, bf16[2048,256]{1,0:T(8,128)(2,1)S(1)}, bf16[128,2048]{1,0:T(8,128)(2,1)S(1)}) custom-call(s32[8]{0:T(128)S(1)} %get-tuple-element.15.order, s32[10]{0:T(128)S(1)} %get-tuple-element.16.counts, bf16[8,128,512]{2,1,0:T(8,128)(2,1)S(1)} %all-to-all-done.1.qd_ref, ...), custom_call_target="tpu_custom_call" | custom-call | tf_op jit(solution)/shard_map/pallas_call | solution.py:297
  40.9 0.0 collective-permute-done.halo_ref
  40.9 1.4 %shard_map.89 = (bf16[8,128,256]{2,1,0:T(8,128)(2,1)}, f32[1024,256]{1,0:T(8,128)S(1)}, bf16[8,128,256]{2,1,0:T(8,128)(2,1)S(1)}, bf16[2048,256]{1,0:T(8,128)(2,...) custom-call(s32[8]{0:T(128)S(1)} %get-tuple-element.15.order, ...), custom_call_target="tpu_custom_call", output_to_operand_aliasing={{0}: (5, {}), {2}: (3, {}), {3}: (6, {}), {4}: (7, {}), {5}... | custom-call | tf_op jit(solution)/shard_map/pallas_call | solution.py:317
  42.3 1.3 %collective-permute-start.1 = (bf16[8,128,256]{2,1,0:T(8,128)(2,1)S(1)}, bf16[8,128,256]{2,1,0:T(8,128)(2,1)S(1)}, u32[]{:S(2)}, u32[]{:S(2)}) collective-permute-start(bf16[8,128,256]{2,1,0:T(8,128)(2,1)S(1)} %get-tuple-element.24), channel_id=1, source_target_pairs={{8,0},{10,2},{12,4},{14,6},{16,8},{18,10},{20,12},{22,14},{24,16},... | collective-permute-start | bytes 1572872 | tf_op jit(solution)/shard_map/ppermute | solution.py:384
  43.6 3.5 %all-to-all-start.2 = ((bf16[8,128,256]{2,1,0:T(8,128)(2,1)}), bf16[8,128,256]{2,1,0:T(8,128)(2,1)S(1)}, u32[]{:S(2)}, u32[]{:S(2)}) async-start(bf16[8,128,256]{2,1,0:T(8,128)(2,1)} %get-tuple-element.22), calls=%async_computation.2 | async-start | bytes 1048576 | tf_op jit(solution)/shard_map/all_to_all | solution.py:372
  47.1 10.1 %collective-permute-done.1.spill_ref = bf16[8,128,256]{2,1,0:T(8,128)(2,1)S(1)} collective-permute-done((bf16[8,128,256]{2,1,0:T(8,128)(2,1)S(1)}, bf16[8,128,256]{2,1,0:T(8,128)(2,1)S(1)}, u32[]{:S(2)}, u32[]{:S(2)}) %collective-permute-start.1) | collective-permute-done | bytes 524320 | tf_op jit(solution)/shard_map/ppermute | solution.py:384
  57.2 0.9 %shard_map.91 = bf16[8,128,256]{2,1,0:T(8,128)(2,1)} custom-call(f32[1024,256]{1,0:T(8,128)S(1)} %get-tuple-element.23.sums_ref, bf16[8,128,256]{2,1,0:T(8,128)(2,1)S(1)} %collective-permute-done.1.spill_ref), custom_call_target="tpu_custom_call" | custom-call | tf_op jit(solution)/shard_map/pallas_call | solution.py:347
  58.1 0.0 all-to-all-done.2.in_ref
  58.1 4.9 %all-to-all-start.3 = ((bf16[8,128,256]{2,1,0:T(8,128)(2,1)}), bf16[8,128,256]{2,1,0:T(8,128)(2,1)S(1)}, u32[]{:S(2)}, u32[]{:S(2)}) async-start(bf16[8,128,256]{2,1,0:T(8,128)(2,1)} %shard_map.91), calls=%async_computation.3 | async-start | bytes 1048576 | tf_op jit(solution)/shard_map/all_to_all | solution.py:372
  63.0 0.8 %shard_map.90 = bf16[128,2048]{1,0:T(8,128)(2,1)} custom-call(bf16[8,128,256]{2,1,0:T(8,128)(2,1)S(1)} %all-to-all-done.2.in_ref), custom_call_target="tpu_custom_call" | custom-call | tf_op jit(solution)/shard_map/pallas_call | solution.py:99
  63.8 8.9 %all-to-all-done.3.in_ref = bf16[8,128,256]{2,1,0:T(8,128)(2,1)S(1)} async-done(((bf16[8,128,256]{2,1,0:T(8,128)(2,1)}), bf16[8,128,256]{2,1,0:T(8,128)(2,1)S(1)}, u32[]{:S(2)}, u32[]{:S(2)}) %all-to-all-start.3) | async-done | bytes 524320 | tf_op jit(solution)/shard_map/all_to_all | solution.py:372
  72.7 0.9 %shard_map.92 = (bf16[128,1024]{1,0:T(8,128)(2,1)}, bf16[128,1024]{1,0:T(8,128)(2,1)}) custom-call(bf16[8,128,256]{2,1,0:T(8,128)(2,1)S(1)} %all-to-all-done.3.in_ref), custom_call_target="tpu_custom_call" | custom-call | tf_op jit(solution)/shard_map/pallas_call | solution.py:99
Async XLA Ops:
  2.5 14.9 %all-to-all-start = ((bf16[8,128,256]{2,1,0:T(8,128)(2,1)}), bf16[8,128,256]{2,1,0:T(8,128)(2,1)S(1)}, u32[]{:S(2)}, u32[]{:S(2)}) async-start(bf16[8,128,256]{2,1,0:T(8,128)(2,1)} %shard_map.85.room_ref), calls=%async_computation | async-start | bytes 1048576 | tf_op jit(solution)/shard_map/all_to_all | solution.py:372
  7.7 16.9 %copy-start = (s32[32]{0:T(128)S(1)}, s32[32]{0:T(128)}, u32[]{:S(2)}) copy-start(s32[32]{0:T(128)} %doc_ref.1) | copy-start | bytes 388
  7.7 16.9 %copy-start.1 = (s32[32]{0:T(128)S(1)}, s32[32]{0:T(128)}, u32[]{:S(2)}) copy-start(s32[32]{0:T(128)} %band_ref.1) | copy-start | bytes 388
  17.4 18.9 %all-to-all-start.1 = ((bf16[8,128,512]{2,1,0:T(8,128)(2,1)}), bf16[8,128,512]{2,1,0:T(8,128)(2,1)S(1)}, u32[]{:S(2)}, u32[]{:S(2)}) async-start(bf16[8,128,512]{2,1,0:T(8,128)(2,1)} %shard_map.87), calls=%async_computation.1 | async-start | bytes 2097152 | tf_op jit(solution)/shard_map/all_to_all | solution.py:372
  21.0 19.9 %collective-permute-start = (bf16[8,128,256]{2,1,0:T(8,128)(2,1)S(1)}, bf16[8,128,256]{2,1,0:T(8,128)(2,1)S(1)}, u32[]{:S(2)}, u32[]{:S(2)}) collective-permute-start(bf16[8,128,256]{2,1,0:T(8,128)(2,1)S(1)} %all-to-all-done.own_ref), channel_id=1, source_target_pairs={{0,8},{2,10},{4,12},{6,14},{8,16},{10,18},{12,20},{14,22},{16,24},... | collective-permute-start | bytes 1572872 | tf_op jit(solution)/shard_map/ppermute | solution.py:378
  42.3 14.9 %collective-permute-start.1 = (bf16[8,128,256]{2,1,0:T(8,128)(2,1)S(1)}, bf16[8,128,256]{2,1,0:T(8,128)(2,1)S(1)}, u32[]{:S(2)}, u32[]{:S(2)}) collective-permute-start(bf16[8,128,256]{2,1,0:T(8,128)(2,1)S(1)} %get-tuple-element.24), channel_id=1, source_target_pairs={{8,0},{10,2},{12,4},{14,6},{16,8},{18,10},{20,12},{22,14},{24,16},... | collective-permute-start | bytes 1572872 | tf_op jit(solution)/shard_map/ppermute | solution.py:384
  43.6 14.5 %all-to-all-start.2 = ((bf16[8,128,256]{2,1,0:T(8,128)(2,1)}), bf16[8,128,256]{2,1,0:T(8,128)(2,1)S(1)}, u32[]{:S(2)}, u32[]{:S(2)}) async-start(bf16[8,128,256]{2,1,0:T(8,128)(2,1)} %get-tuple-element.22), calls=%async_computation.2 | async-start | bytes 1048576 | tf_op jit(solution)/shard_map/all_to_all | solution.py:372
  58.1 14.6 %all-to-all-start.3 = ((bf16[8,128,256]{2,1,0:T(8,128)(2,1)}), bf16[8,128,256]{2,1,0:T(8,128)(2,1)S(1)}, u32[]{:S(2)}, u32[]{:S(2)}) async-start(bf16[8,128,256]{2,1,0:T(8,128)(2,1)} %shard_map.91), calls=%async_computation.3 | async-start | bytes 1048576 | tf_op jit(solution)/shard_map/all_to_all | solution.py:372

commit v8 on v7

--- a/solution.py
+++ b/solution.py
@@ -241,16 +241,20 @@
         for n in lanes:
             scores[n][-1] = jnp.where(causal, scores[n][-1], -jnp.inf)
             seen = [count - b <= sizes[n] for b in range(count)]
-            tops = [
-                jnp.where(seen[b], fold(x, jnp.max), -jnp.inf) for b, x in enumerate(scores[n])
-            ]
-            top = jnp.max(functools.reduce(jnp.maximum, tops), axis=0, keepdims=True)
-            shift = [jnp.where(seen[b], top, jnp.inf) for b in range(count)]
             dprob[n] = split(dot(kv[windows[n], HEAD:], grad[n], NT))
-            expo = [jnp.exp2((x - y) * (SCALE * LOG2E)) for x, y in zip(scores[n], shift)]
-            total = functools.reduce(jnp.add, [fold(x, jnp.sum) for x in expo])
-            inverse = 1.0 / jnp.sum(total, axis=0, keepdims=True)
-            probs[n] = [x * inverse for x in expo]
+            tops, expo, totals = [], [], []
+            for x in scores[n]:
+                top = jnp.max(fold(x, jnp.max), axis=0, keepdims=True)
+                x = jnp.exp2((x - top) * (SCALE * LOG2E))
+                tops.append(top)
+                expo.append(x)
+                totals.append(jnp.sum(fold(x, jnp.sum), axis=0, keepdims=True))
+            shown = [jnp.where(y, x, -jnp.inf) for x, y in zip(tops, seen)]
+            top = functools.reduce(jnp.maximum, shown)
+            parts = [jnp.exp2((x - top) * (SCALE * LOG2E)) for x in shown]
+            total = functools.reduce(jnp.add, [x * y for x, y in zip(totals, parts)])
+            inverse = 1.0 / total
+            probs[n] = [x * (y * inverse) for x, y in zip(expo, parts)]
             probs_b[n] = [x.astype(jnp.bfloat16) for x in probs[n]]
         dscore = {}
         for n in lanes:

time: 74.2 us -> 74 us (level)
  no operation moved by 1% of the time
where the time goes in v8:
time: 74 us; the launch traced here: 73 us
  waiting for transfers between devices  36.3 us (49%)
  starting transfers between devices  22 us (30%)
  Pallas kernels  13.9 us (19%)
  between operations  0.94 us (1%)
    all_to_all x4, waiting for transfers between devices, exchange(): lax.all_to_all(value, axes, split_axis=0, concat_axis=0, axis_index_group...  26.9 us
    all_to_all x4, starting transfers between devices, exchange(): lax.all_to_all(value, axes, split_axis=0, concat_axis=0, axis_index_group...  17.1 us
    ppermute x1, waiting for transfers between devices, per_device(): lax.ppermute(spill, 'blk', [(s + step, s) for s in range(spans - step)])  9.38 us
    pallas_call x1, Pallas kernels, attend_near(): pl.pallas_call(near_kernel, in_specs=[smem] * 2 + [vmem] * 3, out_specs=[...  4.5 us
    pallas_call x2, Pallas kernels, pack(): pl.pallas_call(pack_kernel, in_specs=[hbm] * 2, out_specs=hbm, out_shape=...  4 us
    ppermute x1, starting transfers between devices, per_device(): halo = lax.ppermute(kv, 'blk', [(s, s + step) for s in range(spans - step)])  3.54 us
    pallas_call x2, Pallas kernels, unpack(): pl.pallas_call(unpack_kernel, in_specs=[pl.BlockSpec(memory_space=pltpu.V...  1.76 us
  transfers between devices with their start and end apart: 6, of which 4 were waited for; matrix products, arithmetic and copies ran while one was open for 0% of the time, Pallas kernels for 13%

profile of v8, /device:TPU:0, one launch (start us, length us, event | category | flops | bytes accessed | tf_op | source)
XLA Modules:
  0.0 73.0 jit_solution(7511132276468655477)
XLA Ops:
  0.6 1.8 %shard_map.85.room_ref = bf16[8,128,256]{2,1,0:T(8,128)(2,1)} custom-call(bf16[128,1024]{1,0:T(8,128)(2,1)} %a_ref.2, bf16[128,1024]{1,0:T(8,128)(2,1)} %b_ref.2), custom_call_target="tpu_custom_call" | custom-call | tf_op jit(solution)/shard_map/pallas_call | solution.py:70
  2.5 5.2 %all-to-all-start = ((bf16[8,128,256]{2,1,0:T(8,128)(2,1)}), bf16[8,128,256]{2,1,0:T(8,128)(2,1)S(1)}, u32[]{:S(2)}, u32[]{:S(2)}) async-start(bf16[8,128,256]{2,1,0:T(8,128)(2,1)} %shard_map.85.room_ref), calls=%async_computation | async-start | bytes 1048576 | tf_op jit(solution)/shard_map/all_to_all | solution.py:376
  7.7 0.0 copy-start
  7.7 0.0 copy-start.1
  7.7 2.1 %shard_map.87 = bf16[8,128,512]{2,1,0:T(8,128)(2,1)} custom-call(bf16[128,2048]{1,0:T(8,128)(2,1)} %a_ref.3, bf16[128,2048]{1,0:T(8,128)(2,1)} %b_ref.3), custom_call_target="tpu_custom_call" | custom-call | tf_op jit(solution)/shard_map/pallas_call | solution.py:70
  9.8 7.6 %all-to-all-done.own_ref = bf16[8,128,256]{2,1,0:T(8,128)(2,1)S(1)} async-done(((bf16[8,128,256]{2,1,0:T(8,128)(2,1)}), bf16[8,128,256]{2,1,0:T(8,128)(2,1)S(1)}, u32[]{:S(2)}, u32[]{:S(2)}) %all-to-all-start) | async-done | bytes 524320 | tf_op jit(solution)/shard_map/all_to_all | solution.py:376
  17.4 3.6 %all-to-all-start.1 = ((bf16[8,128,512]{2,1,0:T(8,128)(2,1)}), bf16[8,128,512]{2,1,0:T(8,128)(2,1)S(1)}, u32[]{:S(2)}, u32[]{:S(2)}) async-start(bf16[8,128,512]{2,1,0:T(8,128)(2,1)} %shard_map.87), calls=%async_computation.1 | async-start | bytes 2097152 | tf_op jit(solution)/shard_map/all_to_all | solution.py:376
  21.0 3.5 %collective-permute-start = (bf16[8,128,256]{2,1,0:T(8,128)(2,1)S(1)}, bf16[8,128,256]{2,1,0:T(8,128)(2,1)S(1)}, u32[]{:S(2)}, u32[]{:S(2)}) collective-permute-start(bf16[8,128,256]{2,1,0:T(8,128)(2,1)S(1)} %all-to-all-done.own_ref), channel_id=1, source_target_pairs={{0,8},{2,10},{4,12},{6,14},{8,16},{10,18},{12,20},{14,22},{16,24},... | collective-permute-start | bytes 1572872 | tf_op jit(solution)/shard_map/ppermute | solution.py:382
  24.5 0.0 copy-done
  24.6 0.0 copy-done.1
  24.6 1.3 %shard_map.86 = (s32[8]{0:T(128)S(1)}, s32[10]{0:T(128)S(1)}, bf16[128,1024]{1,0:T(8,128)(2,1)S(1)}) custom-call(s32[1]{0:T(128)} %bitcast.chunk_ref, s32[32]{0:T(128)S(1)} %copy-done, s32[32]{0:T(128)S(1)} %copy-done.1, bf16[8,128,256]{2,1,0:T(8,128)(2,1)S(1)} %all-to-all-done.own_ref), custom_call_target="tpu_custom_call" | custom-call | tf_op jit(solution)/shard_map/pallas_call | solution.py:145
  25.9 10.4 %all-to-all-done.1.qd_ref = bf16[8,128,512]{2,1,0:T(8,128)(2,1)S(1)} async-done(((bf16[8,128,512]{2,1,0:T(8,128)(2,1)}), bf16[8,128,512]{2,1,0:T(8,128)(2,1)S(1)}, u32[]{:S(2)}, u32[]{:S(2)}) %all-to-all-start.1) | async-done | bytes 1048608 | tf_op jit(solution)/shard_map/all_to_all | solution.py:376
  36.3 4.5 %shard_map.88 = (bf16[8,128,256]{2,1,0:T(8,128)(2,1)S(1)}, f32[2048,256]{1,0:T(8,128)S(1)}, bf16[2048,256]{1,0:T(8,128)(2,1)S(1)}, bf16[128,2048]{1,0:T(8,128)(2,1)S(1)}) custom-call(s32[8]{0:T(128)S(1)} %get-tuple-element.15.order, s32[10]{0:T(128)S(1)} %get-tuple-element.16.counts, bf16[8,128,512]{2,1,0:T(8,128)(2,1)S(1)} %all-to-all-done.1.qd_ref, ...), custom_call_target="tpu_custom_call" | custom-call | tf_op jit(solution)/shard_map/pallas_call | solution.py:301
  40.8 0.0 collective-permute-done.halo_ref
  40.8 1.4 %shard_map.89 = (bf16[8,128,256]{2,1,0:T(8,128)(2,1)}, f32[1024,256]{1,0:T(8,128)S(1)}, bf16[8,128,256]{2,1,0:T(8,128)(2,1)S(1)}, bf16[2048,256]{1,0:T(8,128)(2,...) custom-call(s32[8]{0:T(128)S(1)} %get-tuple-element.15.order, ...), custom_call_target="tpu_custom_call", output_to_operand_aliasing={{0}: (5, {}), {2}: (3, {}), {3}: (6, {}), {4}: (7, {}), {5}... | custom-call | tf_op jit(solution)/shard_map/pallas_call | solution.py:321
  42.3 1.3 %collective-permute-start.1 = (bf16[8,128,256]{2,1,0:T(8,128)(2,1)S(1)}, bf16[8,128,256]{2,1,0:T(8,128)(2,1)S(1)}, u32[]{:S(2)}, u32[]{:S(2)}) collective-permute-start(bf16[8,128,256]{2,1,0:T(8,128)(2,1)S(1)} %get-tuple-element.24), channel_id=1, source_target_pairs={{8,0},{10,2},{12,4},{14,6},{16,8},{18,10},{20,12},{22,14},{24,16},... | collective-permute-start | bytes 1572872 | tf_op jit(solution)/shard_map/ppermute | solution.py:388
  43.6 3.5 %all-to-all-start.2 = ((bf16[8,128,256]{2,1,0:T(8,128)(2,1)}), bf16[8,128,256]{2,1,0:T(8,128)(2,1)S(1)}, u32[]{:S(2)}, u32[]{:S(2)}) async-start(bf16[8,128,256]{2,1,0:T(8,128)(2,1)} %get-tuple-element.22), calls=%async_computation.2 | async-start | bytes 1048576 | tf_op jit(solution)/shard_map/all_to_all | solution.py:376
  47.1 9.4 %collective-permute-done.1.spill_ref = bf16[8,128,256]{2,1,0:T(8,128)(2,1)S(1)} collective-permute-done((bf16[8,128,256]{2,1,0:T(8,128)(2,1)S(1)}, bf16[8,128,256]{2,1,0:T(8,128)(2,1)S(1)}, u32[]{:S(2)}, u32[]{:S(2)}) %collective-permute-start.1) | collective-permute-done | bytes 524320 | tf_op jit(solution)/shard_map/ppermute | solution.py:388
  56.4 0.9 %shard_map.91 = bf16[8,128,256]{2,1,0:T(8,128)(2,1)} custom-call(f32[1024,256]{1,0:T(8,128)S(1)} %get-tuple-element.23.sums_ref, bf16[8,128,256]{2,1,0:T(8,128)(2,1)S(1)} %collective-permute-done.1.spill_ref), custom_call_target="tpu_custom_call" | custom-call | tf_op jit(solution)/shard_map/pallas_call | solution.py:351
  57.3 0.0 all-to-all-done.2.in_ref
  57.3 4.9 %all-to-all-start.3 = ((bf16[8,128,256]{2,1,0:T(8,128)(2,1)}), bf16[8,128,256]{2,1,0:T(8,128)(2,1)S(1)}, u32[]{:S(2)}, u32[]{:S(2)}) async-start(bf16[8,128,256]{2,1,0:T(8,128)(2,1)} %shard_map.91), calls=%async_computation.3 | async-start | bytes 1048576 | tf_op jit(solution)/shard_map/all_to_all | solution.py:376
  62.2 0.8 %shard_map.90 = bf16[128,2048]{1,0:T(8,128)(2,1)} custom-call(bf16[8,128,256]{2,1,0:T(8,128)(2,1)S(1)} %all-to-all-done.2.in_ref), custom_call_target="tpu_custom_call" | custom-call | tf_op jit(solution)/shard_map/pallas_call | solution.py:99
  63.1 8.9 %all-to-all-done.3.in_ref = bf16[8,128,256]{2,1,0:T(8,128)(2,1)S(1)} async-done(((bf16[8,128,256]{2,1,0:T(8,128)(2,1)}), bf16[8,128,256]{2,1,0:T(8,128)(2,1)S(1)}, u32[]{:S(2)}, u32[]{:S(2)}) %all-to-all-start.3) | async-done | bytes 524320 | tf_op jit(solution)/shard_map/all_to_all | solution.py:376
  72.0 0.9 %shard_map.92 = (bf16[128,1024]{1,0:T(8,128)(2,1)}, bf16[128,1024]{1,0:T(8,128)(2,1)}) custom-call(bf16[8,128,256]{2,1,0:T(8,128)(2,1)S(1)} %all-to-all-done.3.in_ref), custom_call_target="tpu_custom_call" | custom-call | tf_op jit(solution)/shard_map/pallas_call | solution.py:99
Async XLA Ops:
  2.5 14.9 %all-to-all-start = ((bf16[8,128,256]{2,1,0:T(8,128)(2,1)}), bf16[8,128,256]{2,1,0:T(8,128)(2,1)S(1)}, u32[]{:S(2)}, u32[]{:S(2)}) async-start(bf16[8,128,256]{2,1,0:T(8,128)(2,1)} %shard_map.85.room_ref), calls=%async_computation | async-start | bytes 1048576 | tf_op jit(solution)/shard_map/all_to_all | solution.py:376
  7.7 16.9 %copy-start = (s32[32]{0:T(128)S(1)}, s32[32]{0:T(128)}, u32[]{:S(2)}) copy-start(s32[32]{0:T(128)} %doc_ref.1) | copy-start | bytes 388
  7.7 16.9 %copy-start.1 = (s32[32]{0:T(128)S(1)}, s32[32]{0:T(128)}, u32[]{:S(2)}) copy-start(s32[32]{0:T(128)} %band_ref.1) | copy-start | bytes 388
  17.4 18.9 %all-to-all-start.1 = ((bf16[8,128,512]{2,1,0:T(8,128)(2,1)}), bf16[8,128,512]{2,1,0:T(8,128)(2,1)S(1)}, u32[]{:S(2)}, u32[]{:S(2)}) async-start(bf16[8,128,512]{2,1,0:T(8,128)(2,1)} %shard_map.87), calls=%async_computation.1 | async-start | bytes 2097152 | tf_op jit(solution)/shard_map/all_to_all | solution.py:376
  21.0 19.9 %collective-permute-start = (bf16[8,128,256]{2,1,0:T(8,128)(2,1)S(1)}, bf16[8,128,256]{2,1,0:T(8,128)(2,1)S(1)}, u32[]{:S(2)}, u32[]{:S(2)}) collective-permute-start(bf16[8,128,256]{2,1,0:T(8,128)(2,1)S(1)} %all-to-all-done.own_ref), channel_id=1, source_target_pairs={{0,8},{2,10},{4,12},{6,14},{8,16},{10,18},{12,20},{14,22},{16,24},... | collective-permute-start | bytes 1572872 | tf_op jit(solution)/shard_map/ppermute | solution.py:382
  42.3 14.2 %collective-permute-start.1 = (bf16[8,128,256]{2,1,0:T(8,128)(2,1)S(1)}, bf16[8,128,256]{2,1,0:T(8,128)(2,1)S(1)}, u32[]{:S(2)}, u32[]{:S(2)}) collective-permute-start(bf16[8,128,256]{2,1,0:T(8,128)(2,1)S(1)} %get-tuple-element.24), channel_id=1, source_target_pairs={{8,0},{10,2},{12,4},{14,6},{16,8},{18,10},{20,12},{22,14},{24,16},... | collective-permute-start | bytes 1572872 | tf_op jit(solution)/shard_map/ppermute | solution.py:388
  43.6 13.8 %all-to-all-start.2 = ((bf16[8,128,256]{2,1,0:T(8,128)(2,1)}), bf16[8,128,256]{2,1,0:T(8,128)(2,1)S(1)}, u32[]{:S(2)}, u32[]{:S(2)}) async-start(bf16[8,128,256]{2,1,0:T(8,128)(2,1)} %get-tuple-element.22), calls=%async_computation.2 | async-start | bytes 1048576 | tf_op jit(solution)/shard_map/all_to_all | solution.py:376
  57.3 14.6 %all-to-all-start.3 = ((bf16[8,128,256]{2,1,0:T(8,128)(2,1)}), bf16[8,128,256]{2,1,0:T(8,128)(2,1)S(1)}, u32[]{:S(2)}, u32[]{:S(2)}) async-start(bf16[8,128,256]{2,1,0:T(8,128)(2,1)} %shard_map.91), calls=%async_computation.3 | async-start | bytes 1048576 | tf_op jit(solution)/shard_map/all_to_all | solution.py:376

commit v9 on v8

--- a/solution.py
+++ b/solution.py
@@ -277,10 +277,12 @@
         for n, i in enumerate(members):
             sums[windows[n], :HEAD] += dot(dscore[n], query[n], NN)
             query_grad = dot(keys_t[:, windows[n]], dscore[n], NN) * SCALE
+            query_grad = query_grad.astype(dq_slabs.dtype)
             for h in range(q_heads):
                 dq_slabs[i, :, h * HEAD : (h + 1) * HEAD] = query_grad[
                     :, h * BLOCK : (h + 1) * BLOCK
-                ].T.astype(dq_slabs.dtype)
+                ].T
+        for i in members:
             ready(i)
 
     def one_step(step, carry):

time: 74 us -> 74.2 us (level)
  waiting for transfers between devices: 36.3 us -> 37.9 us
    ppermute x1, waiting for transfers between devices: 9.38 us -> 11 us  [per_device(): lax.ppermute(spill, 'blk', [(s + step, s) for s in range(spans - step)])]
  transfers between devices with their start and end apart: 6 -> 6, of which waited for: 4 -> 4; matrix products, arithmetic and copies ran while one was open for 0% -> 0% of each run, Pallas kernels for 13% -> 12%
where the time goes in v9:
time: 74.2 us; the launch traced here: 73.9 us
  waiting for transfers between devices  37.9 us (51%)
  starting transfers between devices  21.6 us (29%)
  Pallas kernels  13.4 us (18%)
  between operations  0.94 us (1%)
    all_to_all x4, waiting for transfers between devices, exchange(): lax.all_to_all(value, axes, split_axis=0, concat_axis=0, axis_index_group...  26.9 us
    all_to_all x4, starting transfers between devices, exchange(): lax.all_to_all(value, axes, split_axis=0, concat_axis=0, axis_index_group...  16.8 us
    ppermute x1, waiting for transfers between devices, per_device(): lax.ppermute(spill, 'blk', [(s + step, s) for s in range(spans - step)])  11 us
    pallas_call x1, Pallas kernels, attend_near(): pl.pallas_call(near_kernel, in_specs=[smem] * 2 + [vmem] * 3, out_specs=[...  4.01 us
    pallas_call x2, Pallas kernels, pack(): pl.pallas_call(pack_kernel, in_specs=[hbm] * 2, out_specs=hbm, out_shape=...  4 us
    ppermute x1, starting transfers between devices, per_device(): halo = lax.ppermute(kv, 'blk', [(s, s + step) for s in range(spans - step)])  3.54 us
    pallas_call x2, Pallas kernels, unpack(): pl.pallas_call(unpack_kernel, in_specs=[pl.BlockSpec(memory_space=pltpu.V...  1.76 us
  transfers between devices with their start and end apart: 6, of which 4 were waited for; matrix products, arithmetic and copies ran while one was open for 0% of the time, Pallas kernels for 12%

profile of v9, /device:TPU:0, one launch (start us, length us, event | category | flops | bytes accessed | tf_op | source)
XLA Modules:
  0.0 73.9 jit_solution(5808212513247293180)
XLA Ops:
  0.6 1.8 %shard_map.85.room_ref = bf16[8,128,256]{2,1,0:T(8,128)(2,1)} custom-call(bf16[128,1024]{1,0:T(8,128)(2,1)} %a_ref.2, bf16[128,1024]{1,0:T(8,128)(2,1)} %b_ref.2), custom_call_target="tpu_custom_call" | custom-call | tf_op jit(solution)/shard_map/pallas_call | solution.py:70
  2.5 5.2 %all-to-all-start = ((bf16[8,128,256]{2,1,0:T(8,128)(2,1)}), bf16[8,128,256]{2,1,0:T(8,128)(2,1)S(1)}, u32[]{:S(2)}, u32[]{:S(2)}) async-start(bf16[8,128,256]{2,1,0:T(8,128)(2,1)} %shard_map.85.room_ref), calls=%async_computation | async-start | bytes 1048576 | tf_op jit(solution)/shard_map/all_to_all | solution.py:378
  7.7 0.0 copy-start
  7.7 0.0 copy-start.1
  7.7 2.1 %shard_map.87 = bf16[8,128,512]{2,1,0:T(8,128)(2,1)} custom-call(bf16[128,2048]{1,0:T(8,128)(2,1)} %a_ref.3, bf16[128,2048]{1,0:T(8,128)(2,1)} %b_ref.3), custom_call_target="tpu_custom_call" | custom-call | tf_op jit(solution)/shard_map/pallas_call | solution.py:70
  9.8 7.6 %all-to-all-done.own_ref = bf16[8,128,256]{2,1,0:T(8,128)(2,1)S(1)} async-done(((bf16[8,128,256]{2,1,0:T(8,128)(2,1)}), bf16[8,128,256]{2,1,0:T(8,128)(2,1)S(1)}, u32[]{:S(2)}, u32[]{:S(2)}) %all-to-all-start) | async-done | bytes 524320 | tf_op jit(solution)/shard_map/all_to_all | solution.py:378
  17.4 3.6 %all-to-all-start.1 = ((bf16[8,128,512]{2,1,0:T(8,128)(2,1)}), bf16[8,128,512]{2,1,0:T(8,128)(2,1)S(1)}, u32[]{:S(2)}, u32[]{:S(2)}) async-start(bf16[8,128,512]{2,1,0:T(8,128)(2,1)} %shard_map.87), calls=%async_computation.1 | async-start | bytes 2097152 | tf_op jit(solution)/shard_map/all_to_all | solution.py:378
  21.0 3.5 %collective-permute-start = (bf16[8,128,256]{2,1,0:T(8,128)(2,1)S(1)}, bf16[8,128,256]{2,1,0:T(8,128)(2,1)S(1)}, u32[]{:S(2)}, u32[]{:S(2)}) collective-permute-start(bf16[8,128,256]{2,1,0:T(8,128)(2,1)S(1)} %all-to-all-done.own_ref), channel_id=1, source_target_pairs={{0,8},{2,10},{4,12},{6,14},{8,16},{10,18},{12,20},{14,22},{16,24},... | collective-permute-start | bytes 1572872 | tf_op jit(solution)/shard_map/ppermute | solution.py:384
  24.5 0.0 copy-done
  24.6 0.0 copy-done.1
  24.6 1.3 %shard_map.86 = (s32[8]{0:T(128)S(1)}, s32[10]{0:T(128)S(1)}, bf16[128,1024]{1,0:T(8,128)(2,1)S(1)}) custom-call(s32[1]{0:T(128)} %bitcast.chunk_ref, s32[32]{0:T(128)S(1)} %copy-done, s32[32]{0:T(128)S(1)} %copy-done.1, bf16[8,128,256]{2,1,0:T(8,128)(2,1)S(1)} %all-to-all-done.own_ref), custom_call_target="tpu_custom_call" | custom-call | tf_op jit(solution)/shard_map/pallas_call | solution.py:145
  25.9 10.4 %all-to-all-done.1.qd_ref = bf16[8,128,512]{2,1,0:T(8,128)(2,1)S(1)} async-done(((bf16[8,128,512]{2,1,0:T(8,128)(2,1)}), bf16[8,128,512]{2,1,0:T(8,128)(2,1)S(1)}, u32[]{:S(2)}, u32[]{:S(2)}) %all-to-all-start.1) | async-done | bytes 1048608 | tf_op jit(solution)/shard_map/all_to_all | solution.py:378
  36.3 4.0 %shard_map.88 = (bf16[8,128,256]{2,1,0:T(8,128)(2,1)S(1)}, f32[2048,256]{1,0:T(8,128)S(1)}, bf16[2048,256]{1,0:T(8,128)(2,1)S(1)}, bf16[128,2048]{1,0:T(8,128)(2,1)S(1)}) custom-call(s32[8]{0:T(128)S(1)} %get-tuple-element.15.order, s32[10]{0:T(128)S(1)} %get-tuple-element.16.counts, bf16[8,128,512]{2,1,0:T(8,128)(2,1)S(1)} %all-to-all-done.1.qd_ref, ...), custom_call_target="tpu_custom_call" | custom-call | tf_op jit(solution)/shard_map/pallas_call | solution.py:303
  40.3 0.0 collective-permute-done.halo_ref
  40.4 1.4 %shard_map.89 = (bf16[8,128,256]{2,1,0:T(8,128)(2,1)}, f32[1024,256]{1,0:T(8,128)S(1)}, bf16[8,128,256]{2,1,0:T(8,128)(2,1)S(1)}, bf16[2048,256]{1,0:T(8,128)(2,...) custom-call(s32[8]{0:T(128)S(1)} %get-tuple-element.15.order, ...), custom_call_target="tpu_custom_call", output_to_operand_aliasing={{0}: (5, {}), {2}: (3, {}), {3}: (6, {}), {4}: (7, {}), {5}... | custom-call | tf_op jit(solution)/shard_map/pallas_call | solution.py:323
  41.8 1.3 %collective-permute-start.1 = (bf16[8,128,256]{2,1,0:T(8,128)(2,1)S(1)}, bf16[8,128,256]{2,1,0:T(8,128)(2,1)S(1)}, u32[]{:S(2)}, u32[]{:S(2)}) collective-permute-start(bf16[8,128,256]{2,1,0:T(8,128)(2,1)S(1)} %get-tuple-element.24), channel_id=1, source_target_pairs={{8,0},{10,2},{12,4},{14,6},{16,8},{18,10},{20,12},{22,14},{24,16},... | collective-permute-start | bytes 1572872 | tf_op jit(solution)/shard_map/ppermute | solution.py:390
  43.1 3.5 %all-to-all-start.2 = ((bf16[8,128,256]{2,1,0:T(8,128)(2,1)}), bf16[8,128,256]{2,1,0:T(8,128)(2,1)S(1)}, u32[]{:S(2)}, u32[]{:S(2)}) async-start(bf16[8,128,256]{2,1,0:T(8,128)(2,1)} %get-tuple-element.22), calls=%async_computation.2 | async-start | bytes 1048576 | tf_op jit(solution)/shard_map/all_to_all | solution.py:378
  46.6 11.0 %collective-permute-done.1.spill_ref = bf16[8,128,256]{2,1,0:T(8,128)(2,1)S(1)} collective-permute-done((bf16[8,128,256]{2,1,0:T(8,128)(2,1)S(1)}, bf16[8,128,256]{2,1,0:T(8,128)(2,1)S(1)}, u32[]{:S(2)}, u32[]{:S(2)}) %collective-permute-start.1) | collective-permute-done | bytes 524320 | tf_op jit(solution)/shard_map/ppermute | solution.py:390
  57.6 0.9 %shard_map.91 = bf16[8,128,256]{2,1,0:T(8,128)(2,1)} custom-call(f32[1024,256]{1,0:T(8,128)S(1)} %get-tuple-element.23.sums_ref, bf16[8,128,256]{2,1,0:T(8,128)(2,1)S(1)} %collective-permute-done.1.spill_ref), custom_call_target="tpu_custom_call" | custom-call | tf_op jit(solution)/shard_map/pallas_call | solution.py:353
  58.5 0.0 all-to-all-done.2.in_ref
  58.5 4.6 %all-to-all-start.3 = ((bf16[8,128,256]{2,1,0:T(8,128)(2,1)}), bf16[8,128,256]{2,1,0:T(8,128)(2,1)S(1)}, u32[]{:S(2)}, u32[]{:S(2)}) async-start(bf16[8,128,256]{2,1,0:T(8,128)(2,1)} %shard_map.91), calls=%async_computation.3 | async-start | bytes 1048576 | tf_op jit(solution)/shard_map/all_to_all | solution.py:378
  63.0 0.8 %shard_map.90 = bf16[128,2048]{1,0:T(8,128)(2,1)} custom-call(bf16[8,128,256]{2,1,0:T(8,128)(2,1)S(1)} %all-to-all-done.2.in_ref), custom_call_target="tpu_custom_call" | custom-call | tf_op jit(solution)/shard_map/pallas_call | solution.py:99
  63.9 8.9 %all-to-all-done.3.in_ref = bf16[8,128,256]{2,1,0:T(8,128)(2,1)S(1)} async-done(((bf16[8,128,256]{2,1,0:T(8,128)(2,1)}), bf16[8,128,256]{2,1,0:T(8,128)(2,1)S(1)}, u32[]{:S(2)}, u32[]{:S(2)}) %all-to-all-start.3) | async-done | bytes 524320 | tf_op jit(solution)/shard_map/all_to_all | solution.py:378
  72.8 0.9 %shard_map.92 = (bf16[128,1024]{1,0:T(8,128)(2,1)}, bf16[128,1024]{1,0:T(8,128)(2,1)}) custom-call(bf16[8,128,256]{2,1,0:T(8,128)(2,1)S(1)} %all-to-all-done.3.in_ref), custom_call_target="tpu_custom_call" | custom-call | tf_op jit(solution)/shard_map/pallas_call | solution.py:99
Async XLA Ops:
  2.5 14.9 %all-to-all-start = ((bf16[8,128,256]{2,1,0:T(8,128)(2,1)}), bf16[8,128,256]{2,1,0:T(8,128)(2,1)S(1)}, u32[]{:S(2)}, u32[]{:S(2)}) async-start(bf16[8,128,256]{2,1,0:T(8,128)(2,1)} %shard_map.85.room_ref), calls=%async_computation | async-start | bytes 1048576 | tf_op jit(solution)/shard_map/all_to_all | solution.py:378
  7.7 16.9 %copy-start = (s32[32]{0:T(128)S(1)}, s32[32]{0:T(128)}, u32[]{:S(2)}) copy-start(s32[32]{0:T(128)} %doc_ref.1) | copy-start | bytes 388
  7.7 16.9 %copy-start.1 = (s32[32]{0:T(128)S(1)}, s32[32]{0:T(128)}, u32[]{:S(2)}) copy-start(s32[32]{0:T(128)} %band_ref.1) | copy-start | bytes 388
  17.4 18.9 %all-to-all-start.1 = ((bf16[8,128,512]{2,1,0:T(8,128)(2,1)}), bf16[8,128,512]{2,1,0:T(8,128)(2,1)S(1)}, u32[]{:S(2)}, u32[]{:S(2)}) async-start(bf16[8,128,512]{2,1,0:T(8,128)(2,1)} %shard_map.87), calls=%async_computation.1 | async-start | bytes 2097152 | tf_op jit(solution)/shard_map/all_to_all | solution.py:378
  21.0 19.4 %collective-permute-start = (bf16[8,128,256]{2,1,0:T(8,128)(2,1)S(1)}, bf16[8,128,256]{2,1,0:T(8,128)(2,1)S(1)}, u32[]{:S(2)}, u32[]{:S(2)}) collective-permute-start(bf16[8,128,256]{2,1,0:T(8,128)(2,1)S(1)} %all-to-all-done.own_ref), channel_id=1, source_target_pairs={{0,8},{2,10},{4,12},{6,14},{8,16},{10,18},{12,20},{14,22},{16,24},... | collective-permute-start | bytes 1572872 | tf_op jit(solution)/shard_map/ppermute | solution.py:384
  41.8 15.8 %collective-permute-start.1 = (bf16[8,128,256]{2,1,0:T(8,128)(2,1)S(1)}, bf16[8,128,256]{2,1,0:T(8,128)(2,1)S(1)}, u32[]{:S(2)}, u32[]{:S(2)}) collective-permute-start(bf16[8,128,256]{2,1,0:T(8,128)(2,1)S(1)} %get-tuple-element.24), channel_id=1, source_target_pairs={{8,0},{10,2},{12,4},{14,6},{16,8},{18,10},{20,12},{22,14},{24,16},... | collective-permute-start | bytes 1572872 | tf_op jit(solution)/shard_map/ppermute | solution.py:390
  43.1 15.4 %all-to-all-start.2 = ((bf16[8,128,256]{2,1,0:T(8,128)(2,1)}), bf16[8,128,256]{2,1,0:T(8,128)(2,1)S(1)}, u32[]{:S(2)}, u32[]{:S(2)}) async-start(bf16[8,128,256]{2,1,0:T(8,128)(2,1)} %get-tuple-element.22), calls=%async_computation.2 | async-start | bytes 1048576 | tf_op jit(solution)/shard_map/all_to_all | solution.py:378
  58.5 14.3 %all-to-all-start.3 = ((bf16[8,128,256]{2,1,0:T(8,128)(2,1)}), bf16[8,128,256]{2,1,0:T(8,128)(2,1)S(1)}, u32[]{:S(2)}, u32[]{:S(2)}) async-start(bf16[8,128,256]{2,1,0:T(8,128)(2,1)} %shard_map.91), calls=%async_computation.3 | async-start | bytes 1048576 | tf_op jit(solution)/shard_map/all_to_all | solution.py:378

commit v10 on v9

--- a/solution.py
+++ b/solution.py
@@ -241,7 +241,6 @@
         for n in lanes:
             scores[n][-1] = jnp.where(causal, scores[n][-1], -jnp.inf)
             seen = [count - b <= sizes[n] for b in range(count)]
-            dprob[n] = split(dot(kv[windows[n], HEAD:], grad[n], NT))
             tops, expo, totals = [], [], []
             for x in scores[n]:
                 top = jnp.max(fold(x, jnp.max), axis=0, keepdims=True)
@@ -258,6 +257,7 @@
             probs_b[n] = [x.astype(jnp.bfloat16) for x in probs[n]]
         dscore = {}
         for n in lanes:
+            dprob[n] = split(dot(kv[windows[n], HEAD:], grad[n], NT))
             sums[windows[n], HEAD:] += dot(jnp.concatenate(probs_b[n], axis=0), grad[n], NN)
             delta = functools.reduce(
                 jnp.add,

time: 74.2 us -> 74.4 us (level)
  Pallas kernels: 13.4 us -> 15.7 us
  waiting for transfers between devices: 37.9 us -> 35.7 us
    ppermute x1, waiting for transfers between devices: 11 us -> 7.88 us  [per_device(): lax.ppermute(spill, 'blk', [(s + step, s) for s in range(spans - step)])]
    pallas_call x1, Pallas kernels: 4.01 us -> 6.33 us  [attend_near(): pl.pallas_call(near_kernel, in_specs=[smem] * 2 + [vmem] * 3, out_specs=[...]
    all_to_all x4, waiting for transfers between devices: 26.9 us -> 27.8 us  [exchange(): lax.all_to_all(value, axes, split_axis=0, concat_axis=0, axis_index_group...]
  transfers between devices with their start and end apart: 6 -> 6, of which waited for: 4 -> 5; matrix products, arithmetic and copies ran while one was open for 0% -> 0% of each run, Pallas kernels for 12% -> 16%
where the time goes in v10:
time: 74.4 us; the launch traced here: 73.4 us
  waiting for transfers between devices  35.7 us (48%)
  starting transfers between devices  21.1 us (28%)
  Pallas kernels  15.7 us (21%)
  between operations  0.93 us (1%)
    all_to_all x4, waiting for transfers between devices, exchange(): lax.all_to_all(value, axes, split_axis=0, concat_axis=0, axis_index_group...  27.8 us
    all_to_all x4, starting transfers between devices, exchange(): lax.all_to_all(value, axes, split_axis=0, concat_axis=0, axis_index_group...  16.2 us
    ppermute x1, waiting for transfers between devices, per_device(): lax.ppermute(spill, 'blk', [(s + step, s) for s in range(spans - step)])  7.88 us
    pallas_call x1, Pallas kernels, attend_near(): pl.pallas_call(near_kernel, in_specs=[smem] * 2 + [vmem] * 3, out_specs=[...  6.33 us
    pallas_call x2, Pallas kernels, pack(): pl.pallas_call(pack_kernel, in_specs=[hbm] * 2, out_specs=hbm, out_shape=...  4 us
    ppermute x1, starting transfers between devices, per_device(): halo = lax.ppermute(kv, 'blk', [(s, s + step) for s in range(spans - step)])  3.54 us
    pallas_call x2, Pallas kernels, unpack(): pl.pallas_call(unpack_kernel, in_specs=[pl.BlockSpec(memory_space=pltpu.V...  1.76 us
  transfers between devices with their start and end apart: 6, of which 5 were waited for; matrix products, arithmetic and copies ran while one was open for 0% of the time, Pallas kernels for 16%

profile of v10, /device:TPU:0, one launch (start us, length us, event | category | flops | bytes accessed | tf_op | source)
XLA Modules:
  0.0 73.4 jit_solution(16742052771255354322)
XLA Ops:
  0.6 1.8 %shard_map.85.room_ref = bf16[8,128,256]{2,1,0:T(8,128)(2,1)} custom-call(bf16[128,1024]{1,0:T(8,128)(2,1)} %a_ref.2, bf16[128,1024]{1,0:T(8,128)(2,1)} %b_ref.2), custom_call_target="tpu_custom_call" | custom-call | tf_op jit(solution)/shard_map/pallas_call | solution.py:70
  2.5 5.2 %all-to-all-start = ((bf16[8,128,256]{2,1,0:T(8,128)(2,1)}), bf16[8,128,256]{2,1,0:T(8,128)(2,1)S(1)}, u32[]{:S(2)}, u32[]{:S(2)}) async-start(bf16[8,128,256]{2,1,0:T(8,128)(2,1)} %shard_map.85.room_ref), calls=%async_computation | async-start | bytes 1048576 | tf_op jit(solution)/shard_map/all_to_all | solution.py:378
  7.7 0.0 copy-start
  7.7 0.0 copy-start.1
  7.7 2.1 %shard_map.87 = bf16[8,128,512]{2,1,0:T(8,128)(2,1)} custom-call(bf16[128,2048]{1,0:T(8,128)(2,1)} %a_ref.3, bf16[128,2048]{1,0:T(8,128)(2,1)} %b_ref.3), custom_call_target="tpu_custom_call" | custom-call | tf_op jit(solution)/shard_map/pallas_call | solution.py:70
  9.8 7.6 %all-to-all-done.own_ref = bf16[8,128,256]{2,1,0:T(8,128)(2,1)S(1)} async-done(((bf16[8,128,256]{2,1,0:T(8,128)(2,1)}), bf16[8,128,256]{2,1,0:T(8,128)(2,1)S(1)}, u32[]{:S(2)}, u32[]{:S(2)}) %all-to-all-start) | async-done | bytes 524320 | tf_op jit(solution)/shard_map/all_to_all | solution.py:378
  17.4 3.6 %all-to-all-start.1 = ((bf16[8,128,512]{2,1,0:T(8,128)(2,1)}), bf16[8,128,512]{2,1,0:T(8,128)(2,1)S(1)}, u32[]{:S(2)}, u32[]{:S(2)}) async-start(bf16[8,128,512]{2,1,0:T(8,128)(2,1)} %shard_map.87), calls=%async_computation.1 | async-start | bytes 2097152 | tf_op jit(solution)/shard_map/all_to_all | solution.py:378
  21.0 3.5 %collective-permute-start = (bf16[8,128,256]{2,1,0:T(8,128)(2,1)S(1)}, bf16[8,128,256]{2,1,0:T(8,128)(2,1)S(1)}, u32[]{:S(2)}, u32[]{:S(2)}) collective-permute-start(bf16[8,128,256]{2,1,0:T(8,128)(2,1)S(1)} %all-to-all-done.own_ref), channel_id=1, source_target_pairs={{0,8},{2,10},{4,12},{6,14},{8,16},{10,18},{12,20},{14,22},{16,24},... | collective-permute-start | bytes 1572872 | tf_op jit(solution)/shard_map/ppermute | solution.py:384
  24.5 0.0 copy-done
  24.6 0.0 copy-done.1
  24.6 1.3 %shard_map.86 = (s32[8]{0:T(128)S(1)}, s32[10]{0:T(128)S(1)}, bf16[128,1024]{1,0:T(8,128)(2,1)S(1)}) custom-call(s32[1]{0:T(128)} %bitcast.chunk_ref, s32[32]{0:T(128)S(1)} %copy-done, s32[32]{0:T(128)S(1)} %copy-done.1, bf16[8,128,256]{2,1,0:T(8,128)(2,1)S(1)} %all-to-all-done.own_ref), custom_call_target="tpu_custom_call" | custom-call | tf_op jit(solution)/shard_map/pallas_call | solution.py:145
  25.9 10.4 %all-to-all-done.1.qd_ref = bf16[8,128,512]{2,1,0:T(8,128)(2,1)S(1)} async-done(((bf16[8,128,512]{2,1,0:T(8,128)(2,1)}), bf16[8,128,512]{2,1,0:T(8,128)(2,1)S(1)}, u32[]{:S(2)}, u32[]{:S(2)}) %all-to-all-start.1) | async-done | bytes 1048608 | tf_op jit(solution)/shard_map/all_to_all | solution.py:378
  36.3 6.3 %shard_map.88 = (bf16[8,128,256]{2,1,0:T(8,128)(2,1)S(1)}, f32[2048,256]{1,0:T(8,128)S(1)}, bf16[2048,256]{1,0:T(8,128)(2,1)S(1)}, bf16[128,2048]{1,0:T(8,128)(2,1)S(1)}) custom-call(s32[8]{0:T(128)S(1)} %get-tuple-element.15.order, s32[10]{0:T(128)S(1)} %get-tuple-element.16.counts, bf16[8,128,512]{2,1,0:T(8,128)(2,1)S(1)} %all-to-all-done.1.qd_ref, ...), custom_call_target="tpu_custom_call" | custom-call | tf_op jit(solution)/shard_map/pallas_call | solution.py:303
  42.7 0.0 collective-permute-done.halo_ref
  42.7 1.4 %shard_map.89 = (bf16[8,128,256]{2,1,0:T(8,128)(2,1)}, f32[1024,256]{1,0:T(8,128)S(1)}, bf16[8,128,256]{2,1,0:T(8,128)(2,1)S(1)}, bf16[2048,256]{1,0:T(8,128)(2,...) custom-call(s32[8]{0:T(128)S(1)} %get-tuple-element.15.order, ...), custom_call_target="tpu_custom_call", output_to_operand_aliasing={{0}: (5, {}), {2}: (3, {}), {3}: (6, {}), {4}: (7, {}), {5}... | custom-call | tf_op jit(solution)/shard_map/pallas_call | solution.py:323
  44.1 1.3 %collective-permute-start.1 = (bf16[8,128,256]{2,1,0:T(8,128)(2,1)S(1)}, bf16[8,128,256]{2,1,0:T(8,128)(2,1)S(1)}, u32[]{:S(2)}, u32[]{:S(2)}) collective-permute-start(bf16[8,128,256]{2,1,0:T(8,128)(2,1)S(1)} %get-tuple-element.24), channel_id=1, source_target_pairs={{8,0},{10,2},{12,4},{14,6},{16,8},{18,10},{20,12},{22,14},{24,16},... | collective-permute-start | bytes 1572872 | tf_op jit(solution)/shard_map/ppermute | solution.py:390
  45.4 3.5 %all-to-all-start.2 = ((bf16[8,128,256]{2,1,0:T(8,128)(2,1)}), bf16[8,128,256]{2,1,0:T(8,128)(2,1)S(1)}, u32[]{:S(2)}, u32[]{:S(2)}) async-start(bf16[8,128,256]{2,1,0:T(8,128)(2,1)} %get-tuple-element.22), calls=%async_computation.2 | async-start | bytes 1048576 | tf_op jit(solution)/shard_map/all_to_all | solution.py:378
  48.9 7.9 %collective-permute-done.1.spill_ref = bf16[8,128,256]{2,1,0:T(8,128)(2,1)S(1)} collective-permute-done((bf16[8,128,256]{2,1,0:T(8,128)(2,1)S(1)}, bf16[8,128,256]{2,1,0:T(8,128)(2,1)S(1)}, u32[]{:S(2)}, u32[]{:S(2)}) %collective-permute-start.1) | collective-permute-done | bytes 524320 | tf_op jit(solution)/shard_map/ppermute | solution.py:390
  56.8 0.9 %shard_map.91 = bf16[8,128,256]{2,1,0:T(8,128)(2,1)} custom-call(f32[1024,256]{1,0:T(8,128)S(1)} %get-tuple-element.23.sums_ref, bf16[8,128,256]{2,1,0:T(8,128)(2,1)S(1)} %collective-permute-done.1.spill_ref), custom_call_target="tpu_custom_call" | custom-call | tf_op jit(solution)/shard_map/pallas_call | solution.py:353
  57.7 0.9 %all-to-all-done.2.in_ref = bf16[8,128,256]{2,1,0:T(8,128)(2,1)S(1)} async-done(((bf16[8,128,256]{2,1,0:T(8,128)(2,1)}), bf16[8,128,256]{2,1,0:T(8,128)(2,1)S(1)}, u32[]{:S(2)}, u32[]{:S(2)}) %all-to-all-start.2) | async-done | bytes 524320 | tf_op jit(solution)/shard_map/all_to_all | solution.py:378
  58.6 4.0 %all-to-all-start.3 = ((bf16[8,128,256]{2,1,0:T(8,128)(2,1)}), bf16[8,128,256]{2,1,0:T(8,128)(2,1)S(1)}, u32[]{:S(2)}, u32[]{:S(2)}) async-start(bf16[8,128,256]{2,1,0:T(8,128)(2,1)} %shard_map.91), calls=%async_computation.3 | async-start | bytes 1048576 | tf_op jit(solution)/shard_map/all_to_all | solution.py:378
  62.6 0.8 %shard_map.90 = bf16[128,2048]{1,0:T(8,128)(2,1)} custom-call(bf16[8,128,256]{2,1,0:T(8,128)(2,1)S(1)} %all-to-all-done.2.in_ref), custom_call_target="tpu_custom_call" | custom-call | tf_op jit(solution)/shard_map/pallas_call | solution.py:99
  63.4 8.9 %all-to-all-done.3.in_ref = bf16[8,128,256]{2,1,0:T(8,128)(2,1)S(1)} async-done(((bf16[8,128,256]{2,1,0:T(8,128)(2,1)}), bf16[8,128,256]{2,1,0:T(8,128)(2,1)S(1)}, u32[]{:S(2)}, u32[]{:S(2)}) %all-to-all-start.3) | async-done | bytes 524320 | tf_op jit(solution)/shard_map/all_to_all | solution.py:378
  72.3 0.9 %shard_map.92 = (bf16[128,1024]{1,0:T(8,128)(2,1)}, bf16[128,1024]{1,0:T(8,128)(2,1)}) custom-call(bf16[8,128,256]{2,1,0:T(8,128)(2,1)S(1)} %all-to-all-done.3.in_ref), custom_call_target="tpu_custom_call" | custom-call | tf_op jit(solution)/shard_map/pallas_call | solution.py:99
Async XLA Ops:
  2.5 14.9 %all-to-all-start = ((bf16[8,128,256]{2,1,0:T(8,128)(2,1)}), bf16[8,128,256]{2,1,0:T(8,128)(2,1)S(1)}, u32[]{:S(2)}, u32[]{:S(2)}) async-start(bf16[8,128,256]{2,1,0:T(8,128)(2,1)} %shard_map.85.room_ref), calls=%async_computation | async-start | bytes 1048576 | tf_op jit(solution)/shard_map/all_to_all | solution.py:378
  7.7 16.9 %copy-start = (s32[32]{0:T(128)S(1)}, s32[32]{0:T(128)}, u32[]{:S(2)}) copy-start(s32[32]{0:T(128)} %doc_ref.1) | copy-start | bytes 388
  7.7 16.9 %copy-start.1 = (s32[32]{0:T(128)S(1)}, s32[32]{0:T(128)}, u32[]{:S(2)}) copy-start(s32[32]{0:T(128)} %band_ref.1) | copy-start | bytes 388
  17.4 18.9 %all-to-all-start.1 = ((bf16[8,128,512]{2,1,0:T(8,128)(2,1)}), bf16[8,128,512]{2,1,0:T(8,128)(2,1)S(1)}, u32[]{:S(2)}, u32[]{:S(2)}) async-start(bf16[8,128,512]{2,1,0:T(8,128)(2,1)} %shard_map.87), calls=%async_computation.1 | async-start | bytes 2097152 | tf_op jit(solution)/shard_map/all_to_all | solution.py:378
  21.0 21.7 %collective-permute-start = (bf16[8,128,256]{2,1,0:T(8,128)(2,1)S(1)}, bf16[8,128,256]{2,1,0:T(8,128)(2,1)S(1)}, u32[]{:S(2)}, u32[]{:S(2)}) collective-permute-start(bf16[8,128,256]{2,1,0:T(8,128)(2,1)S(1)} %all-to-all-done.own_ref), channel_id=1, source_target_pairs={{0,8},{2,10},{4,12},{6,14},{8,16},{10,18},{12,20},{14,22},{16,24},... | collective-permute-start | bytes 1572872 | tf_op jit(solution)/shard_map/ppermute | solution.py:384
  44.1 12.7 %collective-permute-start.1 = (bf16[8,128,256]{2,1,0:T(8,128)(2,1)S(1)}, bf16[8,128,256]{2,1,0:T(8,128)(2,1)S(1)}, u32[]{:S(2)}, u32[]{:S(2)}) collective-permute-start(bf16[8,128,256]{2,1,0:T(8,128)(2,1)S(1)} %get-tuple-element.24), channel_id=1, source_target_pairs={{8,0},{10,2},{12,4},{14,6},{16,8},{18,10},{20,12},{22,14},{24,16},... | collective-permute-start | bytes 1572872 | tf_op jit(solution)/shard_map/ppermute | solution.py:390
  45.4 13.2 %all-to-all-start.2 = ((bf16[8,128,256]{2,1,0:T(8,128)(2,1)}), bf16[8,128,256]{2,1,0:T(8,128)(2,1)S(1)}, u32[]{:S(2)}, u32[]{:S(2)}) async-start(bf16[8,128,256]{2,1,0:T(8,128)(2,1)} %get-tuple-element.22), calls=%async_computation.2 | async-start | bytes 1048576 | tf_op jit(solution)/shard_map/all_to_all | solution.py:378
  58.6 13.7 %all-to-all-start.3 = ((bf16[8,128,256]{2,1,0:T(8,128)(2,1)}), bf16[8,128,256]{2,1,0:T(8,128)(2,1)S(1)}, u32[]{:S(2)}, u32[]{:S(2)}) async-start(bf16[8,128,256]{2,1,0:T(8,128)(2,1)} %shard_map.91), calls=%async_computation.3 | async-start | bytes 1048576 | tf_op jit(solution)/shard_map/all_to_all | solution.py:378

commit v11 on v8

--- a/solution.py
+++ b/solution.py
@@ -18,6 +18,7 @@
 SMALL = 8 * 1024 * 1024
 LARGE = 40 * 1024 * 1024
 TOGETHER = 2
+CHUNKS = 4
 
 NT = (((1,), (1,)), ((), ()))
 NN = (((1,), (0,)), ((), ()))
@@ -35,29 +36,34 @@
         copy.wait()
 
 
-def pack_kernel(a_ref, b_ref, out_ref, slabs, in_sems, out_sems):
-    heads = out_ref.shape[0]
+def pack_kernel(a_ref, b_ref, out_ref, a_rows, b_rows, slabs, in_sems, out_sems):
+    heads, tokens = out_ref.shape[:2]
     width = out_ref.shape[2] // 2
+    size = tokens // CHUNKS
+    chunks = [pl.ds(c * size, size) for c in range(CHUNKS)]
+    sides = ((a_ref, a_rows), (b_ref, b_rows))
     reads = [
         [
-            pltpu.make_async_copy(
-                ref.at[:, pl.ds(h * width, width)],
-                slabs.at[h, :, pl.ds(n * width, width)],
-                in_sems.at[2 * h + n],
-            )
-            for n, ref in enumerate((a_ref, b_ref))
+            pltpu.make_async_copy(ref.at[rows], held.at[rows], in_sems.at[2 * c + n])
+            for n, (ref, held) in enumerate(sides)
         ]
-        for h in range(heads)
+        for c, rows in enumerate(chunks)
     ]
     writes = [
-        pltpu.make_async_copy(slabs.at[h], out_ref.at[h], out_sems.at[h]) for h in range(heads)
+        pltpu.make_async_copy(slabs.at[:, rows], out_ref.at[:, rows], out_sems.at[c])
+        for c, rows in enumerate(chunks)
     ]
     for pair in reads:
         for copy in pair:
             copy.start()
-    for pair, write in zip(reads, writes):
+    for rows, pair, write in zip(chunks, reads, writes):
         for copy in pair:
             copy.wait()
+        for h in range(heads):
+            for n, (_, held) in enumerate(sides):
+                slabs[h, rows, n * width : (n + 1) * width] = held[
+                    rows, h * width : (h + 1) * width
+                ]
         write.start()
     for write in writes:
         write.wait()
@@ -73,9 +79,11 @@
         out_specs=hbm,
         out_shape=jax.ShapeDtypeStruct(shape, a.dtype),
         scratch_shapes=[
+            pltpu.VMEM(a.shape, a.dtype),
+            pltpu.VMEM(b.shape, b.dtype),
             pltpu.VMEM(shape, a.dtype),
-            pltpu.SemaphoreType.DMA((2 * heads,)),
-            pltpu.SemaphoreType.DMA((heads,)),
+            pltpu.SemaphoreType.DMA((2 * CHUNKS,)),
+            pltpu.SemaphoreType.DMA((CHUNKS,)),
         ],
     )(a, b)
 

time: 74 us -> 73.9 us (level)
  transfers between devices with their start and end apart: 6 -> 6, of which waited for: 4 -> 4; matrix products, arithmetic and copies ran while one was open for 0% -> 0% of each run, Pallas kernels for 13% -> 14%
where the time goes in v11:
time: 73.9 us; the launch traced here: 73.2 us
  waiting for transfers between devices  36 us (49%)
  starting transfers between devices  22 us (30%)
  Pallas kernels  14.3 us (19%)
  between operations  0.94 us (1%)
    all_to_all x4, waiting for transfers between devices, exchange(): lax.all_to_all(value, axes, split_axis=0, concat_axis=0, axis_index_group...  26.9 us
    all_to_all x4, starting transfers between devices, exchange(): lax.all_to_all(value, axes, split_axis=0, concat_axis=0, axis_index_group...  17.1 us
    ppermute x1, waiting for transfers between devices, per_device(): lax.ppermute(spill, 'blk', [(s + step, s) for s in range(spans - step)])  9.11 us
    pallas_call x1, Pallas kernels, attend_near(): pl.pallas_call(near_kernel, in_specs=[smem] * 2 + [vmem] * 3, out_specs=[...  4.9 us
    pallas_call x2, Pallas kernels, pack(): pl.pallas_call(pack_kernel, in_specs=[hbm] * 2, out_specs=hbm, out_shape=...  4 us
    ppermute x1, starting transfers between devices, per_device(): halo = lax.ppermute(kv, 'blk', [(s, s + step) for s in range(spans - step)])  3.54 us
    pallas_call x2, Pallas kernels, unpack(): pl.pallas_call(unpack_kernel, in_specs=[pl.BlockSpec(memory_space=pltpu.V...  1.76 us
  transfers between devices with their start and end apart: 6, of which 4 were waited for; matrix products, arithmetic and copies ran while one was open for 0% of the time, Pallas kernels for 14%

profile of v11, /device:TPU:0, one launch (start us, length us, event | category | flops | bytes accessed | tf_op | source)
XLA Modules:
  0.0 73.2 jit_solution(6834341860274548745)
XLA Ops:
  0.6 1.8 %shard_map.85.room_ref = bf16[8,128,256]{2,1,0:T(8,128)(2,1)} custom-call(bf16[128,1024]{1,0:T(8,128)(2,1)} %a_ref.2, bf16[128,1024]{1,0:T(8,128)(2,1)} %b_ref.2), custom_call_target="tpu_custom_call" | custom-call | tf_op jit(solution)/shard_map/pallas_call | solution.py:76
  2.5 5.2 %all-to-all-start = ((bf16[8,128,256]{2,1,0:T(8,128)(2,1)}), bf16[8,128,256]{2,1,0:T(8,128)(2,1)S(1)}, u32[]{:S(2)}, u32[]{:S(2)}) async-start(bf16[8,128,256]{2,1,0:T(8,128)(2,1)} %shard_map.85.room_ref), calls=%async_computation | async-start | bytes 1048576 | tf_op jit(solution)/shard_map/all_to_all | solution.py:384
  7.7 0.0 copy-start
  7.7 0.0 copy-start.1
  7.7 2.2 %shard_map.87 = bf16[8,128,512]{2,1,0:T(8,128)(2,1)} custom-call(bf16[128,2048]{1,0:T(8,128)(2,1)} %a_ref.3, bf16[128,2048]{1,0:T(8,128)(2,1)} %b_ref.3), custom_call_target="tpu_custom_call" | custom-call | tf_op jit(solution)/shard_map/pallas_call | solution.py:76
  9.8 7.6 %all-to-all-done.own_ref = bf16[8,128,256]{2,1,0:T(8,128)(2,1)S(1)} async-done(((bf16[8,128,256]{2,1,0:T(8,128)(2,1)}), bf16[8,128,256]{2,1,0:T(8,128)(2,1)S(1)}, u32[]{:S(2)}, u32[]{:S(2)}) %all-to-all-start) | async-done | bytes 524320 | tf_op jit(solution)/shard_map/all_to_all | solution.py:384
  17.4 3.6 %all-to-all-start.1 = ((bf16[8,128,512]{2,1,0:T(8,128)(2,1)}), bf16[8,128,512]{2,1,0:T(8,128)(2,1)S(1)}, u32[]{:S(2)}, u32[]{:S(2)}) async-start(bf16[8,128,512]{2,1,0:T(8,128)(2,1)} %shard_map.87), calls=%async_computation.1 | async-start | bytes 2097152 | tf_op jit(solution)/shard_map/all_to_all | solution.py:384
  21.0 3.5 %collective-permute-start = (bf16[8,128,256]{2,1,0:T(8,128)(2,1)S(1)}, bf16[8,128,256]{2,1,0:T(8,128)(2,1)S(1)}, u32[]{:S(2)}, u32[]{:S(2)}) collective-permute-start(bf16[8,128,256]{2,1,0:T(8,128)(2,1)S(1)} %all-to-all-done.own_ref), channel_id=1, source_target_pairs={{0,8},{2,10},{4,12},{6,14},{8,16},{10,18},{12,20},{14,22},{16,24},... | collective-permute-start | bytes 1572872 | tf_op jit(solution)/shard_map/ppermute | solution.py:390
  24.5 0.0 copy-done
  24.6 0.0 copy-done.1
  24.6 1.3 %shard_map.86 = (s32[8]{0:T(128)S(1)}, s32[10]{0:T(128)S(1)}, bf16[128,1024]{1,0:T(8,128)(2,1)S(1)}) custom-call(s32[1]{0:T(128)} %bitcast.chunk_ref, s32[32]{0:T(128)S(1)} %copy-done, s32[32]{0:T(128)S(1)} %copy-done.1, bf16[8,128,256]{2,1,0:T(8,128)(2,1)S(1)} %all-to-all-done.own_ref), custom_call_target="tpu_custom_call" | custom-call | tf_op jit(solution)/shard_map/pallas_call | solution.py:153
  25.9 10.4 %all-to-all-done.1.qd_ref = bf16[8,128,512]{2,1,0:T(8,128)(2,1)S(1)} async-done(((bf16[8,128,512]{2,1,0:T(8,128)(2,1)}), bf16[8,128,512]{2,1,0:T(8,128)(2,1)S(1)}, u32[]{:S(2)}, u32[]{:S(2)}) %all-to-all-start.1) | async-done | bytes 1048608 | tf_op jit(solution)/shard_map/all_to_all | solution.py:384
  36.3 4.9 %shard_map.88 = (bf16[8,128,256]{2,1,0:T(8,128)(2,1)S(1)}, f32[2048,256]{1,0:T(8,128)S(1)}, bf16[2048,256]{1,0:T(8,128)(2,1)S(1)}, bf16[128,2048]{1,0:T(8,128)(2,1)S(1)}) custom-call(s32[8]{0:T(128)S(1)} %get-tuple-element.15.order, s32[10]{0:T(128)S(1)} %get-tuple-element.16.counts, bf16[8,128,512]{2,1,0:T(8,128)(2,1)S(1)} %all-to-all-done.1.qd_ref, ...), custom_call_target="tpu_custom_call" | custom-call | tf_op jit(solution)/shard_map/pallas_call | solution.py:309
  41.2 0.0 collective-permute-done.halo_ref
  41.2 1.4 %shard_map.89 = (bf16[8,128,256]{2,1,0:T(8,128)(2,1)}, f32[1024,256]{1,0:T(8,128)S(1)}, bf16[8,128,256]{2,1,0:T(8,128)(2,1)S(1)}, bf16[2048,256]{1,0:T(8,128)(2,...) custom-call(s32[8]{0:T(128)S(1)} %get-tuple-element.15.order, ...), custom_call_target="tpu_custom_call", output_to_operand_aliasing={{0}: (5, {}), {2}: (3, {}), {3}: (6, {}), {4}: (7, {}), {5}... | custom-call | tf_op jit(solution)/shard_map/pallas_call | solution.py:329
  42.6 1.3 %collective-permute-start.1 = (bf16[8,128,256]{2,1,0:T(8,128)(2,1)S(1)}, bf16[8,128,256]{2,1,0:T(8,128)(2,1)S(1)}, u32[]{:S(2)}, u32[]{:S(2)}) collective-permute-start(bf16[8,128,256]{2,1,0:T(8,128)(2,1)S(1)} %get-tuple-element.24), channel_id=1, source_target_pairs={{8,0},{10,2},{12,4},{14,6},{16,8},{18,10},{20,12},{22,14},{24,16},... | collective-permute-start | bytes 1572872 | tf_op jit(solution)/shard_map/ppermute | solution.py:396
  43.9 3.5 %all-to-all-start.2 = ((bf16[8,128,256]{2,1,0:T(8,128)(2,1)}), bf16[8,128,256]{2,1,0:T(8,128)(2,1)S(1)}, u32[]{:S(2)}, u32[]{:S(2)}) async-start(bf16[8,128,256]{2,1,0:T(8,128)(2,1)} %get-tuple-element.22), calls=%async_computation.2 | async-start | bytes 1048576 | tf_op jit(solution)/shard_map/all_to_all | solution.py:384
  47.5 9.1 %collective-permute-done.1.spill_ref = bf16[8,128,256]{2,1,0:T(8,128)(2,1)S(1)} collective-permute-done((bf16[8,128,256]{2,1,0:T(8,128)(2,1)S(1)}, bf16[8,128,256]{2,1,0:T(8,128)(2,1)S(1)}, u32[]{:S(2)}, u32[]{:S(2)}) %collective-permute-start.1) | collective-permute-done | bytes 524320 | tf_op jit(solution)/shard_map/ppermute | solution.py:396
  56.6 0.9 %shard_map.91 = bf16[8,128,256]{2,1,0:T(8,128)(2,1)} custom-call(f32[1024,256]{1,0:T(8,128)S(1)} %get-tuple-element.23.sums_ref, bf16[8,128,256]{2,1,0:T(8,128)(2,1)S(1)} %collective-permute-done.1.spill_ref), custom_call_target="tpu_custom_call" | custom-call | tf_op jit(solution)/shard_map/pallas_call | solution.py:359
  57.5 0.0 all-to-all-done.2.in_ref
  57.5 4.9 %all-to-all-start.3 = ((bf16[8,128,256]{2,1,0:T(8,128)(2,1)}), bf16[8,128,256]{2,1,0:T(8,128)(2,1)S(1)}, u32[]{:S(2)}, u32[]{:S(2)}) async-start(bf16[8,128,256]{2,1,0:T(8,128)(2,1)} %shard_map.91), calls=%async_computation.3 | async-start | bytes 1048576 | tf_op jit(solution)/shard_map/all_to_all | solution.py:384
  62.4 0.8 %shard_map.90 = bf16[128,2048]{1,0:T(8,128)(2,1)} custom-call(bf16[8,128,256]{2,1,0:T(8,128)(2,1)S(1)} %all-to-all-done.2.in_ref), custom_call_target="tpu_custom_call" | custom-call | tf_op jit(solution)/shard_map/pallas_call | solution.py:107
  63.2 8.9 %all-to-all-done.3.in_ref = bf16[8,128,256]{2,1,0:T(8,128)(2,1)S(1)} async-done(((bf16[8,128,256]{2,1,0:T(8,128)(2,1)}), bf16[8,128,256]{2,1,0:T(8,128)(2,1)S(1)}, u32[]{:S(2)}, u32[]{:S(2)}) %all-to-all-start.3) | async-done | bytes 524320 | tf_op jit(solution)/shard_map/all_to_all | solution.py:384
  72.1 0.9 %shard_map.92 = (bf16[128,1024]{1,0:T(8,128)(2,1)}, bf16[128,1024]{1,0:T(8,128)(2,1)}) custom-call(bf16[8,128,256]{2,1,0:T(8,128)(2,1)S(1)} %all-to-all-done.3.in_ref), custom_call_target="tpu_custom_call" | custom-call | tf_op jit(solution)/shard_map/pallas_call | solution.py:107
Async XLA Ops:
  2.5 14.9 %all-to-all-start = ((bf16[8,128,256]{2,1,0:T(8,128)(2,1)}), bf16[8,128,256]{2,1,0:T(8,128)(2,1)S(1)}, u32[]{:S(2)}, u32[]{:S(2)}) async-start(bf16[8,128,256]{2,1,0:T(8,128)(2,1)} %shard_map.85.room_ref), calls=%async_computation | async-start | bytes 1048576 | tf_op jit(solution)/shard_map/all_to_all | solution.py:384
  7.7 16.9 %copy-start = (s32[32]{0:T(128)S(1)}, s32[32]{0:T(128)}, u32[]{:S(2)}) copy-start(s32[32]{0:T(128)} %doc_ref.1) | copy-start | bytes 388
  7.7 16.9 %copy-start.1 = (s32[32]{0:T(128)S(1)}, s32[32]{0:T(128)}, u32[]{:S(2)}) copy-start(s32[32]{0:T(128)} %band_ref.1) | copy-start | bytes 388
  17.4 18.9 %all-to-all-start.1 = ((bf16[8,128,512]{2,1,0:T(8,128)(2,1)}), bf16[8,128,512]{2,1,0:T(8,128)(2,1)S(1)}, u32[]{:S(2)}, u32[]{:S(2)}) async-start(bf16[8,128,512]{2,1,0:T(8,128)(2,1)} %shard_map.87), calls=%async_computation.1 | async-start | bytes 2097152 | tf_op jit(solution)/shard_map/all_to_all | solution.py:384
  21.0 20.2 %collective-permute-start = (bf16[8,128,256]{2,1,0:T(8,128)(2,1)S(1)}, bf16[8,128,256]{2,1,0:T(8,128)(2,1)S(1)}, u32[]{:S(2)}, u32[]{:S(2)}) collective-permute-start(bf16[8,128,256]{2,1,0:T(8,128)(2,1)S(1)} %all-to-all-done.own_ref), channel_id=1, source_target_pairs={{0,8},{2,10},{4,12},{6,14},{8,16},{10,18},{12,20},{14,22},{16,24},... | collective-permute-start | bytes 1572872 | tf_op jit(solution)/shard_map/ppermute | solution.py:390
  42.6 13.9 %collective-permute-start.1 = (bf16[8,128,256]{2,1,0:T(8,128)(2,1)S(1)}, bf16[8,128,256]{2,1,0:T(8,128)(2,1)S(1)}, u32[]{:S(2)}, u32[]{:S(2)}) collective-permute-start(bf16[8,128,256]{2,1,0:T(8,128)(2,1)S(1)} %get-tuple-element.24), channel_id=1, source_target_pairs={{8,0},{10,2},{12,4},{14,6},{16,8},{18,10},{20,12},{22,14},{24,16},... | collective-permute-start | bytes 1572872 | tf_op jit(solution)/shard_map/ppermute | solution.py:396
  43.9 13.5 %all-to-all-start.2 = ((bf16[8,128,256]{2,1,0:T(8,128)(2,1)}), bf16[8,128,256]{2,1,0:T(8,128)(2,1)S(1)}, u32[]{:S(2)}, u32[]{:S(2)}) async-start(bf16[8,128,256]{2,1,0:T(8,128)(2,1)} %get-tuple-element.22), calls=%async_computation.2 | async-start | bytes 1048576 | tf_op jit(solution)/shard_map/all_to_all | solution.py:384
  57.5 14.6 %all-to-all-start.3 = ((bf16[8,128,256]{2,1,0:T(8,128)(2,1)}), bf16[8,128,256]{2,1,0:T(8,128)(2,1)S(1)}, u32[]{:S(2)}, u32[]{:S(2)}) async-start(bf16[8,128,256]{2,1,0:T(8,128)(2,1)} %shard_map.91), calls=%async_computation.3 | async-start | bytes 1048576 | tf_op jit(solution)/shard_map/all_to_all | solution.py:384
